TPU v7x, 128 devices: a whole 4x4x4 slice. The times are simulated.
128 devices in a mesh: section: 8 (over x, y_hi), seq: 4 (over y_lo, core), tensor: 4 (over z).
Axes of the slice: x: 4, y: 4 (y_hi: 2, y_lo: 2; y = y_hi * 2 + y_lo), z: 4, core: 2. Of those that a mesh axis runs over, the one named last changes fastest.
Arguments:
- patches: bfloat16 [32768, 1280], P(('section', 'seq'), 'tensor'), may hold values from -6 to 6
- norm_gain: float32 [1280], replicated, may hold values from 0.25 to 1.75
- w_in: bfloat16 [5120, 5120], P('seq', 'tensor'), may hold values from -0.078125 to 0.078125
- b_in: float32 [5120], P('tensor'), may hold values from -3 to 3
- w_out: bfloat16 [5120, 8192], P('tensor', 'seq'), may hold values from -0.078125 to 0.078125
- b_out: float32 [8192], P('tensor'), may hold values from -3 to 3
- text_rows: bfloat16 [32768, 8192], P(('section', 'seq'), 'tensor'), may hold values from -6 to 6
- dest_group: int32 [8192, 1], P(('section', 'seq')), may hold values from 0 to 31; in each aligned block of 256 rows (0 to 255, 256 to 511, ...) at most 16 rows name the same one
- dest_row: int32 [8192], P(('section', 'seq')), may hold values from 0 to 1023
- grad_rows: bfloat16 [32768, 8192], P(('section', 'seq'), 'tensor'), may hold values from -6 to 6
Outputs:
- llm_input: bfloat16 [32768, 8192], P(('section', 'seq'), 'tensor')
- grad_hidden: bfloat16 [8192, 5120], P(('section', 'seq'), 'tensor')
Inputs may be any that keep to these rules, and one draw needn't show every extreme that they name: `dest_group`: among the rows of one device (aligned blocks of 256 rows) no index is named more than 16 times, a bound that some block reaches. `dest_row`: several vision tokens may land on one row; their embeddings are then all added.
All inputs are finite; a program needn't handle non-finite values.
Results may differ from a plain program's by a relative error of at most 0.008.
Values may be sent and summed in bfloat16 or wider, within the bound.
No kernel may reach another device: no remote copies, remote signals or barrier semaphores. Data moves between devices by JAX's collectives and lax.ppermute only.
A program may use at most 128 MiB of HBM per device.

v0:
```python
import jax
import jax.numpy as jnp
from jax import lax
from jax.sharding import PartitionSpec as P


def gelu_exact(x):
    return x * 0.5 * (1.0 + lax.erf(x * 0.7071067811865476))


def gelu_slope(x):
    return (
        0.5 * (1.0 + lax.erf(x * 0.7071067811865476))
        + x * jnp.exp(-0.5 * x * x) * 0.3989422804014327
    )


def body(patches, norm_gain, w_in, b_in, w_out, b_out, text_rows, dest_group, dest_row, grad_rows):
    whole = lax.all_gather(patches, "tensor", axis=1, tiled=True)
    values = whole.astype(jnp.float32)
    scale = lax.rsqrt(jnp.mean(values * values, axis=-1, keepdims=True) + 1e-06)
    normed = (values * scale * norm_gain).astype(jnp.bfloat16)
    count = normed.shape[0] // 4
    merged = normed.reshape(count, 4 * normed.shape[1])
    pre = (
        jnp.dot(
            merged,
            lax.all_gather(w_in, "seq", axis=0, tiled=True),
            preferred_element_type=jnp.float32,
        )
        + b_in
    )
    hidden = gelu_exact(pre).astype(jnp.bfloat16)
    w_full = lax.all_gather(w_out, "seq", axis=1, tiled=True)
    partial_terms = jnp.dot(hidden, w_full, preferred_element_type=jnp.float32)
    summed = lax.psum_scatter(
        partial_terms.astype(jnp.bfloat16), "tensor", scatter_dimension=1, tiled=True
    ).astype(jnp.float32)
    vision = (summed + b_out).astype(jnp.bfloat16)
    groups = lax.axis_size(("section", "seq"))
    capacity = max(2, 2 * count // groups)
    width = vision.shape[1]
    target = dest_group.reshape(-1)
    member = (target[:, None] == jnp.arange(groups, dtype=jnp.int32)[None, :]).astype(jnp.int32)
    slot_of = jnp.sum((jnp.cumsum(member, axis=0) - 1) * member, axis=1)
    code = target * capacity + slot_of
    chosen = jnp.arange(groups * capacity, dtype=jnp.int32)[:, None] == code[None, :]
    select = chosen.astype(jnp.bfloat16)
    send = jnp.dot(select, vision, preferred_element_type=jnp.float32).astype(jnp.bfloat16)
    send_rows = jnp.sum(jnp.where(chosen, dest_row[None, :] + 1, 0), axis=1) - 1
    got, got_rows = (
        lax.all_to_all(
            send.reshape(groups, capacity, width),
            ("section", "seq"),
            split_axis=0,
            concat_axis=0,
            tiled=True,
        ),
        lax.all_to_all(
            send_rows.reshape(groups, capacity),
            ("section", "seq"),
            split_axis=0,
            concat_axis=0,
            tiled=True,
        ),
    )
    got = got.reshape(groups * capacity, width)
    got_rows = got_rows.reshape(1, groups * capacity)
    nrows = text_rows.shape[0]
    place = (jnp.arange(nrows, dtype=jnp.int32)[:, None] == got_rows).astype(jnp.bfloat16)
    placed = jnp.dot(place, got, preferred_element_type=jnp.float32)
    llm_input = (text_rows.astype(jnp.float32) + placed).astype(jnp.bfloat16)
    picked = lax.dot_general(
        place, grad_rows, (((0,), (0,)), ((), ())), preferred_element_type=jnp.float32
    ).astype(jnp.bfloat16)
    returned = lax.all_to_all(
        picked.reshape(groups, capacity, width),
        ("section", "seq"),
        split_axis=0,
        concat_axis=0,
        tiled=True,
    )
    returned = returned.reshape(groups * capacity, width)
    grad_vision = lax.dot_general(
        select, returned, (((0,), (0,)), ((), ())), preferred_element_type=jnp.float32
    ).astype(jnp.bfloat16)
    grad_full = lax.all_gather(grad_vision, "tensor", axis=1, tiled=True)
    back = lax.dot_general(
        grad_full, w_full, (((1,), (1,)), ((), ())), preferred_element_type=jnp.float32
    )
    grad_hidden = (back * gelu_slope(pre)).astype(jnp.bfloat16)
    return (llm_input, grad_hidden)


def solution(mesh):
    in_specs = (
        P(("section", "seq"), "tensor"),
        P(),
        P("seq", "tensor"),
        P("tensor"),
        P("tensor", "seq"),
        P("tensor"),
        P(("section", "seq"), "tensor"),
        P(("section", "seq"), None),
        P(("section", "seq")),
        P(("section", "seq"), "tensor"),
    )
    out_specs = (P(("section", "seq"), "tensor"), P(("section", "seq"), "tensor"))
    return jax.shard_map(body, mesh=mesh, in_specs=in_specs, out_specs=out_specs, check_vma=False)
```

profile of v0, /device:TPU:8, one launch (start us, length us, event | category | flops | bytes accessed | tf_op | source)
XLA Modules:
  0.0 502.0 jit_solution(17264910670204722584)
XLA Ops:
  7.2 0.0 all-gather.5.cloned.1.call-start
  7.2 0.7 all-gather.5.cloned.1.call-update
  7.9 0.0 all-gather.7.cloned.1.call-start
  7.9 0.7 all-gather.7.cloned.1.call-update
  8.6 0.0 all-gather.9.cloned.1.call-start
  8.7 0.7 all-gather.9.cloned.1.call-update
  9.4 0.0 copy-start.2
  9.4 0.0 reduce-scatter.2.cloned.1.call-start
  9.4 38.0 %all-gather.5.cloned.1.call-done = bf16[1024,1280]{0,1:T(8,128)(2,1)} async-done(((bf16[1024,320]{0,1:T(8,128)(2,1)}), bf16[1024,1280]{0,1:T(8,128)(2,1)}) %all-gather.5.cloned.1.call-update) | async-done | bytes 2621456 | tf_op jit(solution)/shard_map/all_gather | solution.py:19
  47.4 0.0 copy-start
  47.4 2.5 fusion
  49.9 0.0 copy-done.2
  49.9 0.0 copy-done
  49.9 0.6 fusion.2
  50.6 2.7 copy.19
  53.3 0.0 copy-start.5
  53.3 4.1 reshape.82
  57.3 110.6 %all-gather.7.cloned.1.call-done = bf16[5120,1280]{1,0:T(8,128)(2,1)} async-done(((bf16[1280,1280]{1,0:T(8,128)(2,1)}), bf16[5120,1280]{1,0:T(8,128)(2,1)}) %all-gather.7.cloned.1.call-update) | async-done | bytes 13107216 | tf_op jit(solution)/shard_map/all_gather | solution.py:28
  167.9 0.0 copy-done.5
  167.9 7.8 %convolution_add_fusion = f32[256,1280]{1,0:T(8,128)} fusion(bf16[256,5120]{1,0:T(8,128)(2,1)S(1)} %reshape.82, bf16[5120,1280]{1,0:T(8,128)(2,1)} %all-gather.7.cloned.1.call-done, f32[1280]{0:T(1024)S(1)} %copy-done.5), kind=kOutput, calls=%fused_computation.10 | convolution fusion | flops 3355770880 | bytes 17044480 | tf_op jit(solution)/shard_map/dot_general | solution.py:26
  175.7 182.7 %all-gather.9.cloned.1.call-done = bf16[1280,8192]{1,0:T(8,128)(2,1)} async-done(((bf16[1280,2048]{1,0:T(8,128)(2,1)}), bf16[1280,8192]{1,0:T(8,128)(2,1)}) %all-gather.9.cloned.1.call-update) | async-done | bytes 20971536 | tf_op jit(solution)/shard_map/all_gather | solution.py:34
  358.4 14.4 %convolution_convert_fusion = bf16[256,8192]{1,0:T(8,128)(2,1)} fusion(bf16[1280,8192]{1,0:T(8,128)(2,1)} %all-gather.9.cloned.1.call-done, f32[256,1280]{1,0:T(8,128)} %convolution_add_fusion), kind=kOutput, calls=%fused_computation | convolution fusion | flops 5372444672 | bytes 26476544 | tf_op jit(solution)/shard_map/dot_general | solution.py:35
  372.8 0.0 reduce-scatter.2.cloned.1.call-update
  372.8 0.0 all-gather.11.cloned.1.call-start
  372.9 0.6 copy-done.1
  373.5 0.6 reduce-window.6
  374.0 0.2 slice_reduce_fusion
  374.3 0.1 fusion.15
  374.4 0.0 copy-done.4
  374.4 0.1 select_reduce_fusion
  374.6 0.1 sub.18
  374.6 14.6 %all_to_all.16 = s32[32,1,16]{2,1,0:T(1,128)S(1)} all-to-all(s32[32,1,16]{2,1,0:T(1,128)S(1)} %bitcast.33), channel_id=1, replica_groups=mesh['section'=8,'seq'=4,'tensor'=4] {'section','seq'}, dimensions={0} | all-to-all | bytes 4096 | tf_op jit(solution)/shard_map/all_to_all | solution.py:59
  389.3 0.5 broadcast.95
  389.8 0.7 reduce.5
  390.5 0.1 eq.62
  390.6 4.7 convolution_convert_fusion.1
  395.2 31.2 %all_to_all.17 = bf16[32,16,2048]{2,1,0:T(8,128)(2,1)S(1)} all-to-all(bf16[32,16,2048]{2,1,0:T(8,128)(2,1)S(1)} %bitcast.32), channel_id=1, replica_groups=mesh['section'=8,'seq'=4,'tensor'=4] {'section','seq'}, dimensions={0} | all-to-all | bytes 4194304 | tf_op jit(solution)/shard_map/all_to_all | solution.py:76
  426.5 1.7 convolution_convert_fusion.3
  428.2 0.0 all-gather.11.cloned.1.call-update
  428.2 0.0 reduce-scatter.2.cloned.1.call-done
  428.2 0.0 copy-done.3
  428.3 3.3 convolution_convert_fusion.2
  431.5 5.4 %all-to-all-start.1 = ((bf16[32,16,2048]{2,1,0:T(8,128)(2,1)}), bf16[32,16,2048]{2,1,0:T(8,128)(2,1)S(1)}, u32[]{:S(2)}, u32[]{:S(2)}) async-start(bf16[32,16,2048]{2,1,0:T(8,128)(2,1)} %bitcast.4), calls=%async_computation.2 | async-start | bytes 4194304 | tf_op jit(solution)/shard_map/all_to_all | solution.py:52
  437.0 39.0 %all-gather.11.cloned.1.call-done = bf16[256,8192]{1,0:T(8,128)(2,1)} async-done(((bf16[256,2048]{1,0:T(8,128)(2,1)}), bf16[256,8192]{1,0:T(8,128)(2,1)}) %all-gather.11.cloned.1.call-update) | async-done | bytes 4194320 | tf_op jit(solution)/shard_map/all_gather | solution.py:87
  476.0 0.0 copy-done.6
  476.0 12.9 %fusion.3 = bf16[256,1280]{1,0:T(8,128)(2,1)} fusion(bf16[256,8192]{1,0:T(8,128)(2,1)} %all-gather.11.cloned.1.call-done, bf16[1280,8192]{1,0:T(8,128)(2,1)} %all-gather.9.cloned.1.call-done, f32[256,1280]{1,0:T(8,128)S(1)} %copy-done.6), kind=kOutput, calls=%fused_computation.11 | convolution fusion | flops 5371985920 | bytes 27131904 | tf_op jit(solution)/shard_map/dot_general | solution.py:88
  488.9 0.0 all-to-all-done.1
  488.9 6.6 %add_convert_fusion = bf16[1024,2048]{1,0:T(8,128)(2,1)} fusion(bf16[1024,2048]{1,0:T(8,128)(2,1)} %param.16, bf16[512,2048]{1,0:T(8,128)(2,1)S(1)} %bitcast.31, s32[512]{0:T(512)S(1)} %eq.62), kind=kOutput, calls=%fused_computation.1 | convolution fusion | flops 2154299392 | bytes 10487808 | tf_op jit(solution)/shard_map/dot_general | solution.py:71
  (11 shorter events, 0.1 us)
Async XLA Ops:
  7.2 40.2 %all-gather.5.cloned.1.call-start = ((), (), s32[]{:S(2)}) async-start(), calls=%async_computation.4 | async-start | bytes 3276800 | tf_op jit(solution)/shard_map/all_gather | solution.py:19
  7.9 160.0 %all-gather.7.cloned.1.call-start = ((), (), s32[]{:S(2)}) async-start(), calls=%async_computation.5 | async-start | bytes 16384000 | tf_op jit(solution)/shard_map/all_gather | solution.py:28
  8.6 349.8 %all-gather.9.cloned.1.call-start = ((), (), s32[]{:S(2)}) async-start(), calls=%async_computation.6 | async-start | bytes 26214400 | tf_op jit(solution)/shard_map/all_gather | solution.py:34
  9.4 40.5 %copy-start.2 = (f32[1280]{0:T(1024)S(1)}, f32[1280]{0:T(1024)}, u32[]{:S(2)}) copy-start(f32[1280]{0:T(1024)} %param.11) | copy-start | bytes 15364
  9.4 418.8 %reduce-scatter.2.cloned.1.call-start = ((), (), s32[]{:S(2)}) async-start(), calls=%async_computation.7 | async-start | bytes 5242880 | tf_op jit(solution)/shard_map/reduce_scatter | solution.py:36
  47.4 2.5 copy-start
  53.3 114.7 %copy-start.5 = (f32[1280]{0:T(1024)S(1)}, f32[1280]{0:T(1024)}, u32[]{:S(2)}) copy-start(f32[1280]{0:T(1024)} %param.13) | copy-start | bytes 15364
  372.8 0.7 copy-start.1
  372.8 1.6 copy-start.4
  372.8 103.2 %all-gather.11.cloned.1.call-start = ((), (), s32[]{:S(2)}) async-start(), calls=%async_computation.8 | async-start | bytes 5242880 | tf_op jit(solution)/shard_map/all_gather | solution.py:87
  426.5 1.8 copy-start.3
  431.5 44.5 %copy-start.6 = (f32[256,1280]{1,0:T(8,128)S(1)}, f32[256,1280]{1,0:T(8,128)}, u32[]{:S(2)}) copy-start(f32[256,1280]{1,0:T(8,128)} %convolution_add_fusion) | copy-start | bytes 3932164
  431.5 57.4 %all-to-all-start.1 = ((bf16[32,16,2048]{2,1,0:T(8,128)(2,1)}), bf16[32,16,2048]{2,1,0:T(8,128)(2,1)S(1)}, u32[]{:S(2)}, u32[]{:S(2)}) async-start(bf16[32,16,2048]{2,1,0:T(8,128)(2,1)} %bitcast.4), calls=%async_computation.2 | async-start | bytes 4194304 | tf_op jit(solution)/shard_map/all_to_all | solution.py:52
Sparse Core Ops, SparseCore 0:
  9.7 37.6 all-gather.4
  49.1 118.8 all-gather.6
  169.6 188.7 all-gather.8
  372.9 49.6 reduce-scatter.1
  428.3 47.6 all-gather.10
where the time goes:
time: 503 us; the launch traced here: 502 us
  waiting for transfers between devices  372 us (74%)
  matrix products  51.3 us (10%)
  blocking collectives  45.9 us (9%)
  between operations  13.9 us (3%)
  local copies, waits for them, and re-layouts  8.25 us (2%)
  starting transfers between devices  5.64 us (1%)
    all_gather x1, waiting for transfers between devices, body(): w_full = lax.all_gather(w_out, 'seq', axis=1, tiled=True)  183 us
    all_gather x1, waiting for transfers between devices, body(): lax.all_gather(w_in, 'seq', axis=0, tiled=True)  111 us
    all_gather x1, waiting for transfers between devices, body(): grad_full = lax.all_gather(grad_vision, 'tensor', axis=1, tiled=True)  39 us
    all_gather x1, waiting for transfers between devices, body(): whole = lax.all_gather(patches, 'tensor', axis=1, tiled=True)  38 us
    all_to_all x1, blocking collectives, body(): lax.all_to_all(picked.reshape(groups, capacity, width), ('section', 'seq'...  31.2 us
    all_to_all x1, blocking collectives, body(): lax.all_to_all(send_rows.reshape(groups, capacity), ('section', 'seq'), s...  14.6 us
    dot_general x1, matrix products, body(): partial_terms = jnp.dot(hidden, w_full, preferred_element_type=jnp.float32)  14.4 us
    dot_general x1, matrix products, body(): lax.dot_general(grad_full, w_full, (((1,), (1,)), ((), ())), preferred_el...  12.9 us
  transfers between devices with their start and end apart: 6, of which 4 were waited for; matrix products, arithmetic and copies ran while one was open for 8% of the time, Pallas kernels for 0%

commit v1 on v0

v1 whole, which is shorter than its diff:
```python
import functools

import jax
import jax.numpy as jnp
from jax import lax
from jax.experimental import pallas as pl
from jax.experimental.pallas import tpu as pltpu
from jax.sharding import PartitionSpec as P

PLANE = ("section", "seq")
VMEM = pl.BlockSpec(memory_space=pltpu.VMEM)
SMEM = pl.BlockSpec(memory_space=pltpu.SMEM)
ANY = pl.BlockSpec(memory_space=pl.ANY)


def spot(x, y, c):
    return ((x % 4) * 4 + (y % 4)) * 2 + c


CHIPS = [(x, y, c) for x in range(4) for y in range(4) for c in range(2)]
CORE = [(spot(x, y, c), spot(x, y, 1 - c)) for x, y, c in CHIPS]
ALONG_Y = [(spot(x, y, c), spot(x, y + 1 - 2 * c, c)) for x, y, c in CHIPS]
ALONG_X = [(spot(x, y, c), spot(x + 1 - 2 * c, y, c)) for x, y, c in CHIPS]


def move(value, pairs):
    return lax.ppermute(value, PLANE, pairs)


def gather_pieces(own, axis, core, parity):
    size = own.shape[axis] // 2
    mine = lax.dynamic_slice_in_dim(own, core * size, size, axis)
    other = lax.dynamic_slice_in_dim(own, (1 - core) * size, size, axis)
    s1 = move(other, CORE)
    p1 = move(jnp.where(core == parity, mine, s1), ALONG_Y)
    p2 = move(p1, ALONG_X)
    s2 = move(mine, CORE)
    f1 = move(p1, CORE)
    f2 = move(p2, CORE)
    return own, s1, s2, p1, f1, p2, f2


def fetch(pieces, buffer, sems, axis):
    own, rest = pieces[0], pieces[1:]
    size = own.shape[axis] // 2
    halves = [own.at[pl.ds(h * size, size)] if axis == 0 else own.at[:, pl.ds(h * size, size)] for h in range(2)]
    copies = [pltpu.make_async_copy(s, buffer.at[i], sems.at[i]) for i, s in enumerate([*halves, *rest])]
    for copy in copies:
        copy.start()
    return copies


def merge_kernel(x_ref, gain_ref, out_ref):
    rows = 256
    tokens = rows // 4
    width = x_ref.shape[0]
    r = lax.broadcasted_iota(jnp.int32, (rows, rows), 1)
    q = lax.broadcasted_iota(jnp.int32, (rows, rows), 0)
    pick = (r == (q % tokens) * 4 + q // tokens).astype(jnp.bfloat16)
    for j in range(x_ref.shape[1] // rows):
        v = lax.dot_general(
            pick, x_ref[:, j * rows:(j + 1) * rows], (((1,), (1,)), ((), ())), preferred_element_type=jnp.float32
        )
        scale = lax.rsqrt(jnp.mean(v * v, axis=-1, keepdims=True) + 1e-06)
        n = (v * scale * gain_ref[...]).astype(jnp.bfloat16)
        for p in range(4):
            out_ref[j * tokens:(j + 1) * tokens, p * width:(p + 1) * width] = n[p * tokens:(p + 1) * tokens]


def merge(x, gain):
    width, rows = x.shape
    return pl.pallas_call(
        merge_kernel,
        out_shape=jax.ShapeDtypeStruct((rows // 4, 4 * width), jnp.bfloat16),
        in_specs=[VMEM, VMEM],
        out_specs=VMEM,
        compiler_params=pltpu.CompilerParams(vmem_limit_bytes=40 << 20),
        cost_estimate=pl.CostEstimate(flops=1 << 30, bytes_accessed=6 << 20, transcendentals=0),
    )(x, gain.reshape(1, -1))


def first_kernel(place_ref, x_ref, b_ref, *refs):
    pieces, (hidden_ref, slope_ref, buffer, acc, sems) = refs[:7], refs[7:]
    copies = fetch(pieces, buffer, sems, 0)
    depth = buffer.shape[1]
    for i, copy in enumerate(copies):
        copy.wait()
        at = pl.multiple_of(place_ref[i] * depth, 128)
        part = jnp.dot(x_ref[:, pl.ds(at, depth)], buffer[i], preferred_element_type=jnp.float32)
        if i == 0:
            acc[...] = part
        else:
            acc[...] += part
    pre = acc[...] + b_ref[...]
    phi = 0.5 * (1.0 + lax.erf(pre * 0.7071067811865476))
    hidden_ref[...] = (pre * phi).astype(jnp.bfloat16)
    slope_ref[...] = phi + pre * jnp.exp(-0.5 * pre * pre) * 0.3989422804014327


def first(place, x, b, pieces):
    rows, cols = x.shape[0], pieces[0].shape[1]
    return pl.pallas_call(
        first_kernel,
        out_shape=(
            jax.ShapeDtypeStruct((rows, cols), jnp.bfloat16),
            jax.ShapeDtypeStruct((rows, cols), jnp.float32),
        ),
        in_specs=[SMEM, VMEM, VMEM] + [ANY] * 7,
        out_specs=(VMEM, VMEM),
        scratch_shapes=[
            pltpu.VMEM((8,) + pieces[1].shape, jnp.bfloat16),
            pltpu.VMEM((rows, cols), jnp.float32),
            pltpu.SemaphoreType.DMA((8,)),
        ],
        compiler_params=pltpu.CompilerParams(vmem_limit_bytes=40 << 20),
        cost_estimate=pl.CostEstimate(flops=34 << 27, bytes_accessed=18 << 20, transcendentals=0),
    )(place, x, b.reshape(1, -1), *pieces)


def second_kernel(place_ref, h_ref, *refs):
    pieces, (out_ref, buffer, sems) = refs[:7], refs[7:]
    copies = fetch(pieces, buffer, sems, 1)
    width = buffer.shape[2]
    for i, copy in enumerate(copies):
        copy.wait()
        part = jnp.dot(h_ref[...], buffer[i], preferred_element_type=jnp.float32)
        at = pl.multiple_of((place_ref[i] % 2) * width, 128)
        out_ref[place_ref[i] // 2, :, pl.ds(at, width)] = part.astype(jnp.bfloat16)


def second(place, h, pieces):
    rows = h.shape[0]
    return pl.pallas_call(
        second_kernel,
        out_shape=jax.ShapeDtypeStruct((4, rows, pieces[0].shape[1]), jnp.bfloat16),
        in_specs=[SMEM, VMEM] + [ANY] * 7,
        out_specs=VMEM,
        scratch_shapes=[
            pltpu.VMEM((8,) + pieces[1].shape, jnp.bfloat16),
            pltpu.SemaphoreType.DMA((8,)),
        ],
        compiler_params=pltpu.CompilerParams(vmem_limit_bytes=40 << 20),
        cost_estimate=pl.CostEstimate(flops=54 << 27, bytes_accessed=26 << 20, transcendentals=0),
    )(place, h, *pieces)


def back_kernel(place_ref, g_ref, slope_ref, *refs):
    pieces, (out_ref, buffer, acc, sems) = refs[:7], refs[7:]
    copies = fetch(pieces, buffer, sems, 1)
    width = buffer.shape[2]
    for i, copy in enumerate(copies):
        copy.wait()
        at = pl.multiple_of((place_ref[i] % 2) * width, 128)
        part = lax.dot_general(
            g_ref[place_ref[i] // 2, :, pl.ds(at, width)],
            buffer[i],
            (((1,), (1,)), ((), ())),
            preferred_element_type=jnp.float32,
        )
        if i == 0:
            acc[...] = part
        else:
            acc[...] += part
    out_ref[...] = (acc[...] * slope_ref[...]).astype(jnp.bfloat16)


def back(place, g, slope, pieces):
    rows, cols = slope.shape
    return pl.pallas_call(
        back_kernel,
        out_shape=jax.ShapeDtypeStruct((rows, cols), jnp.bfloat16),
        in_specs=[SMEM, VMEM, VMEM] + [ANY] * 7,
        out_specs=VMEM,
        scratch_shapes=[
            pltpu.VMEM((8,) + pieces[1].shape, jnp.bfloat16),
            pltpu.VMEM((rows, cols), jnp.float32),
            pltpu.SemaphoreType.DMA((8,)),
        ],
        compiler_params=pltpu.CompilerParams(vmem_limit_bytes=40 << 20),
        cost_estimate=pl.CostEstimate(flops=54 << 27, bytes_accessed=28 << 20, transcendentals=0),
    )(place, g, slope, *pieces)


def body(patches, norm_gain, w_in, b_in, w_out, b_out, text_rows, dest_group, dest_row, grad_rows):
    seq = lax.axis_index("seq")
    core, y_lo = seq % 2, seq // 2
    parity = (lax.axis_index("section") // 2) % 2
    near, far = 2 * y_lo, 2 * (1 - y_lo)
    place = jnp.stack([
        2 * seq, 2 * seq + 1,
        2 * (near + 1 - core) + core, 2 * (near + 1 - core) + 1 - core,
        2 * (far + parity) + core, 2 * (far + parity) + 1 - core,
        2 * (far + 1 - parity) + core, 2 * (far + 1 - parity) + 1 - core,
    ]).astype(jnp.int32)

    whole = lax.all_gather(patches.T, "tensor", axis=0, tiled=True)
    in_pieces = gather_pieces(w_in, 0, core, parity)
    out_pieces = gather_pieces(w_out, 1, core, parity)

    merged = merge(whole, norm_gain)
    hidden, slope = first(place, merged, b_in, in_pieces)
    partial_terms = second(place, hidden, out_pieces)
    summed = lax.psum_scatter(partial_terms, "tensor", scatter_dimension=0, tiled=False).astype(jnp.float32)
    vision = (summed + b_out).astype(jnp.bfloat16)

    count = dest_row.shape[0]
    groups = lax.axis_size(PLANE)
    capacity = max(2, 2 * count // groups)
    width = vision.shape[1]
    target = dest_group.reshape(-1)
    member = (target[:, None] == jnp.arange(groups, dtype=jnp.int32)[None, :]).astype(jnp.int32)
    slot_of = jnp.sum((jnp.cumsum(member, axis=0) - 1) * member, axis=1)
    code = target * capacity + slot_of
    chosen = jnp.arange(groups * capacity, dtype=jnp.int32)[:, None] == code[None, :]
    select = chosen.astype(jnp.bfloat16)
    send_rows = jnp.sum(jnp.where(chosen, dest_row[None, :] + 1, 0), axis=1) - 1
    swap = functools.partial(lax.all_to_all, axis_name=PLANE, split_axis=0, concat_axis=0, tiled=True)
    got_rows = swap(send_rows.reshape(groups, capacity)).reshape(1, groups * capacity)
    nrows = text_rows.shape[0]
    place_rows = (jnp.arange(nrows, dtype=jnp.int32)[:, None] == got_rows).astype(jnp.bfloat16)
    picked = lax.dot_general(
        place_rows, grad_rows, (((0,), (0,)), ((), ())), preferred_element_type=jnp.float32
    ).astype(jnp.bfloat16)
    returned = swap(picked.reshape(groups, capacity, width)).reshape(groups * capacity, width)
    grad_vision = lax.dot_general(
        select, returned, (((0,), (0,)), ((), ())), preferred_element_type=jnp.float32
    ).astype(jnp.bfloat16)
    grad_full = lax.all_gather(grad_vision, "tensor", axis=0, tiled=False)

    send = jnp.dot(select, vision, preferred_element_type=jnp.float32).astype(jnp.bfloat16)
    got = swap(send.reshape(groups, capacity, width)).reshape(groups * capacity, width)
    placed = jnp.dot(place_rows, got, preferred_element_type=jnp.float32)
    llm_input = (text_rows.astype(jnp.float32) + placed).astype(jnp.bfloat16)
    grad_hidden = back(place, grad_full, slope, out_pieces)
    return (llm_input, grad_hidden)


def solution(mesh):
    in_specs = (
        P(("section", "seq"), "tensor"),
        P(),
        P("seq", "tensor"),
        P("tensor"),
        P("tensor", "seq"),
        P("tensor"),
        P(("section", "seq"), "tensor"),
        P(("section", "seq"), None),
        P(("section", "seq")),
        P(("section", "seq"), "tensor"),
    )
    out_specs = (P(("section", "seq"), "tensor"), P(("section", "seq"), "tensor"))
    return jax.shard_map(body, mesh=mesh, in_specs=in_specs, out_specs=out_specs, check_vma=False)
```

time: 503 us -> 260 us (0.52)
  waiting for transfers between devices: 372 us -> 115 us
  matrix products: 51.3 us -> 16.9 us
  Pallas kernels: 0 us -> 33.3 us
  starting transfers between devices: 5.64 us -> 13.2 us
  other arithmetic: 4.69 us -> 10.8 us
    all_gather x4 -> x2, waiting for transfers between devices: 370 us -> 39.6 us  [the longest x1 39.6 us: body(): grad_full = lax.all_gather(grad_vision, 'tensor', axis=0, tiled=False)]
    ppermute x0 -> x12, waiting for transfers between devices: none -> 75.1 us  [move(): return lax.ppermute(value, PLANE, pairs)]
    dot_general x5 -> x2, matrix products: 46.3 us -> 11.8 us  [the longest x1 7.2 us: body(): placed = jnp.dot(place_rows, got, preferred_element_type=jnp.float32)]
    pallas_call x0 -> x4, Pallas kernels: none -> 33.3 us  [the longest x1 12.7 us: back(): pl.pallas_call(back_kernel, out_shape=jax.ShapeDtypeStruct((rows, cols),...]
    select_n x0 -> x2, other arithmetic: none -> 9.21 us  [gather_pieces(): p1 = move(jnp.where(core == parity, mine, s1), ALONG_Y)]
    ppermute x0 -> x12, starting transfers between devices: none -> 7.22 us  [move(): return lax.ppermute(value, PLANE, pairs)]
    unnamed x14 -> x22, local copies, waits for them, and re-layouts: 0.65 us -> 5.89 us
  transfers between devices with their start and end apart: 6 -> 16, of which waited for: 4 -> 8; matrix products, arithmetic and copies ran while one was open for 8% -> 7% of each run, Pallas kernels for 0% -> 9%
where the time goes in v1:
time: 260 us; the launch traced here: 258 us
  waiting for transfers between devices  115 us (44%)
  blocking collectives  43.6 us (17%)
  Pallas kernels  33.3 us (13%)
  matrix products  16.9 us (6%)
  between operations  14 us (5%)
  starting transfers between devices  13.2 us (5%)
  local copies, waits for them, and re-layouts  11.6 us (4%)
  other arithmetic  10.8 us (4%)
    ppermute x12, waiting for transfers between devices, move(): return lax.ppermute(value, PLANE, pairs)  75.1 us
    all_gather x1, waiting for transfers between devices, body(): grad_full = lax.all_gather(grad_vision, 'tensor', axis=0, tiled=False)  39.6 us
    all_to_all x1, blocking collectives, body(): swap(picked.reshape(groups, capacity, width))  31.3 us
    pallas_call x1, Pallas kernels, back(): pl.pallas_call(back_kernel, out_shape=jax.ShapeDtypeStruct((rows, cols),...  12.7 us
    all_to_all x1, blocking collectives, body(): swap(send_rows.reshape(groups, capacity)).reshape(1, groups * capacity)  12.3 us
    pallas_call x1, Pallas kernels, second(): pl.pallas_call(second_kernel, out_shape=jax.ShapeDtypeStruct((4, rows, pi...  11.1 us
    select_n x2, other arithmetic, gather_pieces(): p1 = move(jnp.where(core == parity, mine, s1), ALONG_Y)  9.21 us
    pallas_call x1, Pallas kernels, first(): pl.pallas_call(first_kernel, out_shape=(jax.ShapeDtypeStruct((rows, cols)...  8.07 us
  transfers between devices with their start and end apart: 16, of which 8 were waited for; matrix products, arithmetic and copies ran while one was open for 7% of the time, Pallas kernels for 9%

profile of v1, /device:TPU:8, one launch (start us, length us, event | category | flops | bytes accessed | tf_op | source)
XLA Modules:
  0.0 258.0 jit_solution(5312939137727724146)
XLA Ops:
  7.2 0.0 all-gather.4.cloned.1.call-start
  7.2 3.5 %constant_dynamic-slice_fusion.1 = bf16[1280,1024]{1,0:T(8,128)(2,1)} fusion(bf16[1280,2048]{1,0:T(8,128)(2,1)} %refs_0_.5, s32[]{:T(128)S(6)} %select_n.59), kind=kLoop, calls=%fused_computation.27 | loop fusion | bytes 5242884 | tf_op jit(solution)/shard_map/dynamic_slice | solution.py:33
  10.7 5.1 %collective-permute-done.6.refs_1_ = bf16[1280,1024]{1,0:T(8,128)(2,1)S(1)} collective-permute-done((bf16[1280,1024]{1,0:T(8,128)(2,1)}, bf16[1280,1024]{1,0:T(8,128)(2,1)S(1)}, u32[]{:S(2)}, u32[]{:S(2)}) %collective-permute-start.6) | collective-permute-done | bytes 2621472 | tf_op jit(solution)/shard_map/ppermute | solution.py:27
  15.8 5.7 %broadcast_select_fusion = (bf16[1280,1024]{1,0:T(8,128)(2,1)}, bf16[1280,1024]{1,0:T(8,128)(2,1)}) fusion(bf16[1280,1024]{1,0:T(8,128)(2,1)S(1)} %collective-permute-done.6.refs_1_, pred[]{:T(512)S(6)} %eq.72, bf16[1280,2048]{1,0:T(8,128)(2,1)} %refs_0_.5, s32[]{:T(128)S(6)} %select_n.60), kind=kLoop, calls=%fused_computation.3 | loop fusion | flops 1310720 | bytes 10485765 | tf_op jit(solution)/shard_map/jit(_where)/select_n | solution.py:35
  21.5 1.6 collective-permute-start.8
  23.1 1.3 constant_dynamic-slice_fusion.3
  24.4 3.8 %collective-permute-done.refs_1_ = bf16[640,1280]{1,0:T(8,128)(2,1)} collective-permute-done((bf16[640,1280]{1,0:T(8,128)(2,1)}, bf16[640,1280]{1,0:T(8,128)(2,1)}, u32[]{:S(2)}, u32[]{:S(2)}) %collective-permute-start) | collective-permute-done | bytes 1638432 | tf_op jit(solution)/shard_map/ppermute | solution.py:27
  28.2 3.5 %broadcast_select_fusion.1 = (bf16[640,1280]{1,0:T(8,128)(2,1)}, bf16[640,1280]{1,0:T(8,128)(2,1)}) fusion(bf16[640,1280]{1,0:T(8,128)(2,1)} %collective-permute-done.refs_1_, pred[]{:T(512)S(6)} %eq.72, bf16[1280,1280]{1,0:T(8,128)(2,1)} %refs_0_.3, s32[]{:T(128)S(6)} %select_n.56), kind=kLoop, calls=%fused_computation.8 | loop fusion | flops 819200 | bytes 6553605 | tf_op jit(solution)/shard_map/jit(_where)/select_n | solution.py:35
  31.7 1.3 collective-permute-start.2
  33.0 20.5 %collective-permute-done.8.refs_3_ = bf16[1280,1024]{1,0:T(8,128)(2,1)} collective-permute-done((bf16[1280,1024]{1,0:T(8,128)(2,1)}, bf16[1280,1024]{1,0:T(8,128)(2,1)}, u32[]{:S(2)}, u32[]{:S(2)}) %collective-permute-start.8) | collective-permute-done | bytes 2621472 | tf_op jit(solution)/shard_map/ppermute | solution.py:27
  53.5 1.5 collective-permute-start.10
  55.0 0.0 reduce-scatter.2.cloned.1.call-start
  55.0 0.3 collective-permute-start.1
  55.4 15.6 %collective-permute-done.2.refs_3_ = bf16[640,1280]{1,0:T(8,128)(2,1)} collective-permute-done((bf16[640,1280]{1,0:T(8,128)(2,1)}, bf16[640,1280]{1,0:T(8,128)(2,1)}, u32[]{:S(2)}, u32[]{:S(2)}) %collective-permute-start.2) | collective-permute-done | bytes 1638432 | tf_op jit(solution)/shard_map/ppermute | solution.py:27
  71.0 1.5 collective-permute-start.4
  72.5 0.3 collective-permute-start.7
  72.8 0.2 collective-permute-start.9
  73.0 13.6 %collective-permute-done.10.refs_5_ = bf16[1280,1024]{1,0:T(8,128)(2,1)} collective-permute-done((bf16[1280,1024]{1,0:T(8,128)(2,1)}, bf16[1280,1024]{1,0:T(8,128)(2,1)}, u32[]{:S(2)}, u32[]{:S(2)}) %collective-permute-start.10) | collective-permute-done | bytes 2621472 | tf_op jit(solution)/shard_map/ppermute | solution.py:27
  86.7 1.2 copy-done.3
  87.8 0.5 collective-permute-start.3
  88.3 15.9 %collective-permute-done.4.refs_5_ = bf16[640,1280]{1,0:T(8,128)(2,1)} collective-permute-done((bf16[640,1280]{1,0:T(8,128)(2,1)}, bf16[640,1280]{1,0:T(8,128)(2,1)}, u32[]{:S(2)}, u32[]{:S(2)}) %collective-permute-start.4) | collective-permute-done | bytes 1638432 | tf_op jit(solution)/shard_map/ppermute | solution.py:27
  104.2 0.1 stack.35.place_ref
  104.3 1.7 copy-done
  106.1 1.4 shard_map.113.x_ref
  107.5 0.6 collective-permute-done.5.refs_6_
  108.1 8.1 %shard_map.114 = (bf16[256,1280]{1,0:T(8,128)(2,1)S(1)}, f32[256,1280]{1,0:T(8,128)S(1)}) custom-call(s32[8]{0:T(128)S(1)} %stack.35.place_ref, bf16[256,5120]{1,0:T(8,128)(2,1)S(1)} %shard_map.113.x_ref, f32[1,1280]{1,0:T(1,128)S(1)} %reshape.78.b_ref, bf16[1280,1280]{1,0:T(8,128)(2,1)} %refs_0_.3, bf16[640,1280]{1,0:T(8,128)(2,1)} %collective-permute-done.refs_1_, ...), custom_call_target="tpu_custom_call" | custom-call | flops 4563402752 | bytes 18874368 | tf_op jit(solution)/shard_map/pallas_call | solution.py:102
  116.2 1.1 copy-done.1
  117.2 11.1 %shard_map.115 = bf16[4,256,2048]{2,1,0:T(8,128)(2,1)} custom-call(s32[8]{0:T(128)S(1)} %stack.35.place_ref, bf16[256,1280]{1,0:T(8,128)(2,1)S(1)} %get-tuple-element.4.h_ref, bf16[1280,2048]{1,0:T(8,128)(2,1)} %refs_0_.5, bf16[1280,1024]{1,0:T(8,128)(2,1)S(1)} %collective-permute-done.6.refs_1_, bf16[1280,1024]{1,0:T(8,128)(2,1)} %collective-permute-done.7.refs_2_, ...), custom_call_target="tpu_custom_call" | custom-call | flops 7247757312 | bytes 27262976 | tf_op jit(solution)/shard_map/pallas_call | solution.py:133
  128.4 0.0 all-gather.6.cloned.1.call-start
  128.5 0.6 copy-done.6
  129.1 0.6 reduce-window.6
  129.6 0.2 slice_reduce_fusion
  129.9 0.1 fusion.9
  130.0 0.1 select_reduce_fusion
  130.2 0.1 sub.49
  130.2 12.3 %all_to_all.16 = s32[32,1,16]{2,1,0:T(1,128)S(1)} all-to-all(s32[32,1,16]{2,1,0:T(1,128)S(1)} %bitcast.46), channel_id=1, replica_groups=mesh['section'=8,'seq'=4,'tensor'=4] {'section','seq'}, dimensions={0} | all-to-all | bytes 4096 | tf_op jit(solution)/shard_map/all_to_all | solution.py:218
  142.5 0.5 broadcast.57
  143.0 0.7 reduce.5
  143.7 0.1 eq.69
  143.8 4.6 %convolution_convert_fusion = bf16[512,2048]{1,0:T(8,128)(2,1)S(1)} fusion(bf16[1024,2048]{1,0:T(8,128)(2,1)} %param.19, s32[512]{0:T(512)S(1)} %eq.69), kind=kOutput, calls=%fused_computation.1 | convolution fusion | flops 2149056512 | bytes 6293504 | tf_op jit(solution)/shard_map/dot_general | solution.py:221
  148.4 31.3 %all_to_all.17 = bf16[32,16,2048]{2,1,0:T(8,128)(2,1)S(1)} all-to-all(bf16[32,16,2048]{2,1,0:T(8,128)(2,1)S(1)} %bitcast.44), channel_id=1, replica_groups=mesh['section'=8,'seq'=4,'tensor'=4] {'section','seq'}, dimensions={0} | all-to-all | bytes 4194304 | tf_op jit(solution)/shard_map/all_to_all | solution.py:224
  179.7 1.8 convolution_convert_fusion.2
  181.5 3.3 %convolution_convert_fusion.1 = bf16[512,2048]{1,0:T(8,128)(2,1)} fusion(bf16[1,256,2048]{2,1,0:T(8,128)(2,1)} %reduce-scatter.2.cloned.1.call-done, f32[2048]{0:T(1024)S(1)} %copy-done.7, s32[256]{0:T(256)S(1)} %multiply_add_fusion), kind=kOutput, calls=%fused_computation.2 | convolution fusion | flops 539623424 | bytes 3154944 | tf_op jit(solution)/shard_map/dot_general | solution.py:230
  184.8 5.9 %all-to-all-start.1 = ((bf16[32,16,2048]{2,1,0:T(8,128)(2,1)}), bf16[32,16,2048]{2,1,0:T(8,128)(2,1)}, u32[]{:S(2)}, u32[]{:S(2)}) async-start(bf16[32,16,2048]{2,1,0:T(8,128)(2,1)} %bitcast.41), calls=%async_computation.2 | async-start | bytes 4194304 | tf_op jit(solution)/shard_map/all_to_all | solution.py:231
  190.7 39.6 %all-gather.6.cloned.1.call-done = bf16[1024,2048]{1,0:T(8,128)(2,1)} async-done(((bf16[256,2048]{1,0:T(8,128)(2,1)}), bf16[1024,2048]{1,0:T(8,128)(2,1)}) %all-gather.6.cloned.1.call-update) | async-done | bytes 4194320 | tf_op jit(solution)/shard_map/all_gather | solution.py:228
  230.3 1.3 copy-done.2
  231.6 12.7 %shard_map.116 = bf16[256,1280]{1,0:T(8,128)(2,1)} custom-call(s32[8]{0:T(128)S(1)} %stack.35.place_ref, bf16[4,256,2048]{2,1,0:T(8,128)(2,1)} %bitcast.43, f32[256,1280]{1,0:T(8,128)S(1)} %copy-done.2, bf16[1280,2048]{1,0:T(8,128)(2,1)} %refs_0_.5, bf16[1280,1024]{1,0:T(8,128)(2,1)S(1)} %collective-permute-done.6.refs_1_, ...), custom_call_target="tpu_custom_call" | custom-call | flops 7247757312 | bytes 29360128 | tf_op jit(solution)/shard_map/pallas_call | solution.py:169
  244.3 7.2 %add_convert_fusion = bf16[1024,2048]{1,0:T(8,128)(2,1)} fusion(bf16[1024,2048]{1,0:T(8,128)(2,1)} %param.16, bf16[512,2048]{1,0:T(8,128)(2,1)} %bitcast.15, s32[512]{0:T(512)S(1)} %eq.69), kind=kOutput, calls=%fused_computation | convolution fusion | flops 2154299392 | bytes 10487808 | tf_op jit(solution)/shard_map/dot_general | solution.py:232
  (40 shorter events, 0.2 us)
Async XLA Ops:
  7.2 97.2 %all-gather.4.cloned.1.call-start = ((), (), s32[]{:S(2)}) async-start(), calls=%async_computation.4 | async-start | bytes 3276800 | tf_op jit(solution)/shard_map/all_gather | solution.py:196
  10.7 5.1 %collective-permute-start.6 = (bf16[1280,1024]{1,0:T(8,128)(2,1)}, bf16[1280,1024]{1,0:T(8,128)(2,1)S(1)}, u32[]{:S(2)}, u32[]{:S(2)}) collective-permute-start(bf16[1280,1024]{1,0:T(8,128)(2,1)} %constant_dynamic-slice_fusion.1), channel_id=1, source_target_pairs={{0,4},{4,0},{8,12},{12,8},{16,20},{20,16},{24,28},{28,24},{32,36},... | collective-permute-start | bytes 7864328 | tf_op jit(solution)/shard_map/ppermute | solution.py:27
  10.7 12.4 %copy-start.5 = (bf16[1280,1280]{1,0:T(8,128)(2,1)S(1)}, bf16[1280,1280]{1,0:T(8,128)(2,1)}, u32[]{:S(2)}) copy-start(bf16[1280,1280]{1,0:T(8,128)(2,1)} %refs_0_.3) | copy-start | bytes 9830404
  21.5 32.0 %collective-permute-start.8 = (bf16[1280,1024]{1,0:T(8,128)(2,1)}, bf16[1280,1024]{1,0:T(8,128)(2,1)}, u32[]{:S(2)}, u32[]{:S(2)}) collective-permute-start(bf16[1280,1024]{1,0:T(8,128)(2,1)} %get-tuple-element.6), channel_id=1, source_target_pairs={{0,8},{4,28},{8,16},{12,4},{16,24},{20,12},{24,0},{28,20},{32,40},... | collective-permute-start | bytes 7864328 | tf_op jit(solution)/shard_map/ppermute | solution.py:27
  24.4 3.8 %collective-permute-start = (bf16[640,1280]{1,0:T(8,128)(2,1)}, bf16[640,1280]{1,0:T(8,128)(2,1)}, u32[]{:S(2)}, u32[]{:S(2)}) collective-permute-start(bf16[640,1280]{1,0:T(8,128)(2,1)} %constant_dynamic-slice_fusion.3), channel_id=1, source_target_pairs={{0,4},{4,0},{8,12},{12,8},{16,20},{20,16},{24,28},{28,24},{32,36},... | collective-permute-start | bytes 4915208 | tf_op jit(solution)/shard_map/ppermute | solution.py:27
  24.4 79.8 %copy-start.8 = (f32[1280]{0:T(1024)S(1)}, f32[1280]{0:T(1024)}, u32[]{:S(2)}) copy-start(f32[1280]{0:T(1024)} %param.11) | copy-start | bytes 15364
  24.4 79.9 %copy-start.9 = (f32[1280]{0:T(1024)S(1)}, f32[1280]{0:T(1024)}, u32[]{:S(2)}) copy-start(f32[1280]{0:T(1024)} %param.13) | copy-start | bytes 15364
  31.7 39.3 %collective-permute-start.2 = (bf16[640,1280]{1,0:T(8,128)(2,1)}, bf16[640,1280]{1,0:T(8,128)(2,1)}, u32[]{:S(2)}, u32[]{:S(2)}) collective-permute-start(bf16[640,1280]{1,0:T(8,128)(2,1)} %get-tuple-element.8), channel_id=1, source_target_pairs={{0,8},{4,28},{8,16},{12,4},{16,24},{20,12},{24,0},{28,20},{32,40},... | collective-permute-start | bytes 4915208 | tf_op jit(solution)/shard_map/ppermute | solution.py:27
  53.5 33.2 %collective-permute-start.10 = (bf16[1280,1024]{1,0:T(8,128)(2,1)}, bf16[1280,1024]{1,0:T(8,128)(2,1)}, u32[]{:S(2)}, u32[]{:S(2)}) collective-permute-start(bf16[1280,1024]{1,0:T(8,128)(2,1)} %collective-permute-done.8.refs_3_), channel_id=1, source_target_pairs={{0,32},{4,100},{8,40},{12,108},{16,48},{20,116},{24,56},{28,124},{... | collective-permute-start | bytes 7864328 | tf_op jit(solution)/shard_map/ppermute | solution.py:27
  55.0 126.5 %reduce-scatter.2.cloned.1.call-start = ((), (), s32[]{:S(2)}) async-start(), calls=%async_computation.5 | async-start | bytes 5242880 | tf_op jit(solution)/shard_map/reduce_scatter | solution.py:203
  55.0 31.6 %collective-permute-start.1 = (bf16[640,1280]{1,0:T(8,128)(2,1)}, bf16[640,1280]{1,0:T(8,128)(2,1)S(1)}, u32[]{:S(2)}, u32[]{:S(2)}) collective-permute-start(bf16[640,1280]{1,0:T(8,128)(2,1)} %get-tuple-element.9), channel_id=1, source_target_pairs={{0,4},{4,0},{8,12},{12,8},{16,20},{20,16},{24,28},{28,24},{32,36},... | collective-permute-start | bytes 4915208 | tf_op jit(solution)/shard_map/ppermute | solution.py:27
  71.0 33.2 %collective-permute-start.4 = (bf16[640,1280]{1,0:T(8,128)(2,1)}, bf16[640,1280]{1,0:T(8,128)(2,1)}, u32[]{:S(2)}, u32[]{:S(2)}) collective-permute-start(bf16[640,1280]{1,0:T(8,128)(2,1)} %collective-permute-done.2.refs_3_), channel_id=1, source_target_pairs={{0,32},{4,100},{8,40},{12,108},{16,48},{20,116},{24,56},{28,124},{... | collective-permute-start | bytes 4915208 | tf_op jit(solution)/shard_map/ppermute | solution.py:27
  72.5 44.7 %collective-permute-start.7 = (bf16[1280,1024]{1,0:T(8,128)(2,1)}, bf16[1280,1024]{1,0:T(8,128)(2,1)}, u32[]{:S(2)}, u32[]{:S(2)}) collective-permute-start(bf16[1280,1024]{1,0:T(8,128)(2,1)} %get-tuple-element.7), channel_id=1, source_target_pairs={{0,4},{4,0},{8,12},{12,8},{16,20},{20,16},{24,28},{28,24},{32,36},... | collective-permute-start | bytes 7864328 | tf_op jit(solution)/shard_map/ppermute | solution.py:27
  72.8 44.4 %collective-permute-start.9 = (bf16[1280,1024]{1,0:T(8,128)(2,1)}, bf16[1280,1024]{1,0:T(8,128)(2,1)}, u32[]{:S(2)}, u32[]{:S(2)}) collective-permute-start(bf16[1280,1024]{1,0:T(8,128)(2,1)} %collective-permute-done.8.refs_3_), channel_id=1, source_target_pairs={{0,4},{4,0},{8,12},{12,8},{16,20},{20,16},{24,28},{28,24},{32,36},... | collective-permute-start | bytes 7864328 | tf_op jit(solution)/shard_map/ppermute | solution.py:27
  86.7 30.6 %collective-permute-start.11 = (bf16[1280,1024]{1,0:T(8,128)(2,1)}, bf16[1280,1024]{1,0:T(8,128)(2,1)}, u32[]{:S(2)}, u32[]{:S(2)}) collective-permute-start(bf16[1280,1024]{1,0:T(8,128)(2,1)} %collective-permute-done.10.refs_5_), channel_id=1, source_target_pairs={{0,4},{4,0},{8,12},{12,8},{16,20},{20,16},{24,28},{28,24},{32,36},... | collective-permute-start | bytes 7864328 | tf_op jit(solution)/shard_map/ppermute | solution.py:27
  86.7 1.2 copy-start.3
  87.8 19.7 %collective-permute-start.3 = (bf16[640,1280]{1,0:T(8,128)(2,1)}, bf16[640,1280]{1,0:T(8,128)(2,1)}, u32[]{:S(2)}, u32[]{:S(2)}) collective-permute-start(bf16[640,1280]{1,0:T(8,128)(2,1)} %collective-permute-done.2.refs_3_), channel_id=1, source_target_pairs={{0,4},{4,0},{8,12},{12,8},{16,20},{20,16},{24,28},{28,24},{32,36},... | collective-permute-start | bytes 4915208 | tf_op jit(solution)/shard_map/ppermute | solution.py:27
  104.2 3.8 %collective-permute-start.5 = (bf16[640,1280]{1,0:T(8,128)(2,1)}, bf16[640,1280]{1,0:T(8,128)(2,1)}, u32[]{:S(2)}, u32[]{:S(2)}) collective-permute-start(bf16[640,1280]{1,0:T(8,128)(2,1)} %collective-permute-done.4.refs_5_), channel_id=1, source_target_pairs={{0,4},{4,0},{8,12},{12,8},{16,20},{20,16},{24,28},{28,24},{32,36},... | collective-permute-start | bytes 4915208 | tf_op jit(solution)/shard_map/ppermute | solution.py:27
  104.3 1.7 copy-start
  106.1 2.0 copy-start.4
  116.1 1.1 copy-start.1
  128.4 0.7 copy-start.6
  128.4 1.6 copy-start.10
  128.4 101.9 %all-gather.6.cloned.1.call-start = ((), (), s32[]{:S(2)}) async-start(), calls=%async_computation.6 | async-start | bytes 5242880 | tf_op jit(solution)/shard_map/all_gather | solution.py:228
  179.7 1.8 copy-start.7
  184.8 59.5 %all-to-all-start.1 = ((bf16[32,16,2048]{2,1,0:T(8,128)(2,1)}), bf16[32,16,2048]{2,1,0:T(8,128)(2,1)}, u32[]{:S(2)}, u32[]{:S(2)}) async-start(bf16[32,16,2048]{2,1,0:T(8,128)(2,1)} %bitcast.41), calls=%async_computation.2 | async-start | bytes 4194304 | tf_op jit(solution)/shard_map/all_to_all | solution.py:231
  230.3 1.3 copy-start.2
Sparse Core Ops, SparseCore 0:
  55.1 37.4 all-gather.3
  128.5 48.1 reduce-scatter.1
  181.6 48.6 all-gather.5

commit v2 on v0

v2 whole, which is shorter than its diff:
```python
import functools

import jax
import jax.numpy as jnp
from jax import lax
from jax.experimental import pallas as pl
from jax.experimental.pallas import tpu as pltpu
from jax.sharding import PartitionSpec as P

PLANE = ("section", "seq")
VMEM = pl.BlockSpec(memory_space=pltpu.VMEM)
SMEM = pl.BlockSpec(memory_space=pltpu.SMEM)
ANY = pl.BlockSpec(memory_space=pl.ANY)
BF16, F32 = jnp.bfloat16, jnp.float32
DIRECT = 384


TOKEN = jax.ShapeDtypeStruct((8, 128), F32)


def spot(x, y, c):
    return ((x % 4) * 4 + (y % 4)) * 2 + c


CHIPS = [(x, y, c) for x in range(4) for y in range(4) for c in range(2)]
CORE = [(spot(x, y, c), spot(x, y, 1 - c)) for x, y, c in CHIPS]
ALONG_Y = [(spot(x, y, c), spot(x, y + 1 - 2 * c, c)) for x, y, c in CHIPS]
ALONG_X = [(spot(x, y, c), spot(x + 1 - 2 * c, y, c)) for x, y, c in CHIPS]


def move(value, pairs):
    return lax.ppermute(value, PLANE, pairs)


def up(value):
    return lax.ppermute(value, "tensor", [(z, (z + 1) % 4) for z in range(4)])


def down(value):
    return lax.ppermute(value, "tensor", [(z, (z + 3) % 4) for z in range(4)])


def after(value, *others):
    return pl.pallas_call(
        lambda *refs: None,
        out_shape=jax.ShapeDtypeStruct(value.shape, value.dtype),
        in_specs=[ANY] * (1 + len(others)),
        out_specs=ANY,
        input_output_aliases={0: 0},
    )(value, *others)


def call(kernel, out_shape, in_specs, out_specs, scratch, flops, moved, *args, limit=46):
    return pl.pallas_call(
        kernel,
        out_shape=out_shape,
        in_specs=in_specs,
        out_specs=out_specs,
        scratch_shapes=scratch,
        compiler_params=pltpu.CompilerParams(vmem_limit_bytes=limit << 20),
        cost_estimate=pl.CostEstimate(flops=flops, bytes_accessed=moved, transcendentals=0),
    )(*args)


def parts_kernel(cuts, info_ref, own_ref, *refs):
    outs, sems = refs[-1 - len(cuts):-1], refs[-1]
    copies = []
    for i, (low, rows, left, cols) in enumerate(cuts):
        if low is None:
            low = pl.multiple_of(info_ref[3] * rows, rows)
        if left is None:
            left = pl.multiple_of(info_ref[3] * cols, cols)
        from_ref = own_ref.at[pl.ds(low, rows), pl.ds(left, cols)]
        copies.append(pltpu.make_async_copy(from_ref, outs[i], sems.at[i]))
    for copy in copies:
        copy.start()
    for copy in copies:
        copy.wait()


def parts_of(info, own, cuts, *tokens):
    out = [jax.ShapeDtypeStruct((rows, cols), BF16) for _, rows, _, cols in cuts]
    return call(
        functools.partial(parts_kernel, cuts), out, [SMEM] + [ANY] * (1 + len(tokens)), [VMEM] * len(out),
        [pltpu.SemaphoreType.DMA((len(out),))], 0, 2 * own.size, info, own, *tokens,
    )


def merge_kernel(info_ref, gain_ref, own_ref, *refs):
    parts, (out_ref, token_ref, x_ref, sems) = refs[:4], refs[4:]
    token_ref[...] = jnp.zeros_like(token_ref)
    z = info_ref[0]
    size = own_ref.shape[0] // 2
    width = 8 * size
    copies = []
    for i, (ref, step, half) in enumerate(zip((own_ref, *parts), (0, 3, 1, 2, 2), (0, 0, 0, 0, 1))):
        at = pl.multiple_of(((z + step) % 4) * 2 * size + half * size, 32)
        copies.append(pltpu.make_async_copy(ref, x_ref.at[pl.ds(at, ref.shape[0])], sems.at[i]))
    for copy in copies:
        copy.start()
    for copy in copies:
        copy.wait()
    rows = 256
    tokens = rows // 4
    r = lax.broadcasted_iota(jnp.int32, (rows, rows), 1)
    q = lax.broadcasted_iota(jnp.int32, (rows, rows), 0)
    pick = (r == (q % tokens) * 4 + q // tokens).astype(BF16)
    for j in range(x_ref.shape[1] // rows):
        v = lax.dot_general(
            pick, x_ref[:, j * rows:(j + 1) * rows], (((1,), (1,)), ((), ())), preferred_element_type=F32
        )
        scale = lax.rsqrt(jnp.mean(v * v, axis=-1, keepdims=True) + 1e-06)
        n = (v * scale * gain_ref[...]).astype(BF16)
        for p in range(4):
            out_ref[j * tokens:(j + 1) * tokens, p * width:(p + 1) * width] = n[p * tokens:(p + 1) * tokens]


def merge(info, gain, own, parts):
    width, rows = 4 * own.shape[0], own.shape[1]
    return call(
        merge_kernel,
        (jax.ShapeDtypeStruct((rows // 4, 4 * width), BF16), TOKEN),
        [SMEM, VMEM] + [ANY] * 5, (VMEM, VMEM),
        [pltpu.VMEM((width, rows), BF16), pltpu.SemaphoreType.DMA((5,))],
        1 << 30, 6 << 20,
        info, gain.reshape(1, -1), own, *parts,
    )


def load_parts(jobs, buffer, sems):
    copies = [pltpu.make_async_copy(ref, buffer.at[i], sems.at[i]) for i, (ref, _, _) in enumerate(jobs)]
    for copy in copies:
        copy.start()
    return copies


def add_parts(jobs, copies, x_ref, buffer, total):
    depth = buffer.shape[1]
    for i, (copy, (_, block, half)) in enumerate(zip(copies, jobs)):
        copy.wait()
        at = pl.multiple_of((2 * block + half) * depth, 128)
        part = jnp.dot(x_ref[:, pl.ds(at, depth)], buffer[i], preferred_element_type=F32)
        total = part if total is None else total + part
    return total


def first_near_kernel(info_ref, x_ref, own_ref, other_ref, out_ref, token_ref, buffer, sems):
    token_ref[...] = jnp.zeros_like(token_ref)
    y_lo, core = info_ref[1], info_ref[2]
    depth = buffer.shape[1]
    jobs = [
        (ref.at[pl.ds(half * depth, depth)], 2 * y_lo + low, half)
        for ref, low in ((own_ref, core), (other_ref, 1 - core)) for half in range(2)
    ]
    out_ref[...] = add_parts(jobs, load_parts(jobs, buffer, sems), x_ref, buffer, None)


def first_far_kernel(info_ref, x_ref, b_ref, near_ref, p1, f1, p2, f2, hidden_ref, slope_ref, buffer, sems):
    y_lo, core, parity = info_ref[1], info_ref[2], info_ref[3]
    far = 2 - 2 * y_lo
    jobs = [
        (p1, far + core, parity), (f1, far + 1 - core, parity),
        (p2, far + core, 1 - parity), (f2, far + 1 - core, 1 - parity),
    ]
    pre = add_parts(jobs, load_parts(jobs, buffer, sems), x_ref, buffer, near_ref[...] + b_ref[...])
    phi = 0.5 * (1.0 + lax.erf(pre * 0.7071067811865476))
    hidden_ref[...] = (pre * phi).astype(BF16)
    slope_ref[...] = phi + pre * jnp.exp(-0.5 * pre * pre) * 0.3989422804014327


def first_scratch(depth, cols):
    return [pltpu.VMEM((4, depth, cols), BF16), pltpu.SemaphoreType.DMA((4,))]


def first_near(info, x, near):
    rows, (depth, cols) = x.shape[0], near[0].shape
    return call(
        first_near_kernel,
        (jax.ShapeDtypeStruct((rows, cols), F32), TOKEN),
        [SMEM, VMEM, ANY, ANY], (VMEM, VMEM), first_scratch(depth // 2, cols), 17 << 27, 9 << 20,
        info, x, *near,
    )


def first_far(info, x, b, total, far):
    rows, (depth, cols) = x.shape[0], far[0].shape
    return call(
        first_far_kernel,
        (jax.ShapeDtypeStruct((rows, cols), BF16), jax.ShapeDtypeStruct((rows, cols), F32)),
        [SMEM, VMEM, VMEM, VMEM] + [ANY] * 4, (VMEM, VMEM), first_scratch(depth, cols), 17 << 27, 12 << 20,
        info, x, b.reshape(1, -1), total, *far,
    )


def near_kernel(info_ref, h_ref, own_ref, other_ref, out_ref, token_ref, buffer, sems):
    token_ref[...] = jnp.zeros_like(token_ref)
    core = info_ref[2]
    width = buffer.shape[2]
    jobs = [(ref, low, half) for ref, low in ((own_ref, core), (other_ref, 1 - core)) for half in range(2)]
    copies = [
        pltpu.make_async_copy(ref.at[:, pl.ds(half * width, width)], buffer.at[i], sems.at[i])
        for i, (ref, _, half) in enumerate(jobs)
    ]
    for copy in copies:
        copy.start()
    for i, (copy, (_, low, half)) in enumerate(zip(copies, jobs)):
        copy.wait()
        part = jnp.dot(h_ref[...], buffer[i], preferred_element_type=F32)
        out_ref[low, :, half * width:(half + 1) * width] = part.astype(BF16)


def far_kernel(info_ref, h_ref, near_ref, p1, f1, p2, f2, direct, crossed, *refs):
    outs, (buffer, whole, sems, out_sems) = refs[:8], refs[8:]
    z, y_lo, core, parity = info_ref[0], info_ref[1], info_ref[2], info_ref[3]
    width = buffer.shape[2]
    jobs = [
        (p1, core, parity), (f1, 1 - core, parity), (p2, core, 1 - parity), (f2, 1 - core, 1 - parity),
    ]
    for i, (ref, low, half) in enumerate(jobs):
        at = pl.ds(pl.multiple_of(half * width, width), width)
        straight = (direct, crossed)[i % 2].at[:, at]
        pltpu.make_async_copy(ref, buffer.at[i, pl.ds(DIRECT, ref.shape[0])], sems.at[i]).start()
        pltpu.make_async_copy(straight, buffer.at[i, pl.ds(0, DIRECT)], sems.at[i]).start()
    here = pltpu.make_async_copy(near_ref, whole.at[pl.ds(2 * y_lo, 2)], sems.at[4])
    here.start()
    for i, (_, low, half) in enumerate(jobs):
        pltpu.make_async_copy(buffer.at[i], buffer.at[i], sems.at[i]).wait()
        part = jnp.dot(h_ref[...], buffer[i], preferred_element_type=F32)
        at = pl.multiple_of(half * width, width)
        whole[2 - 2 * y_lo + low, :, pl.ds(at, width)] = part.astype(BF16)
    here.wait()
    copies = []
    for i, step in enumerate((2, 1, 3, 0)):
        for half in range(2):
            from_ref = whole.at[(z + step) % 4, :, pl.ds(half * width, width)]
            copies.append(pltpu.make_async_copy(from_ref, outs[2 * i + half], out_sems.at[2 * i + half]))
    for copy in copies:
        copy.start()
    for copy in copies:
        copy.wait()


def far_terms(info, h, near, pieces):
    rows, width = near.shape[1:]
    out = jax.ShapeDtypeStruct((rows, width // 2), BF16)
    return call(
        far_kernel,
        [out] * 8,
        [SMEM, VMEM, ANY] + [ANY] * 6, [ANY] * 8,
        [
            pltpu.VMEM((4, h.shape[1], width // 2), BF16),
            pltpu.VMEM((4, rows, width), BF16),
            pltpu.SemaphoreType.DMA((5,)),
            pltpu.SemaphoreType.DMA((8,)),
        ],
        27 << 27, 17 << 20,
        info, h, near, *pieces,
    )


def near_blocks(info, h, own, other):
    rows, width = own.shape
    return call(
        near_kernel,
        (jax.ShapeDtypeStruct((2, h.shape[0], width), BF16), TOKEN),
        [SMEM, VMEM, ANY, ANY], (VMEM, VMEM),
        [pltpu.VMEM((4, rows, width // 2), BF16), pltpu.SemaphoreType.DMA((4,))],
        27 << 27, 13 << 20,
        info, h, own, other,
    )


def send_kernel(code_ref, bias_ref, *refs):
    parts, (out_ref, sum_ref) = refs[:6], refs[6:]
    half = parts[0].shape[1]
    for i in range(2):
        at = slice(i * half, (i + 1) * half)
        total = sum(ref[...].astype(F32) for ref in parts[3 * i:3 * i + 3])
        sum_ref[:, at] = (total + bias_ref[:, at]).astype(BF16)
    slots, tokens = out_ref.shape[0], sum_ref.shape[0]
    chosen = lax.broadcasted_iota(jnp.int32, (slots, tokens), 0) == code_ref[...]
    out_ref[...] = jnp.dot(chosen.astype(BF16), sum_ref[...], preferred_element_type=F32).astype(BF16)


def rows_to_send(code, bias, parts, slots):
    rows, half = parts[0].shape
    return call(
        send_kernel,
        jax.ShapeDtypeStruct((slots, 2 * half), BF16),
        [VMEM] * 8, VMEM, [pltpu.VMEM((rows, 2 * half), BF16)],
        4 << 27, 6 << 20,
        code.reshape(1, -1), bias.reshape(1, -1), *parts,
    )


def pick_kernel(at_ref, rows_ref, out_ref, token_ref):
    token_ref[...] = jnp.zeros_like(token_ref)
    slots, rows = out_ref.shape[0], rows_ref.shape[0]
    named = (lax.broadcasted_iota(jnp.int32, (rows, slots), 0) == at_ref[...]).astype(BF16)
    out_ref[...] = lax.dot_general(
        named, rows_ref[...], (((0,), (0,)), ((), ())), preferred_element_type=F32
    ).astype(BF16)


def pick_rows(at, rows):
    slots, (count, width) = at.shape[1], rows.shape
    step = width // 4
    return pl.pallas_call(
        pick_kernel,
        grid=(4,),
        out_shape=(jax.ShapeDtypeStruct((slots, width), BF16), TOKEN),
        in_specs=[pl.BlockSpec((1, slots), lambda i: (0, 0)), pl.BlockSpec((count, step), lambda i: (0, i))],
        out_specs=(pl.BlockSpec((slots, step), lambda i: (0, i)), pl.BlockSpec((8, 128), lambda i: (0, 0))),
        compiler_params=pltpu.CompilerParams(vmem_limit_bytes=46 << 20),
        cost_estimate=pl.CostEstimate(flops=16 << 27, bytes_accessed=6 << 20, transcendentals=0),
    )(at, rows)


def place_kernel(at_ref, text_ref, got_ref, out_ref, token_ref):
    token_ref[...] = jnp.zeros_like(token_ref)
    rows, slots = out_ref.shape[0], got_ref.shape[0]
    named = (lax.broadcasted_iota(jnp.int32, (rows, slots), 0) == at_ref[...]).astype(BF16)
    added = jnp.dot(named, got_ref[...], preferred_element_type=F32)
    out_ref[...] = (text_ref[...].astype(F32) + added).astype(BF16)


def place_rows(at, text, got):
    (count, width), slots = text.shape, got.shape[0]
    step = width // 4
    return pl.pallas_call(
        place_kernel,
        grid=(4,),
        out_shape=(jax.ShapeDtypeStruct(text.shape, BF16), TOKEN),
        in_specs=[
            pl.BlockSpec((1, slots), lambda i: (0, 0)),
            pl.BlockSpec((count, step), lambda i: (0, i)),
            pl.BlockSpec((slots, step), lambda i: (0, i)),
        ],
        out_specs=(pl.BlockSpec((count, step), lambda i: (0, i)), pl.BlockSpec((8, 128), lambda i: (0, 0))),
        compiler_params=pltpu.CompilerParams(vmem_limit_bytes=60 << 20),
        cost_estimate=pl.CostEstimate(flops=16 << 27, bytes_accessed=10 << 20, transcendentals=0),
    )(at, text, got)


def home_kernel(code_ref, rows_ref, _, *outs):
    slots, tokens = rows_ref.shape[0], outs[0].shape[0]
    chosen = lax.broadcasted_iota(jnp.int32, (slots, tokens), 0) == code_ref[...]
    width = outs[0].shape[1]
    for i, out_ref in enumerate(outs):
        out_ref[...] = lax.dot_general(
            chosen.astype(BF16),
            rows_ref[:, i * width:(i + 1) * width],
            (((0,), (0,)), ((), ())),
            preferred_element_type=F32,
        ).astype(BF16)


def gradients_home(code, rows, token):
    half = jax.ShapeDtypeStruct((code.shape[0], rows.shape[1] // 2), BF16)
    return call(
        home_kernel, (half, half), [VMEM, VMEM, ANY], (VMEM, VMEM), [],
        4 << 27, 3 << 20, code.reshape(1, -1), rows, token,
    )


def load_any(slot, sem, info_ref, block, half, own, other, p1, f1, p2, f2, direct, crossed):
    y_lo, core, parity = info_ref[1], info_ref[2], info_ref[3]
    width = slot.shape[1]
    at = pl.ds(half * width, width)
    near, low = block // 2 == y_lo, block % 2
    for ref, same in ((own, low == core), (other, low != core)):
        @pl.when(jnp.logical_and(near, same))
        def _():
            pltpu.make_async_copy(ref.at[:, at], slot, sem).start()

    far = jnp.logical_not(near)
    for ref, same in ((direct, low == core), (crossed, low != core)):
        @pl.when(jnp.logical_and(far, same))
        def _():
            pltpu.make_async_copy(ref.at[:, at], slot.at[pl.ds(0, DIRECT)], sem).start()

    for ref, test in (
        (p1, jnp.logical_and(low == core, half == parity)),
        (f1, jnp.logical_and(low != core, half == parity)),
        (p2, jnp.logical_and(low == core, half != parity)),
        (f2, jnp.logical_and(low != core, half != parity)),
    ):
        @pl.when(jnp.logical_and(far, test))
        def _():
            pltpu.make_async_copy(ref, slot.at[pl.ds(DIRECT, ref.shape[0])], sem).start()


def back_kernel(steps, starts, ends, info_ref, *refs):
    refs = list(refs)
    grads = [refs.pop(0) for _ in steps]
    before = None if starts else refs.pop(0)
    slope_ref = refs.pop(0) if ends else None
    pieces = [refs.pop(0) for _ in range(8)]
    out_ref, buffer, sems = refs[-3:]
    z = info_ref[0]
    for i, (step, half) in enumerate(steps):
        load_any(buffer.at[i], sems.at[i], info_ref, (z + step) % 4, half, *pieces)
    total = None if starts else before[...]
    for i in range(len(steps)):
        pltpu.make_async_copy(buffer.at[i], buffer.at[i], sems.at[i]).wait()
        part = lax.dot_general(grads[i][...], buffer[i], (((1,), (1,)), ((), ())), preferred_element_type=F32)
        total = part if total is None else total + part
    out_ref[...] = (total * slope_ref[...]).astype(BF16) if ends else total


def back(info, steps, grads, before, slope, pieces, *tokens):
    rows, (depth, width) = grads[0].shape[0], pieces[0].shape
    extra = [a for a in (before, slope) if a is not None]
    out = jax.ShapeDtypeStruct((rows, depth), F32 if slope is None else BF16)
    return call(
        functools.partial(back_kernel, steps, before is None, slope is not None),
        out,
        [SMEM] + [VMEM] * (len(grads) + len(extra)) + [ANY] * (8 + len(tokens)), VMEM,
        [pltpu.VMEM((len(steps), depth, width // 2), BF16), pltpu.SemaphoreType.DMA((len(steps),))],
        len(steps) * 7 << 27, len(steps) * 3 << 20,
        info, *grads, *extra, *pieces, *tokens, limit=60 if slope is not None else 46,
    )


def body(patches, norm_gain, w_in, b_in, w_out, b_out, text_rows, dest_group, dest_row, grad_rows):
    seq = lax.axis_index("seq")
    core, y_lo = seq % 2, seq // 2
    parity = (lax.axis_index("section") // 2) % 2
    z = lax.axis_index("tensor")
    info = jnp.stack([z, y_lo, core, parity]).astype(jnp.int32)

    count = dest_row.shape[0]
    groups = lax.axis_size(PLANE)
    capacity = max(2, 2 * count // groups)
    width = grad_rows.shape[1]
    target = dest_group.reshape(-1)
    member = (target[:, None] == jnp.arange(groups, dtype=jnp.int32)[None, :]).astype(jnp.int32)
    slot_of = jnp.sum((jnp.cumsum(member, axis=0) - 1) * member, axis=1)
    code = target * capacity + slot_of
    chosen = jnp.arange(groups * capacity, dtype=jnp.int32)[:, None] == code[None, :]
    send_rows = jnp.sum(jnp.where(chosen, dest_row[None, :] + 1, 0), axis=1) - 1
    swap = functools.partial(lax.all_to_all, axis_name=PLANE, split_axis=0, concat_axis=0, tiled=True)
    got_rows = swap(send_rows.reshape(groups, capacity)).reshape(1, groups * capacity)

    rows, cols = w_in.shape
    p1_in = move(parts_of(info, w_in, [(None, rows // 2, 0, cols)])[0], ALONG_Y)
    other_in = move(w_in, CORE)
    other_out = move(w_out, CORE)
    x = patches.T
    size = x.shape[0] // 2
    xa, xb = up(x), down(x)
    xc1, xc2 = up(xa[:size]), down(xb[size:])
    rows, cols = w_out.shape
    relayed, straight = parts_of(
        info, w_out, [(DIRECT, rows - DIRECT, None, cols // 2), (0, DIRECT, 0, cols)]
    )
    p1_in = after(p1_in, relayed, other_in, other_out, got_rows, xa, xb)
    p2_in = move(p1_in, ALONG_X)
    f1_in = move(p1_in, CORE)
    p1 = move(after(relayed, p1_in), ALONG_Y)
    picked, picked_token = pick_rows(got_rows, grad_rows)
    merged, merged_token = merge(info, norm_gain, x, (xa, xb, xc1, xc2))
    total, first_token = first_near(info, merged, (w_in, other_in))
    p1 = after(p1, first_token, picked_token)
    p2 = move(p1, ALONG_X)
    f1 = move(p1, CORE)
    direct = move(after(straight, p1), ALONG_Y)

    hidden, slope = first_far(info, merged, b_in, total, (p1_in, f1_in, p2_in, move(p2_in, CORE)))
    near, near_token = near_blocks(info, hidden, w_out, other_out)
    p2, direct = after(p2, near_token), after(direct, near_token)
    picked = after(picked, p2, direct)
    f2 = move(p2, CORE)
    crossed = move(direct, CORE)
    t20, t21, t10, t11, t30, t31, t00, t01 = far_terms(info, hidden, near, (p1, f1, p2, f2, direct, crossed))

    returned = swap(picked.reshape(groups, capacity, width)).reshape(groups * capacity, width)

    def add(one, two):
        return (one.astype(F32) + two.astype(F32)).astype(BF16)

    sa1, sa2 = up(t20), down(t21)
    sb1, sb2 = up(t11), down(t30)
    sc1, sc2 = up(add(t10, sa1)), down(add(t31, sa2))
    send = rows_to_send(code, b_out, (t00, sb2, sc1, t01, sb1, sc2), groups * capacity)
    got = swap(send.reshape(groups, capacity, width)).reshape(groups * capacity, width)

    g1, g2 = gradients_home(code, returned, send)
    ga1, ga2 = up(g1), down(g2)
    gb1, gb2 = up(g2), down(g1)
    gc1, gc2 = up(ga1), down(ga2)
    pieces = (w_out, other_out, p1, f1, p2, f2, direct, crossed)
    total = back(info, ((0, 0), (0, 1)), (g1, g2), None, None, pieces)
    total = back(info, ((3, 0), (3, 1), (1, 0), (1, 1)), (ga1, gb1, gb2, ga2), total, None, pieces)
    llm_input, placed = place_rows(got_rows, text_rows, got)
    grad_hidden = back(info, ((2, 0), (2, 1)), (gc1, gc2), total, slope, pieces, placed)

    return (llm_input, grad_hidden)


def solution(mesh):
    in_specs = (
        P(("section", "seq"), "tensor"),
        P(),
        P("seq", "tensor"),
        P("tensor"),
        P("tensor", "seq"),
        P("tensor"),
        P(("section", "seq"), "tensor"),
        P(("section", "seq"), None),
        P(("section", "seq")),
        P(("section", "seq"), "tensor"),
    )
    out_specs = (P(("section", "seq"), "tensor"), P(("section", "seq"), "tensor"))
    return jax.shard_map(body, mesh=mesh, in_specs=in_specs, out_specs=out_specs, check_vma=False)
```

time: 503 us -> 207 us (0.41)
  waiting for transfers between devices: 372 us -> 64.3 us
  Pallas kernels: 0 us -> 59.5 us
  starting transfers between devices: 5.64 us -> 60.3 us
  matrix products: 51.3 us -> 0 us
  blocking collectives: 45.9 us -> 0 us
  between operations: 13.9 us -> 1.35 us
  local copies, waits for them, and re-layouts: 8.25 us -> 19.1 us
    all_gather x4 -> x0, waiting for transfers between devices: 370 us -> none  [the longest x1 183 us: body(): w_full = lax.all_gather(w_out, 'seq', axis=1, tiled=True)]
    ppermute x0 -> x28, waiting for transfers between devices: none -> 62.6 us  [the longest x8 27.9 us: up(): return lax.ppermute(value, 'tensor', [(z, (z + 1) % 4) for z in range(4)])]
    pallas_call x0 -> x21, Pallas kernels: none -> 59.5 us  [the longest x12 49.5 us: call(): pl.pallas_call(kernel, out_shape=out_shape, in_specs=in_specs, out_specs=...]
    dot_general x7 -> x0, matrix products: 51.3 us -> none  [the longest x1 14.4 us: body(): partial_terms = jnp.dot(hidden, w_full, preferred_element_type=jnp.float32)]
    all_to_all x2 -> x0, blocking collectives: 45.9 us -> none  [the longest x1 31.2 us: body(): lax.all_to_all(picked.reshape(groups, capacity, width), ('section', 'seq'...]
    ppermute x0 -> x28, starting transfers between devices: none -> 38.2 us  [the longest x8 22.6 us: down(): return lax.ppermute(value, 'tensor', [(z, (z + 3) % 4) for z in range(4)])]
    all_to_all x1 -> x3, starting transfers between devices: 5.45 us -> 22 us  [the longest x1 7.56 us: body(): swap(send.reshape(groups, capacity, width))]
    unnamed x14 -> x70, local copies, waits for them, and re-layouts: 0.65 us -> 17 us
  transfers between devices with their start and end apart: 6 -> 31, of which waited for: 4 -> 8; matrix products, arithmetic and copies ran while one was open for 8% -> 2% of each run, Pallas kernels for 0% -> 26%
where the time goes in v2:
time: 207 us
  waiting for transfers between devices  64.3 us (31%)
  starting transfers between devices  60.3 us (29%)
  Pallas kernels  59.5 us (29%)
  local copies, waits for them, and re-layouts  19.1 us (9%)
    pallas_call x12, Pallas kernels, call(): pl.pallas_call(kernel, out_shape=out_shape, in_specs=in_specs, out_specs=...  49.5 us
    ppermute x8, waiting for transfers between devices, up(): return lax.ppermute(value, 'tensor', [(z, (z + 1) % 4) for z in range(4)])  27.9 us
    ppermute x8, starting transfers between devices, down(): return lax.ppermute(value, 'tensor', [(z, (z + 3) % 4) for z in range(4)])  22.6 us
    ppermute x12, waiting for transfers between devices, move(): return lax.ppermute(value, PLANE, pairs)  19.1 us
    unnamed x70, local copies, waits for them, and re-layouts  17 us
    ppermute x8, waiting for transfers between devices, down(): return lax.ppermute(value, 'tensor', [(z, (z + 3) % 4) for z in range(4)])  15.5 us
    ppermute x12, starting transfers between devices, move(): return lax.ppermute(value, PLANE, pairs)  11.9 us
    all_to_all x1, starting transfers between devices, body(): swap(send.reshape(groups, capacity, width))  7.56 us
  transfers between devices with their start and end apart: 31, of which 8 were waited for; matrix products, arithmetic and copies ran while one was open for 2% of the time, Pallas kernels for 26%

profile of v2, /device:TPU:8, one launch (start us, length us, event | category | flops | bytes accessed | tf_op | source)
XLA Modules:
  0.0 206.7 jit_solution(9746896186986311836)
XLA Ops:
  1.3 1.9 copy-done.3
  4.0 1.6 collective-permute-start.5
  5.6 4.0 %collective-permute-start.1 = (bf16[320,1024]{1,0:T(8,128)(2,1)}, bf16[320,1024]{1,0:T(8,128)(2,1)S(1)}, u32[]{:S(2)}, u32[]{:S(2)}) collective-permute-start(bf16[320,1024]{1,0:T(8,128)(2,1)} %bitcast.11.own_ref), channel_id=1, source_target_pairs={{0,3},{1,0},{2,1},{3,2},{4,7},{5,4},{6,5},{7,6},{8,11},{9,8},{10,9... | collective-permute-start | bytes 1966088 | tf_op jit(solution)/shard_map/ppermute | solution.py:40
  11.5 7.2 %all-to-all-start = ((s32[32,1,16]{2,1,0:T(1,128)}), s32[32,1,16]{2,1,0:T(1,128)S(1)}, u32[]{:S(2)}, u32[]{:S(2)}) async-start(s32[32,1,16]{2,1,0:T(1,128)} %bitcast.3), calls=%async_computation | async-start | bytes 32768 | tf_op jit(solution)/shard_map/all_to_all | solution.py:443
  18.7 2.5 %shard_map.116 = (bf16[896,1024]{1,0:T(8,128)(2,1)S(1)}, bf16[384,2048]{1,0:T(8,128)(2,1)S(1)}) custom-call(s32[4]{0:T(128)S(1)} %pad_add_fusion.info_ref, bf16[1280,2048]{1,0:T(8,128)(2,1)} %refs_4_.1), custom_call_target="tpu_custom_call" | custom-call | bytes 5242880 | tf_op jit(solution)/shard_map/pallas_call | solution.py:54
  21.3 1.2 copy-done.7
  22.5 1.2 copy-done.9
  23.7 1.8 all-to-all-done
  28.4 1.6 collective-permute-start.8
  30.0 1.6 collective-permute-start.10
  31.6 4.1 %collective-permute-start.3 = (bf16[160,1024]{1,0:T(8,128)(2,1)S(1)}, bf16[160,1024]{1,0:T(8,128)(2,1)S(1)}, u32[]{:S(2)}, u32[]{:S(2)}) collective-permute-start(bf16[160,1024]{1,0:T(8,128)(2,1)S(1)} %slice.18), channel_id=1, source_target_pairs={{0,3},{1,0},{2,1},{3,2},{4,7},{5,4},{6,5},{7,6},{8,11},{9,8},{10,9... | collective-permute-start | bytes 983048 | tf_op jit(solution)/shard_map/ppermute | solution.py:40
  35.8 1.5 collective-permute-start.7
  37.3 13.8 %collective-permute-done.8.p2 = bf16[640,1280]{1,0:T(8,128)(2,1)} collective-permute-done((bf16[640,1280]{1,0:T(8,128)(2,1)}, bf16[640,1280]{1,0:T(8,128)(2,1)}, u32[]{:S(2)}, u32[]{:S(2)}) %collective-permute-start.8) | collective-permute-done | bytes 1638432 | tf_op jit(solution)/shard_map/ppermute | solution.py:32
  51.1 2.2 %copy-done.23 = bf16[1024,2048]{1,0:T(8,128)(2,1)S(1)} copy-done((bf16[1024,2048]{1,0:T(8,128)(2,1)S(1)}, bf16[1024,2048]{1,0:T(8,128)(2,1)}, u32[]{:S(2)}) %copy-start.23) | copy-done | bytes 4194328
  53.3 3.4 %shard_map.121 = (bf16[512,2048]{1,0:T(8,128)(2,1)S(1)}, f32[8,128]{1,0:T(8,128)S(1)}) custom-call(s32[1,512]{1,0:T(1,128)S(1)} %copy-done.20, bf16[1024,2048]{1,0:T(8,128)(2,1)S(1)} %copy-done.23), custom_call_target="tpu_custom_call" | custom-call | flops 2147483648 | bytes 6291456 | tf_op jit(solution)/shard_map/pallas_call | solution.py:308
  56.8 1.3 copy-done.6
  58.1 3.1 %shard_map.113 = (bf16[256,5120]{1,0:T(8,128)(2,1)S(1)}, f32[8,128]{1,0:T(8,128)}) custom-call(s32[4]{0:T(128)S(1)} %pad_add_fusion.info_ref, f32[1,1280]{1,0:T(1,128)S(1)} %reshape.94.gain_ref, bf16[320,1024]{1,0:T(8,128)(2,1)} %bitcast.11.own_ref, bf16[320,1024]{1,0:T(8,128)(2,1)S(1)} %copy-done.13, bf16[320,1024]{1,0:T(8,128)(2,1)S(1)} %copy-done.11, ...), custom_call_target="tpu_custom_call" | custom-call | flops 1073741824 | bytes 6291456 | tf_op jit(solution)/shard_map/pallas_call | solution.py:54
  61.2 3.8 %shard_map.114 = (f32[256,1280]{1,0:T(8,128)S(1)}, f32[8,128]{1,0:T(8,128)S(1)}) custom-call(s32[4]{0:T(128)S(1)} %pad_add_fusion.info_ref, bf16[256,5120]{1,0:T(8,128)(2,1)S(1)} %get-tuple-element.25.x_ref, bf16[1280,1280]{1,0:T(8,128)(2,1)S(1)} %copy-done.4, bf16[1280,1280]{1,0:T(8,128)(2,1)} %collective-permute-done.4.other_ref.refs_2_), custom_call_target="tpu_custom_call" | custom-call | flops 2281701376 | bytes 9437184 | tf_op jit(solution)/shard_map/pallas_call | solution.py:54
  66.6 1.2 copy-done
  68.2 1.6 collective-permute-start.14
  69.7 2.7 %collective-permute-start.11 = (bf16[896,1024]{1,0:T(8,128)(2,1)S(1)}, bf16[896,1024]{1,0:T(8,128)(2,1)}, u32[]{:S(2)}, u32[]{:S(2)}) collective-permute-start(bf16[896,1024]{1,0:T(8,128)(2,1)S(1)} %copy-done.1), channel_id=1, source_target_pairs={{0,4},{4,0},{8,12},{12,8},{16,20},{20,16},{24,28},{28,24},{32,36},... | collective-permute-start | bytes 5505032 | tf_op jit(solution)/shard_map/ppermute | solution.py:32
  72.4 1.3 copy-done.16
  73.7 6.6 %shard_map.118 = (bf16[256,1280]{1,0:T(8,128)(2,1)S(1)}, f32[256,1280]{1,0:T(8,128)S(1)}) custom-call(s32[4]{0:T(128)S(1)} %pad_add_fusion.info_ref, bf16[256,5120]{1,0:T(8,128)(2,1)} %copy-done.5, f32[1,1280]{1,0:T(1,128)S(1)} %reshape.95.b_ref, f32[256,1280]{1,0:T(8,128)S(1)} %copy-done.16, bf16[640,1280]{1,0:T(8,128)(2,1)} %shard_map.117.p1.refs_1_, ...), custom_call_target="tpu_custom_call" | custom-call | flops 2281701376 | bytes 12582912 | tf_op jit(solution)/shard_map/pallas_call | solution.py:54
  80.4 5.0 %shard_map.119 = (bf16[2,256,2048]{2,1,0:T(8,128)(2,1)S(1)}, f32[8,128]{1,0:T(8,128)S(1)}) custom-call(s32[4]{0:T(128)S(1)} %pad_add_fusion.info_ref, bf16[256,1280]{1,0:T(8,128)(2,1)S(1)} %get-tuple-element.28.h_ref, bf16[1280,2048]{1,0:T(8,128)(2,1)S(1)} %bitcast.32, bf16[1280,2048]{1,0:T(8,128)(2,1)} %collective-permute-done.6.refs_3_.other_ref.refs_6_.refs_5_), custom_call_target="tpu_custom_call" | custom-call | flops 3623878656 | bytes 13631488 | tf_op jit(solution)/shard_map/pallas_call | solution.py:54
  86.0 1.3 copy-done.26
  87.3 5.3 %collective-permute-done.12.refs_0_ = bf16[896,1024]{1,0:T(8,128)(2,1)} collective-permute-done((bf16[896,1024]{1,0:T(8,128)(2,1)}, bf16[896,1024]{1,0:T(8,128)(2,1)}, u32[]{:S(2)}, u32[]{:S(2)}) %collective-permute-start.12) | collective-permute-done | bytes 1835040 | tf_op jit(solution)/shard_map/ppermute | solution.py:32
  93.1 7.2 %all-to-all-start.2 = ((bf16[32,16,2048]{2,1,0:T(8,128)(2,1)}), bf16[32,16,2048]{2,1,0:T(8,128)(2,1)}, u32[]{:S(2)}, u32[]{:S(2)}) async-start(bf16[32,16,2048]{2,1,0:T(8,128)(2,1)} %bitcast.33), calls=%async_computation.2 | async-start | bytes 4194304 | tf_op jit(solution)/shard_map/all_to_all | solution.py:477
  100.4 6.1 %shard_map.126 = (bf16[256,1024]{1,0:T(8,128)(2,1)S(1)}, bf16[256,1024]{1,0:T(8,128)(2,1)S(1)}, bf16[256,1024]{1,0:T(8,128)(2,1)S(1)}, bf16[256,1024]{1,0:T(8,12...) custom-call(s32[4]{0:T(128)S(1)} %pad_add_fusion.info_ref, ...), custom_call_target="tpu_custom_call" | custom-call | flops 3623878656 | bytes 17825792 | tf_op jit(solution)/shard_map/pallas_call | solution.py:54
  106.6 2.0 collective-permute-start.17
  108.6 2.2 %collective-permute-start.20 = (bf16[256,1024]{1,0:T(8,128)(2,1)S(1)}, bf16[256,1024]{1,0:T(8,128)(2,1)S(1)}, u32[]{:S(2)}, u32[]{:S(2)}) collective-permute-start(bf16[256,1024]{1,0:T(8,128)(2,1)S(1)} %get-tuple-element.41), channel_id=1, source_target_pairs={{0,3},{1,0},{2,1},{3,2},{4,7},{5,4},{6,5},{7,6},{8,11},{9,8},{10,9... | collective-permute-start | bytes 1572872 | tf_op jit(solution)/shard_map/ppermute | solution.py:40
  110.8 1.9 collective-permute-start.16
  112.8 10.6 %collective-permute-done.17 = bf16[256,1024]{1,0:T(8,128)(2,1)S(1)} collective-permute-done((bf16[256,1024]{1,0:T(8,128)(2,1)S(1)}, bf16[256,1024]{1,0:T(8,128)(2,1)S(1)}, u32[]{:S(2)}, u32[]{:S(2)}) %collective-permute-start.17) | collective-permute-done | bytes 524320 | tf_op jit(solution)/shard_map/ppermute | solution.py:36
  123.9 3.3 %collective-permute-start.21 = (bf16[256,1024]{1,0:T(8,128)(2,1)S(1)}, bf16[256,1024]{1,0:T(8,128)(2,1)S(1)}, u32[]{:S(2)}, u32[]{:S(2)}) collective-permute-start(bf16[256,1024]{1,0:T(8,128)(2,1)S(1)} %add_convert_fusion), channel_id=1, source_target_pairs={{0,3},{1,0},{2,1},{3,2},{4,7},{5,4},{6,5},{7,6},{8,11},{9,8},{10,9... | collective-permute-start | bytes 1572872 | tf_op jit(solution)/shard_map/ppermute | solution.py:40
  127.2 7.4 %collective-permute-done.16.refs_1_ = bf16[256,1024]{1,0:T(8,128)(2,1)S(1)} collective-permute-done((bf16[256,1024]{1,0:T(8,128)(2,1)S(1)}, bf16[256,1024]{1,0:T(8,128)(2,1)S(1)}, u32[]{:S(2)}, u32[]{:S(2)}) %collective-permute-start.16) | collective-permute-done | bytes 524320 | tf_op jit(solution)/shard_map/ppermute | solution.py:40
  134.6 10.8 %collective-permute-done.18.refs_2_ = bf16[256,1024]{1,0:T(8,128)(2,1)S(1)} collective-permute-done((bf16[256,1024]{1,0:T(8,128)(2,1)S(1)}, bf16[256,1024]{1,0:T(8,128)(2,1)S(1)}, u32[]{:S(2)}, u32[]{:S(2)}) %collective-permute-start.18) | collective-permute-done | bytes 524320 | tf_op jit(solution)/shard_map/ppermute | solution.py:36
  145.4 2.2 %shard_map.127._ = bf16[512,2048]{1,0:T(8,128)(2,1)} custom-call(s32[1,256]{1,0:T(1,128)S(1)} %bitcast_add_fusion.code_ref, f32[1,2048]{1,0:T(1,128)S(1)} %bitcast.34, bf16[256,1024]{1,0:T(8,128)(2,1)S(1)} %get-tuple-element.34.refs_0_, bf16[256,1024]{1,0:T(8,128)(2,1)S(1)} %collective-permute-done.16.refs_1_, ...), custom_call_target="tpu_custom_call" | custom-call | flops 536870912 | bytes 6291456 | tf_op jit(solution)/shard_map/pallas_call | solution.py:54
  147.6 7.6 %all-to-all-start.1 = ((bf16[32,16,2048]{2,1,0:T(8,128)(2,1)}), bf16[32,16,2048]{2,1,0:T(8,128)(2,1)}, u32[]{:S(2)}, u32[]{:S(2)}) async-start(bf16[32,16,2048]{2,1,0:T(8,128)(2,1)} %bitcast.12), calls=%async_computation.1 | async-start | bytes 4194304 | tf_op jit(solution)/shard_map/all_to_all | solution.py:486
  155.1 2.5 %shard_map.130 = (bf16[256,1024]{1,0:T(8,128)(2,1)S(1)}, bf16[256,1024]{1,0:T(8,128)(2,1)S(1)}) custom-call(s32[1,256]{1,0:T(1,128)S(1)} %bitcast_add_fusion.code_ref, bf16[512,2048]{1,0:T(8,128)(2,1)} %bitcast.15.rows_ref, bf16[512,2048]{1,0:T(8,128)(2,1)} %shard_map.127._), custom_call_target="tpu_custom_call" | custom-call | flops 536870912 | bytes 3145728 | tf_op jit(solution)/shard_map/pallas_call | solution.py:54
  157.6 1.3 collective-permute-start.22
  158.9 2.0 collective-permute-start.24
  160.9 1.8 collective-permute-start.27
  162.9 4.2 %shard_map.131.refs_4_ = f32[256,1280]{1,0:T(8,128)S(1)} custom-call(s32[4]{0:T(128)S(1)} %pad_add_fusion.info_ref, bf16[256,1024]{1,0:T(8,128)(2,1)S(1)} %get-tuple-element.44.refs_0_, bf16[256,1024]{1,0:T(8,128)(2,1)S(1)} %get-tuple-element.45.refs_1_, bf16[1280,2048]{1,0:T(8,128)(2,1)} %refs_4_.1, ...), custom_call_target="tpu_custom_call" | custom-call | flops 1879048192 | bytes 6291456 | tf_op jit(solution)/shard_map/pallas_call | solution.py:54
  167.1 6.5 %collective-permute-done.22.refs_0_ = bf16[256,1024]{1,0:T(8,128)(2,1)S(1)} collective-permute-done((bf16[256,1024]{1,0:T(8,128)(2,1)S(1)}, bf16[256,1024]{1,0:T(8,128)(2,1)S(1)}, u32[]{:S(2)}, u32[]{:S(2)}) %collective-permute-start.22) | collective-permute-done | bytes 524320 | tf_op jit(solution)/shard_map/ppermute | solution.py:36
  173.7 3.2 %collective-permute-start.25 = (bf16[256,1024]{1,0:T(8,128)(2,1)S(1)}, bf16[256,1024]{1,0:T(8,128)(2,1)S(1)}, u32[]{:S(2)}, u32[]{:S(2)}) collective-permute-start(bf16[256,1024]{1,0:T(8,128)(2,1)S(1)} %collective-permute-done.24.refs_3_), channel_id=1, source_target_pairs={{0,3},{1,0},{2,1},{3,2},{4,7},{5,4},{6,5},{7,6},{8,11},{9,8},{10,9... | collective-permute-start | bytes 1572872 | tf_op jit(solution)/shard_map/ppermute | solution.py:40
  176.9 8.1 %collective-permute-done.27.refs_2_ = bf16[256,1024]{1,0:T(8,128)(2,1)S(1)} collective-permute-done((bf16[256,1024]{1,0:T(8,128)(2,1)S(1)}, bf16[256,1024]{1,0:T(8,128)(2,1)S(1)}, u32[]{:S(2)}, u32[]{:S(2)}) %collective-permute-start.27) | collective-permute-done | bytes 524320 | tf_op jit(solution)/shard_map/ppermute | solution.py:40
  185.0 6.3 %shard_map.132.refs_2_ = f32[256,1280]{1,0:T(8,128)S(1)} custom-call(s32[4]{0:T(128)S(1)} %pad_add_fusion.info_ref, bf16[256,1024]{1,0:T(8,128)(2,1)S(1)} %collective-permute-done.22.refs_0_, bf16[256,1024]{1,0:T(8,128)(2,1)S(1)} %collective-permute-done.26.refs_1_, bf16[256,1024]{1,0:T(8,128)(2,1)S(1)} %collective-permute-done.27.refs_2_, ...), custom_call_target="tpu_custom_call" | custom-call | flops 3758096384 | bytes 12582912 | tf_op jit(solution)/shard_map/pallas_call | solution.py:54
  192.3 6.6 %shard_map.128 = (bf16[1024,2048]{1,0:T(8,128)(2,1)}, f32[8,128]{1,0:T(8,128)}) custom-call(s32[1,512]{1,0:T(1,128)} %reshape.92.refs_4_.at_ref, bf16[1024,2048]{1,0:T(8,128)(2,1)} %text_ref.1, bf16[512,2048]{1,0:T(8,128)(2,1)} %bitcast.13.got_ref), custom_call_target="tpu_custom_call" | custom-call | flops 2147483648 | bytes 10485760 | tf_op jit(solution)/shard_map/pallas_call | solution.py:330
  199.9 6.6 %shard_map.133 = bf16[256,1280]{1,0:T(8,128)(2,1)} custom-call(s32[4]{0:T(128)} %copy-done.17, bf16[256,1024]{1,0:T(8,128)(2,1)} %copy-done.27, bf16[256,1024]{1,0:T(8,128)(2,1)} %copy-done.28, f32[256,1280]{1,0:T(8,128)} %copy-done.8, f32[256,1280]{1,0:T(8,128)} %copy-done.14, bf16[1280,2048]{1,0:T(8,128)(2,1)} %refs_4_.1, ...), custom_call_target="tpu_custom_call" | custom-call | flops 1879048192 | bytes 6291456 | tf_op jit(solution)/shard_map/pallas_call | solution.py:54
  (127 shorter events, 12.3 us)
Async XLA Ops:
  0.6 26.7 %collective-permute-start.6 = (bf16[1280,2048]{1,0:T(8,128)(2,1)}, bf16[1280,2048]{1,0:T(8,128)(2,1)}, u32[]{:S(2)}, u32[]{:S(2)}) collective-permute-start(bf16[1280,2048]{1,0:T(8,128)(2,1)} %refs_4_.1), channel_id=1, source_target_pairs={{0,4},{4,0},{8,12},{12,8},{16,20},{20,16},{24,28},{28,24},{32,36},... | collective-permute-start | bytes 15728648 | tf_op jit(solution)/shard_map/ppermute | solution.py:32
  0.7 26.6 %collective-permute-start.4 = (bf16[1280,1280]{1,0:T(8,128)(2,1)}, bf16[1280,1280]{1,0:T(8,128)(2,1)}, u32[]{:S(2)}, u32[]{:S(2)}) collective-permute-start(bf16[1280,1280]{1,0:T(8,128)(2,1)} %own_ref.5), channel_id=1, source_target_pairs={{0,4},{4,0},{8,12},{12,8},{16,20},{20,16},{24,28},{28,24},{32,36},... | collective-permute-start | bytes 9830408 | tf_op jit(solution)/shard_map/ppermute | solution.py:32
  3.2 181.7 %copy-start.17 = (s32[4]{0:T(128)}, s32[4]{0:T(128)S(1)}, u32[]{:S(2)}) copy-start(s32[4]{0:T(128)S(1)} %pad_add_fusion.info_ref) | copy-start | bytes 52
  3.2 6.4 %copy-start.29 = (s32[256,1]{0,1:T(1,128)S(1)}, s32[256,1]{0,1:T(1,128)}, u32[]{:S(2)}) copy-start(s32[256,1]{0,1:T(1,128)} %param.17) | copy-start | bytes 3076
  3.2 7.4 %copy-start.32 = (s32[256]{0:T(256)S(1)}, s32[256]{0:T(256)}, u32[]{:S(2)}) copy-start(s32[256]{0:T(256)} %param.18) | copy-start | bytes 3076
  4.0 23.4 %collective-permute-start.5 = (bf16[640,1280]{1,0:T(8,128)(2,1)S(1)}, bf16[640,1280]{1,0:T(8,128)(2,1)}, u32[]{:S(2)}, u32[]{:S(2)}) collective-permute-start(bf16[640,1280]{1,0:T(8,128)(2,1)S(1)} %shard_map.115), channel_id=1, source_target_pairs={{0,8},{4,28},{8,16},{12,4},{16,24},{20,12},{24,0},{28,20},{32,40},... | collective-permute-start | bytes 4915208 | tf_op jit(solution)/shard_map/ppermute | solution.py:32
  5.6 21.7 %collective-permute-start.1 = (bf16[320,1024]{1,0:T(8,128)(2,1)}, bf16[320,1024]{1,0:T(8,128)(2,1)S(1)}, u32[]{:S(2)}, u32[]{:S(2)}) collective-permute-start(bf16[320,1024]{1,0:T(8,128)(2,1)} %bitcast.11.own_ref), channel_id=1, source_target_pairs={{0,3},{1,0},{2,1},{3,2},{4,7},{5,4},{6,5},{7,6},{8,11},{9,8},{10,9... | collective-permute-start | bytes 1966088 | tf_op jit(solution)/shard_map/ppermute | solution.py:40
  9.7 17.7 %collective-permute-start = (bf16[320,1024]{1,0:T(8,128)(2,1)}, bf16[320,1024]{1,0:T(8,128)(2,1)S(1)}, u32[]{:S(2)}, u32[]{:S(2)}) collective-permute-start(bf16[320,1024]{1,0:T(8,128)(2,1)} %bitcast.11.own_ref), channel_id=1, source_target_pairs={{0,1},{1,2},{2,3},{3,0},{4,5},{5,6},{6,7},{7,4},{8,9},{9,10},{10,1... | collective-permute-start | bytes 1966088 | tf_op jit(solution)/shard_map/ppermute | solution.py:36
  11.5 14.0 %all-to-all-start = ((s32[32,1,16]{2,1,0:T(1,128)}), s32[32,1,16]{2,1,0:T(1,128)S(1)}, u32[]{:S(2)}, u32[]{:S(2)}) async-start(s32[32,1,16]{2,1,0:T(1,128)} %bitcast.3), calls=%async_computation | async-start | bytes 32768 | tf_op jit(solution)/shard_map/all_to_all | solution.py:443
  28.4 3.1 %copy-start.11 = (bf16[320,1024]{1,0:T(8,128)(2,1)S(1)}, bf16[320,1024]{1,0:T(8,128)(2,1)}, u32[]{:S(2)}) copy-start(bf16[320,1024]{1,0:T(8,128)(2,1)} %copy-done.10) | copy-start | bytes 1966084
  28.4 7.3 %copy-start.13 = (bf16[320,1024]{1,0:T(8,128)(2,1)S(1)}, bf16[320,1024]{1,0:T(8,128)(2,1)}, u32[]{:S(2)}) copy-start(bf16[320,1024]{1,0:T(8,128)(2,1)} %copy-done.12) | copy-start | bytes 1966084
  28.4 7.4 %copy-start.30 = (f32[1280]{0:T(1024)S(1)}, f32[1280]{0:T(1024)}, u32[]{:S(2)}) copy-start(f32[1280]{0:T(1024)} %param.11) | copy-start | bytes 15364
  28.4 22.7 %copy-start.20 = (s32[1,512]{1,0:T(1,128)S(1)}, s32[1,512]{1,0:T(1,128)}, u32[]{:S(2)}) copy-start(s32[1,512]{1,0:T(1,128)} %reshape.92.refs_4_.at_ref) | copy-start | bytes 6148
  28.4 22.7 %collective-permute-start.8 = (bf16[640,1280]{1,0:T(8,128)(2,1)}, bf16[640,1280]{1,0:T(8,128)(2,1)}, u32[]{:S(2)}, u32[]{:S(2)}) collective-permute-start(bf16[640,1280]{1,0:T(8,128)(2,1)} %shard_map.117.p1.refs_1_), channel_id=1, source_target_pairs={{0,32},{4,100},{8,40},{12,108},{16,48},{20,116},{24,56},{28,124},{... | collective-permute-start | bytes 4915208 | tf_op jit(solution)/shard_map/ppermute | solution.py:32
  30.0 36.7 %collective-permute-start.10 = (bf16[896,1024]{1,0:T(8,128)(2,1)}, bf16[896,1024]{1,0:T(8,128)(2,1)S(1)}, u32[]{:S(2)}, u32[]{:S(2)}) collective-permute-start(bf16[896,1024]{1,0:T(8,128)(2,1)} %shard_map.120), channel_id=1, source_target_pairs={{0,8},{4,28},{8,16},{12,4},{16,24},{20,12},{24,0},{28,20},{32,40},... | collective-permute-start | bytes 5505032 | tf_op jit(solution)/shard_map/ppermute | solution.py:32
  31.6 25.2 %collective-permute-start.3 = (bf16[160,1024]{1,0:T(8,128)(2,1)S(1)}, bf16[160,1024]{1,0:T(8,128)(2,1)S(1)}, u32[]{:S(2)}, u32[]{:S(2)}) collective-permute-start(bf16[160,1024]{1,0:T(8,128)(2,1)S(1)} %slice.18), channel_id=1, source_target_pairs={{0,3},{1,0},{2,1},{3,2},{4,7},{5,4},{6,5},{7,6},{8,11},{9,8},{10,9... | collective-permute-start | bytes 983048 | tf_op jit(solution)/shard_map/ppermute | solution.py:40
  35.7 22.4 %collective-permute-start.2 = (bf16[160,1024]{1,0:T(8,128)(2,1)S(1)}, bf16[160,1024]{1,0:T(8,128)(2,1)S(1)}, u32[]{:S(2)}, u32[]{:S(2)}) collective-permute-start(bf16[160,1024]{1,0:T(8,128)(2,1)S(1)} %slice.17), channel_id=1, source_target_pairs={{0,1},{1,2},{2,3},{3,0},{4,5},{5,6},{6,7},{7,4},{8,9},{9,10},{10,1... | collective-permute-start | bytes 983048 | tf_op jit(solution)/shard_map/ppermute | solution.py:36
  35.8 36.6 %collective-permute-start.7 = (bf16[640,1280]{1,0:T(8,128)(2,1)}, bf16[640,1280]{1,0:T(8,128)(2,1)}, u32[]{:S(2)}, u32[]{:S(2)}) collective-permute-start(bf16[640,1280]{1,0:T(8,128)(2,1)} %shard_map.117.p1.refs_1_), channel_id=1, source_target_pairs={{0,4},{4,0},{8,12},{12,8},{16,20},{20,16},{24,28},{28,24},{32,36},... | collective-permute-start | bytes 4915208 | tf_op jit(solution)/shard_map/ppermute | solution.py:32
  51.1 21.3 %collective-permute-start.9 = (bf16[640,1280]{1,0:T(8,128)(2,1)}, bf16[640,1280]{1,0:T(8,128)(2,1)}, u32[]{:S(2)}, u32[]{:S(2)}) collective-permute-start(bf16[640,1280]{1,0:T(8,128)(2,1)} %collective-permute-done.8.p2), channel_id=1, source_target_pairs={{0,4},{4,0},{8,12},{12,8},{16,20},{20,16},{24,28},{28,24},{32,36},... | collective-permute-start | bytes 4915208 | tf_op jit(solution)/shard_map/ppermute | solution.py:32
  56.8 4.4 %copy-start.21 = (f32[8,128]{1,0:T(8,128)}, f32[8,128]{1,0:T(8,128)S(1)}, u32[]{:S(2)}) copy-start(f32[8,128]{1,0:T(8,128)S(1)} %get-tuple-element.31.refs_2_) | copy-start | bytes 12292
  56.8 4.4 %copy-start.4 = (bf16[1280,1280]{1,0:T(8,128)(2,1)S(1)}, bf16[1280,1280]{1,0:T(8,128)(2,1)}, u32[]{:S(2)}) copy-start(bf16[1280,1280]{1,0:T(8,128)(2,1)} %own_ref.5) | copy-start | bytes 9830404
  61.2 3.8 %copy-start.5 = (bf16[256,5120]{1,0:T(8,128)(2,1)}, bf16[256,5120]{1,0:T(8,128)(2,1)S(1)}, u32[]{:S(2)}) copy-start(bf16[256,5120]{1,0:T(8,128)(2,1)S(1)} %get-tuple-element.25.x_ref) | copy-start | bytes 7864324
  67.9 24.8 %collective-permute-start.12 = (bf16[896,1024]{1,0:T(8,128)(2,1)}, bf16[896,1024]{1,0:T(8,128)(2,1)}, u32[]{:S(2)}, u32[]{:S(2)}) collective-permute-start(bf16[896,1024]{1,0:T(8,128)(2,1)} %shard_map.122.refs_1_.p1.refs_4_.refs_7_.refs_6_), channel_id=1, source_target_pairs={{0,32},{4,100},{8,40},{12,108},{16,48},{20,116},{24,56},{28,124},{... | collective-permute-start | bytes 5505032 | tf_op jit(solution)/shard_map/ppermute | solution.py:32
  68.2 12.2 %slice-start = ((s8[5242880]{0:T(1024)(128)(4,1)}), s8[1048576]{0:T(1024)(128)(4,1)S(1)}, s32[]{:S(2)}) async-start(s8[5242880]{0:T(1024)(128)(4,1)} %bitcast.31), calls=%async_computation.3 | async-start | bytes 2097152
  68.2 24.5 %collective-permute-start.14 = (bf16[384,2048]{1,0:T(8,128)(2,1)}, bf16[384,2048]{1,0:T(8,128)(2,1)}, u32[]{:S(2)}, u32[]{:S(2)}) collective-permute-start(bf16[384,2048]{1,0:T(8,128)(2,1)} %shard_map.124), channel_id=1, source_target_pairs={{0,8},{4,28},{8,16},{12,4},{16,24},{20,12},{24,0},{28,20},{32,40},... | collective-permute-start | bytes 4718600 | tf_op jit(solution)/shard_map/ppermute | solution.py:32
  69.7 30.7 %collective-permute-start.11 = (bf16[896,1024]{1,0:T(8,128)(2,1)S(1)}, bf16[896,1024]{1,0:T(8,128)(2,1)}, u32[]{:S(2)}, u32[]{:S(2)}) collective-permute-start(bf16[896,1024]{1,0:T(8,128)(2,1)S(1)} %copy-done.1), channel_id=1, source_target_pairs={{0,4},{4,0},{8,12},{12,8},{16,20},{20,16},{24,28},{28,24},{32,36},... | collective-permute-start | bytes 5505032 | tf_op jit(solution)/shard_map/ppermute | solution.py:32
  73.7 6.6 %slice-start.1 = ((s8[5242880]{0:T(1024)(128)(4,1)}), s8[4194304]{0:T(1024)(128)(4,1)S(1)}, s32[]{:S(2)}) async-start(s8[5242880]{0:T(1024)(128)(4,1)} %bitcast.31), calls=%async_computation.4 | async-start | bytes 8388608
  80.3 5.1 %copy-start.14 = (f32[256,1280]{1,0:T(8,128)}, f32[256,1280]{1,0:T(8,128)S(1)}, u32[]{:S(2)}) copy-start(f32[256,1280]{1,0:T(8,128)S(1)} %get-tuple-element.46.refs_3_) | copy-start | bytes 3932164
  80.3 5.1 %copy-start.24 = (bf16[256,1280]{1,0:T(8,128)(2,1)}, bf16[256,1280]{1,0:T(8,128)(2,1)S(1)}, u32[]{:S(2)}) copy-start(bf16[256,1280]{1,0:T(8,128)(2,1)S(1)} %get-tuple-element.28.h_ref) | copy-start | bytes 1966084
  92.6 7.8 %collective-permute-start.13 = (bf16[896,1024]{1,0:T(8,128)(2,1)}, bf16[896,1024]{1,0:T(8,128)(2,1)}, u32[]{:S(2)}, u32[]{:S(2)}) collective-permute-start(bf16[896,1024]{1,0:T(8,128)(2,1)} %shard_map.123.p2.refs_1_.refs_6_.refs_9_.refs_8_), channel_id=1, source_target_pairs={{0,4},{4,0},{8,12},{12,8},{16,20},{20,16},{24,28},{28,24},{32,36},... | collective-permute-start | bytes 5505032 | tf_op jit(solution)/shard_map/ppermute | solution.py:32
  92.6 7.8 %collective-permute-start.15 = (bf16[384,2048]{1,0:T(8,128)(2,1)}, bf16[384,2048]{1,0:T(8,128)(2,1)}, u32[]{:S(2)}, u32[]{:S(2)}) collective-permute-start(bf16[384,2048]{1,0:T(8,128)(2,1)} %shard_map.125.direct.refs_2_.refs_8_.refs_11_.refs_10_), channel_id=1, source_target_pairs={{0,4},{4,0},{8,12},{12,8},{16,20},{20,16},{24,28},{28,24},{32,36},... | collective-permute-start | bytes 4718600 | tf_op jit(solution)/shard_map/ppermute | solution.py:32
  93.1 7.3 %copy-start.25 = (bf16[256,1280]{1,0:T(8,128)(2,1)S(1)}, bf16[256,1280]{1,0:T(8,128)(2,1)}, u32[]{:S(2)}) copy-start(bf16[256,1280]{1,0:T(8,128)(2,1)} %copy-done.24) | copy-start | bytes 1966084
  93.1 54.4 %all-to-all-start.2 = ((bf16[32,16,2048]{2,1,0:T(8,128)(2,1)}), bf16[32,16,2048]{2,1,0:T(8,128)(2,1)}, u32[]{:S(2)}, u32[]{:S(2)}) async-start(bf16[32,16,2048]{2,1,0:T(8,128)(2,1)} %bitcast.33), calls=%async_computation.2 | async-start | bytes 4194304 | tf_op jit(solution)/shard_map/all_to_all | solution.py:477
  106.6 38.8 %copy-start.19 = (f32[2048]{0:T(1024)S(1)}, f32[2048]{0:T(1024)}, u32[]{:S(2)}) copy-start(f32[2048]{0:T(1024)} %param.15) | copy-start | bytes 24580
  106.6 16.8 %collective-permute-start.17 = (bf16[256,1024]{1,0:T(8,128)(2,1)S(1)}, bf16[256,1024]{1,0:T(8,128)(2,1)S(1)}, u32[]{:S(2)}, u32[]{:S(2)}) collective-permute-start(bf16[256,1024]{1,0:T(8,128)(2,1)S(1)} %get-tuple-element.37), channel_id=1, source_target_pairs={{0,1},{1,2},{2,3},{3,0},{4,5},{5,6},{6,7},{7,4},{8,9},{9,10},{10,1... | collective-permute-start | bytes 1572872 | tf_op jit(solution)/shard_map/ppermute | solution.py:36
  108.6 15.1 %collective-permute-start.20 = (bf16[256,1024]{1,0:T(8,128)(2,1)S(1)}, bf16[256,1024]{1,0:T(8,128)(2,1)S(1)}, u32[]{:S(2)}, u32[]{:S(2)}) collective-permute-start(bf16[256,1024]{1,0:T(8,128)(2,1)S(1)} %get-tuple-element.41), channel_id=1, source_target_pairs={{0,3},{1,0},{2,1},{3,2},{4,7},{5,4},{6,5},{7,6},{8,11},{9,8},{10,9... | collective-permute-start | bytes 1572872 | tf_op jit(solution)/shard_map/ppermute | solution.py:40
  110.8 23.8 %collective-permute-start.16 = (bf16[256,1024]{1,0:T(8,128)(2,1)S(1)}, bf16[256,1024]{1,0:T(8,128)(2,1)S(1)}, u32[]{:S(2)}, u32[]{:S(2)}) collective-permute-start(bf16[256,1024]{1,0:T(8,128)(2,1)S(1)} %get-tuple-element.35), channel_id=1, source_target_pairs={{0,3},{1,0},{2,1},{3,2},{4,7},{5,4},{6,5},{7,6},{8,11},{9,8},{10,9... | collective-permute-start | bytes 1572872 | tf_op jit(solution)/shard_map/ppermute | solution.py:40
  112.7 21.9 %collective-permute-start.19 = (bf16[256,1024]{1,0:T(8,128)(2,1)S(1)}, bf16[256,1024]{1,0:T(8,128)(2,1)S(1)}, u32[]{:S(2)}, u32[]{:S(2)}) collective-permute-start(bf16[256,1024]{1,0:T(8,128)(2,1)S(1)} %get-tuple-element.39), channel_id=1, source_target_pairs={{0,1},{1,2},{2,3},{3,0},{4,5},{5,6},{6,7},{7,4},{8,9},{9,10},{10,1... | collective-permute-start | bytes 1572872 | tf_op jit(solution)/shard_map/ppermute | solution.py:36
  123.6 21.8 %collective-permute-start.18 = (bf16[256,1024]{1,0:T(8,128)(2,1)S(1)}, bf16[256,1024]{1,0:T(8,128)(2,1)S(1)}, u32[]{:S(2)}, u32[]{:S(2)}) collective-permute-start(bf16[256,1024]{1,0:T(8,128)(2,1)S(1)} %add_convert_fusion.1), channel_id=1, source_target_pairs={{0,1},{1,2},{2,3},{3,0},{4,5},{5,6},{6,7},{7,4},{8,9},{9,10},{10,1... | collective-permute-start | bytes 1572872 | tf_op jit(solution)/shard_map/ppermute | solution.py:36
  123.9 21.5 %collective-permute-start.21 = (bf16[256,1024]{1,0:T(8,128)(2,1)S(1)}, bf16[256,1024]{1,0:T(8,128)(2,1)S(1)}, u32[]{:S(2)}, u32[]{:S(2)}) collective-permute-start(bf16[256,1024]{1,0:T(8,128)(2,1)S(1)} %add_convert_fusion), channel_id=1, source_target_pairs={{0,3},{1,0},{2,1},{3,2},{4,7},{5,4},{6,5},{7,6},{8,11},{9,8},{10,9... | collective-permute-start | bytes 1572872 | tf_op jit(solution)/shard_map/ppermute | solution.py:40
  147.6 44.8 %all-to-all-start.1 = ((bf16[32,16,2048]{2,1,0:T(8,128)(2,1)}), bf16[32,16,2048]{2,1,0:T(8,128)(2,1)}, u32[]{:S(2)}, u32[]{:S(2)}) async-start(bf16[32,16,2048]{2,1,0:T(8,128)(2,1)} %bitcast.12), calls=%async_computation.1 | async-start | bytes 4194304 | tf_op jit(solution)/shard_map/all_to_all | solution.py:486
  155.1 7.8 %copy-start.2 = (bf16[896,1024]{1,0:T(8,128)(2,1)S(1)}, bf16[896,1024]{1,0:T(8,128)(2,1)}, u32[]{:S(2)}) copy-start(bf16[896,1024]{1,0:T(8,128)(2,1)} %shard_map.122.refs_1_.p1.refs_4_.refs_7_.refs_6_) | copy-start | bytes 5505028
  157.6 16.0 %collective-permute-start.22 = (bf16[256,1024]{1,0:T(8,128)(2,1)S(1)}, bf16[256,1024]{1,0:T(8,128)(2,1)S(1)}, u32[]{:S(2)}, u32[]{:S(2)}) collective-permute-start(bf16[256,1024]{1,0:T(8,128)(2,1)S(1)} %get-tuple-element.44.refs_0_), channel_id=1, source_target_pairs={{0,1},{1,2},{2,3},{3,0},{4,5},{5,6},{6,7},{7,4},{8,9},{9,10},{10,1... | collective-permute-start | bytes 1572872 | tf_op jit(solution)/shard_map/ppermute | solution.py:36
  158.9 14.8 %collective-permute-start.24 = (bf16[256,1024]{1,0:T(8,128)(2,1)S(1)}, bf16[256,1024]{1,0:T(8,128)(2,1)S(1)}, u32[]{:S(2)}, u32[]{:S(2)}) collective-permute-start(bf16[256,1024]{1,0:T(8,128)(2,1)S(1)} %get-tuple-element.45.refs_1_), channel_id=1, source_target_pairs={{0,3},{1,0},{2,1},{3,2},{4,7},{5,4},{6,5},{7,6},{8,11},{9,8},{10,9... | collective-permute-start | bytes 1572872 | tf_op jit(solution)/shard_map/ppermute | solution.py:40
  160.9 24.1 %collective-permute-start.27 = (bf16[256,1024]{1,0:T(8,128)(2,1)S(1)}, bf16[256,1024]{1,0:T(8,128)(2,1)S(1)}, u32[]{:S(2)}, u32[]{:S(2)}) collective-permute-start(bf16[256,1024]{1,0:T(8,128)(2,1)S(1)} %get-tuple-element.44.refs_0_), channel_id=1, source_target_pairs={{0,3},{1,0},{2,1},{3,2},{4,7},{5,4},{6,5},{7,6},{8,11},{9,8},{10,9... | collective-permute-start | bytes 1572872 | tf_op jit(solution)/shard_map/ppermute | solution.py:40
  162.7 22.2 %collective-permute-start.26 = (bf16[256,1024]{1,0:T(8,128)(2,1)S(1)}, bf16[256,1024]{1,0:T(8,128)(2,1)S(1)}, u32[]{:S(2)}, u32[]{:S(2)}) collective-permute-start(bf16[256,1024]{1,0:T(8,128)(2,1)S(1)} %get-tuple-element.45.refs_1_), channel_id=1, source_target_pairs={{0,1},{1,2},{2,3},{3,0},{4,5},{5,6},{6,7},{7,4},{8,9},{9,10},{10,1... | collective-permute-start | bytes 1572872 | tf_op jit(solution)/shard_map/ppermute | solution.py:36
  173.6 25.3 %collective-permute-start.23 = (bf16[256,1024]{1,0:T(8,128)(2,1)S(1)}, bf16[256,1024]{1,0:T(8,128)(2,1)S(1)}, u32[]{:S(2)}, u32[]{:S(2)}) collective-permute-start(bf16[256,1024]{1,0:T(8,128)(2,1)S(1)} %collective-permute-done.22.refs_0_), channel_id=1, source_target_pairs={{0,1},{1,2},{2,3},{3,0},{4,5},{5,6},{6,7},{7,4},{8,9},{9,10},{10,1... | collective-permute-start | bytes 1572872 | tf_op jit(solution)/shard_map/ppermute | solution.py:36
  173.7 25.2 %collective-permute-start.25 = (bf16[256,1024]{1,0:T(8,128)(2,1)S(1)}, bf16[256,1024]{1,0:T(8,128)(2,1)S(1)}, u32[]{:S(2)}, u32[]{:S(2)}) collective-permute-start(bf16[256,1024]{1,0:T(8,128)(2,1)S(1)} %collective-permute-done.24.refs_3_), channel_id=1, source_target_pairs={{0,3},{1,0},{2,1},{3,2},{4,7},{5,4},{6,5},{7,6},{8,11},{9,8},{10,9... | collective-permute-start | bytes 1572872 | tf_op jit(solution)/shard_map/ppermute | solution.py:40
  (18 other events, 21.9 us)

commit v3 on v2

--- a/solution.py
+++ b/solution.py
@@ -270,7 +270,7 @@
     )
 
 
-def send_kernel(code_ref, bias_ref, *refs):
+def send_kernel(code_ref, bias_ref, _, *refs):
     parts, (out_ref, sum_ref) = refs[:6], refs[6:]
     half = parts[0].shape[1]
     for i in range(2):
@@ -282,14 +282,14 @@
     out_ref[...] = jnp.dot(chosen.astype(BF16), sum_ref[...], preferred_element_type=F32).astype(BF16)
 
 
-def rows_to_send(code, bias, parts, slots):
+def rows_to_send(code, bias, token, parts, slots):
     rows, half = parts[0].shape
     return call(
         send_kernel,
         jax.ShapeDtypeStruct((slots, 2 * half), BF16),
-        [VMEM] * 8, VMEM, [pltpu.VMEM((rows, 2 * half), BF16)],
+        [VMEM, VMEM, ANY] + [VMEM] * 6, VMEM, [pltpu.VMEM((rows, 2 * half), BF16)],
         4 << 27, 6 << 20,
-        code.reshape(1, -1), bias.reshape(1, -1), *parts,
+        code.reshape(1, -1), bias.reshape(1, -1), token, *parts,
     )
 
 
@@ -319,25 +319,25 @@
 def place_kernel(at_ref, text_ref, got_ref, out_ref, token_ref):
     token_ref[...] = jnp.zeros_like(token_ref)
     rows, slots = out_ref.shape[0], got_ref.shape[0]
-    named = (lax.broadcasted_iota(jnp.int32, (rows, slots), 0) == at_ref[...]).astype(BF16)
-    added = jnp.dot(named, got_ref[...], preferred_element_type=F32)
+    row = lax.broadcasted_iota(jnp.int32, (rows, slots), 0) + pl.program_id(0) * rows
+    added = jnp.dot((row == at_ref[...]).astype(BF16), got_ref[...], preferred_element_type=F32)
     out_ref[...] = (text_ref[...].astype(F32) + added).astype(BF16)
 
 
 def place_rows(at, text, got):
     (count, width), slots = text.shape, got.shape[0]
-    step = width // 4
+    step = count // 4
     return pl.pallas_call(
         place_kernel,
         grid=(4,),
         out_shape=(jax.ShapeDtypeStruct(text.shape, BF16), TOKEN),
         in_specs=[
             pl.BlockSpec((1, slots), lambda i: (0, 0)),
-            pl.BlockSpec((count, step), lambda i: (0, i)),
-            pl.BlockSpec((slots, step), lambda i: (0, i)),
+            pl.BlockSpec((step, width), lambda i: (i, 0)),
+            pl.BlockSpec((slots, width), lambda i: (0, 0)),
         ],
-        out_specs=(pl.BlockSpec((count, step), lambda i: (0, i)), pl.BlockSpec((8, 128), lambda i: (0, 0))),
-        compiler_params=pltpu.CompilerParams(vmem_limit_bytes=60 << 20),
+        out_specs=(pl.BlockSpec((step, width), lambda i: (i, 0)), pl.BlockSpec((8, 128), lambda i: (0, 0))),
+        compiler_params=pltpu.CompilerParams(vmem_limit_bytes=56 << 20),
         cost_estimate=pl.CostEstimate(flops=16 << 27, bytes_accessed=10 << 20, transcendentals=0),
     )(at, text, got)
 
@@ -418,7 +418,7 @@
         [SMEM] + [VMEM] * (len(grads) + len(extra)) + [ANY] * (8 + len(tokens)), VMEM,
         [pltpu.VMEM((len(steps), depth, width // 2), BF16), pltpu.SemaphoreType.DMA((len(steps),))],
         len(steps) * 7 << 27, len(steps) * 3 << 20,
-        info, *grads, *extra, *pieces, *tokens, limit=60 if slope is not None else 46,
+        info, *grads, *extra, *pieces, *tokens, limit=46,
     )
 
 
@@ -440,7 +440,8 @@
     chosen = jnp.arange(groups * capacity, dtype=jnp.int32)[:, None] == code[None, :]
     send_rows = jnp.sum(jnp.where(chosen, dest_row[None, :] + 1, 0), axis=1) - 1
     swap = functools.partial(lax.all_to_all, axis_name=PLANE, split_axis=0, concat_axis=0, tiled=True)
-    got_rows = swap(send_rows.reshape(groups, capacity)).reshape(1, groups * capacity)
+    named = swap(send_rows.reshape(groups, capacity))
+    got_rows = named.reshape(1, groups * capacity)
 
     rows, cols = w_in.shape
     p1_in = move(parts_of(info, w_in, [(None, rows // 2, 0, cols)])[0], ALONG_Y)
@@ -454,14 +455,14 @@
     relayed, straight = parts_of(
         info, w_out, [(DIRECT, rows - DIRECT, None, cols // 2), (0, DIRECT, 0, cols)]
     )
-    p1_in = after(p1_in, relayed, other_in, other_out, got_rows, xa, xb)
+    p1_in = after(p1_in, relayed, other_in, other_out, named, xa, xb)
     p2_in = move(p1_in, ALONG_X)
     f1_in = move(p1_in, CORE)
     p1 = move(after(relayed, p1_in), ALONG_Y)
     picked, picked_token = pick_rows(got_rows, grad_rows)
     merged, merged_token = merge(info, norm_gain, x, (xa, xb, xc1, xc2))
     total, first_token = first_near(info, merged, (w_in, other_in))
-    p1 = after(p1, first_token, picked_token)
+    p2_in = after(p2_in, first_token, picked_token)
     p2 = move(p1, ALONG_X)
     f1 = move(p1, CORE)
     direct = move(after(straight, p1), ALONG_Y)
@@ -482,19 +483,20 @@
     sa1, sa2 = up(t20), down(t21)
     sb1, sb2 = up(t11), down(t30)
     sc1, sc2 = up(add(t10, sa1)), down(add(t31, sa2))
-    send = rows_to_send(code, b_out, (t00, sb2, sc1, t01, sb1, sc2), groups * capacity)
+    g1, g2 = gradients_home(code, returned, sb1)
+    send = rows_to_send(code, b_out, g1, (t00, sb2, sc1, t01, sb1, sc2), groups * capacity)
     got = swap(send.reshape(groups, capacity, width)).reshape(groups * capacity, width)
 
-    g1, g2 = gradients_home(code, returned, send)
     ga1, ga2 = up(g1), down(g2)
     gb1, gb2 = up(g2), down(g1)
-    gc1, gc2 = up(ga1), down(ga2)
     pieces = (w_out, other_out, p1, f1, p2, f2, direct, crossed)
     total = back(info, ((0, 0), (0, 1)), (g1, g2), None, None, pieces)
-    total = back(info, ((3, 0), (3, 1), (1, 0), (1, 1)), (ga1, gb1, gb2, ga2), total, None, pieces)
+    gc1, gc2 = up(after(ga1, total)), down(after(ga2, total))
+    total = back(info, ((3, 0), (1, 1)), (ga1, ga2), total, None, pieces)
     llm_input, placed = place_rows(got_rows, text_rows, got)
-    grad_hidden = back(info, ((2, 0), (2, 1)), (gc1, gc2), total, slope, pieces, placed)
-
+    grad_hidden = back(
+        info, ((3, 1), (1, 0), (2, 0), (2, 1)), (gb1, gb2, gc1, gc2), total, slope, pieces, placed
+    )
     return (llm_input, grad_hidden)
 
 

time: 207 us -> 193 us (0.932)
  waiting for transfers between devices: 64.3 us -> 38.8 us
  local copies, waits for them, and re-layouts: 19.1 us -> 29.1 us
  starting transfers between devices: 60.3 us -> 57.7 us
  Pallas kernels: 59.5 us -> 61.7 us
    ppermute x8, waiting for transfers between devices: 15.5 us -> 0.31 us  [down(): return lax.ppermute(value, 'tensor', [(z, (z + 3) % 4) for z in range(4)])]
    ppermute x12, waiting for transfers between devices: 19.1 us -> 6.23 us  [move(): return lax.ppermute(value, PLANE, pairs)]
    unnamed x70 -> x98, local copies, waits for them, and re-layouts: 17 us -> 26 us
    ppermute x8, starting transfers between devices: 3.8 us -> 7.38 us  [up(): return lax.ppermute(value, 'tensor', [(z, (z + 1) % 4) for z in range(4)])]
    ppermute x12, starting transfers between devices: 11.9 us -> 9.35 us  [move(): return lax.ppermute(value, PLANE, pairs)]
    ppermute x8, starting transfers between devices: 22.6 us -> 20.2 us  [down(): return lax.ppermute(value, 'tensor', [(z, (z + 3) % 4) for z in range(4)])]
    ppermute x8, waiting for transfers between devices: 27.9 us -> 30.2 us  [up(): return lax.ppermute(value, 'tensor', [(z, (z + 1) % 4) for z in range(4)])]
  transfers between devices with their start and end apart: 31 -> 31, of which waited for: 8 -> 11; matrix products, arithmetic and copies ran while one was open for 2% -> 4% of each run, Pallas kernels for 26% -> 27%
where the time goes in v3:
time: 193 us; the launch traced here: 192 us
  Pallas kernels  61.7 us (32%)
  starting transfers between devices  57.7 us (30%)
  waiting for transfers between devices  38.8 us (20%)
  local copies, waits for them, and re-layouts  29.1 us (15%)
  other arithmetic  3.71 us (2%)
    pallas_call x12, Pallas kernels, call(): pl.pallas_call(kernel, out_shape=out_shape, in_specs=in_specs, out_specs=...  51.3 us
    ppermute x8, waiting for transfers between devices, up(): return lax.ppermute(value, 'tensor', [(z, (z + 1) % 4) for z in range(4)])  30.2 us
    unnamed x98, local copies, waits for them, and re-layouts  26 us
    ppermute x8, starting transfers between devices, down(): return lax.ppermute(value, 'tensor', [(z, (z + 3) % 4) for z in range(4)])  20.2 us
    ppermute x12, starting transfers between devices, move(): return lax.ppermute(value, PLANE, pairs)  9.35 us
    all_to_all x1, starting transfers between devices, body(): swap(send.reshape(groups, capacity, width))  7.44 us
    ppermute x8, starting transfers between devices, up(): return lax.ppermute(value, 'tensor', [(z, (z + 1) % 4) for z in range(4)])  7.38 us
    all_to_all x1, starting transfers between devices, body(): named = swap(send_rows.reshape(groups, capacity))  7.24 us
  transfers between devices with their start and end apart: 31, of which 11 were waited for; matrix products, arithmetic and copies ran while one was open for 4% of the time, Pallas kernels for 27%

profile of v3, /device:TPU:8, one launch (start us, length us, event | category | flops | bytes accessed | tf_op | source)
XLA Modules:
  0.0 192.4 jit_solution(5079538837278205200)
XLA Ops:
  1.3 1.9 %copy-done.6 = bf16[1280,1280]{1,0:T(8,128)(2,1)S(1)} copy-done((bf16[1280,1280]{1,0:T(8,128)(2,1)S(1)}, bf16[1280,1280]{1,0:T(8,128)(2,1)}, u32[]{:S(2)}) %copy-start.6) | copy-done | bytes 3276824
  4.0 1.6 collective-permute-start
  5.6 1.9 collective-permute-start.3
  7.5 2.1 %collective-permute-start.4 = (bf16[320,1024]{1,0:T(8,128)(2,1)}, bf16[320,1024]{1,0:T(8,128)(2,1)S(1)}, u32[]{:S(2)}, u32[]{:S(2)}) collective-permute-start(bf16[320,1024]{1,0:T(8,128)(2,1)} %bitcast.12.own_ref), channel_id=1, source_target_pairs={{0,3},{1,0},{2,1},{3,2},{4,7},{5,4},{6,5},{7,6},{8,11},{9,8},{10,9... | collective-permute-start | bytes 1966088 | tf_op jit(solution)/shard_map/ppermute | solution.py:40
  11.5 7.2 %all-to-all-start = ((s32[32,1,16]{2,1,0:T(1,128)}), s32[32,1,16]{2,1,0:T(1,128)S(1)}, u32[]{:S(2)}, u32[]{:S(2)}) async-start(s32[32,1,16]{2,1,0:T(1,128)} %bitcast.3), calls=%async_computation | async-start | bytes 32768 | tf_op jit(solution)/shard_map/all_to_all | solution.py:443
  18.7 2.5 %shard_map.114 = (bf16[896,1024]{1,0:T(8,128)(2,1)S(1)}, bf16[384,2048]{1,0:T(8,128)(2,1)S(1)}) custom-call(s32[4]{0:T(128)S(1)} %pad_add_fusion.info_ref, bf16[1280,2048]{1,0:T(8,128)(2,1)} %refs_6_.1), custom_call_target="tpu_custom_call" | custom-call | bytes 5242880 | tf_op jit(solution)/shard_map/pallas_call | solution.py:54
  23.8 1.7 all-to-all-done
  26.5 1.6 collective-permute-start.10
  28.1 1.6 collective-permute-start.5
  30.4 1.9 collective-permute-start.7
  33.1 2.1 %collective-permute-start.8 = (bf16[160,1024]{1,0:T(8,128)(2,1)}, bf16[160,1024]{1,0:T(8,128)(2,1)}, u32[]{:S(2)}, u32[]{:S(2)}) collective-permute-start(bf16[160,1024]{1,0:T(8,128)(2,1)} %slice.18), channel_id=1, source_target_pairs={{0,3},{1,0},{2,1},{3,2},{4,7},{5,4},{6,5},{7,6},{8,11},{9,8},{10,9... | collective-permute-start | bytes 983048 | tf_op jit(solution)/shard_map/ppermute | solution.py:40
  36.6 2.2 %copy-done.37 = bf16[1024,2048]{1,0:T(8,128)(2,1)S(1)} copy-done((bf16[1024,2048]{1,0:T(8,128)(2,1)S(1)}, bf16[1024,2048]{1,0:T(8,128)(2,1)}, u32[]{:S(2)}) %copy-start.37) | copy-done | bytes 4194328
  38.8 3.5 %shard_map.113 = (bf16[512,2048]{1,0:T(8,128)(2,1)S(1)}, f32[8,128]{1,0:T(8,128)S(1)}) custom-call(s32[1,512]{1,0:T(1,128)S(1)} %reshape.92.at_ref, bf16[1024,2048]{1,0:T(8,128)(2,1)S(1)} %copy-done.37), custom_call_target="tpu_custom_call" | custom-call | flops 2147483648 | bytes 6291456 | tf_op jit(solution)/shard_map/pallas_call | solution.py:308
  43.6 3.5 %shard_map.118 = (bf16[256,5120]{1,0:T(8,128)(2,1)S(1)}, f32[8,128]{1,0:T(8,128)}) custom-call(s32[4]{0:T(128)S(1)} %pad_add_fusion.info_ref, f32[1,1280]{1,0:T(1,128)S(1)} %reshape.94.gain_ref, bf16[320,1024]{1,0:T(8,128)(2,1)} %bitcast.12.own_ref, bf16[320,1024]{1,0:T(8,128)(2,1)S(1)} %copy-done.20, bf16[320,1024]{1,0:T(8,128)(2,1)S(1)} %copy-done.22, ...), custom_call_target="tpu_custom_call" | custom-call | flops 1073741824 | bytes 6291456 | tf_op jit(solution)/shard_map/pallas_call | solution.py:54
  47.2 3.8 %shard_map.119 = (f32[256,1280]{1,0:T(8,128)S(1)}, f32[8,128]{1,0:T(8,128)S(1)}) custom-call(s32[4]{0:T(128)S(1)} %pad_add_fusion.info_ref, bf16[256,5120]{1,0:T(8,128)(2,1)S(1)} %get-tuple-element.27.x_ref, bf16[1280,1280]{1,0:T(8,128)(2,1)S(1)} %copy-done.7, bf16[1280,1280]{1,0:T(8,128)(2,1)} %collective-permute-done.1.refs_2_.other_ref), custom_call_target="tpu_custom_call" | custom-call | flops 2281701376 | bytes 9437184 | tf_op jit(solution)/shard_map/pallas_call | solution.py:54
  52.6 1.4 collective-permute-start.9
  55.8 1.5 collective-permute-start.12
  57.5 2.3 %collective-permute-done.11.f2 = bf16[640,1280]{1,0:T(8,128)(2,1)} collective-permute-done((bf16[640,1280]{1,0:T(8,128)(2,1)}, bf16[640,1280]{1,0:T(8,128)(2,1)}, u32[]{:S(2)}, u32[]{:S(2)}) %collective-permute-start.11) | collective-permute-done | bytes 1638432 | tf_op jit(solution)/shard_map/ppermute | solution.py:32
  59.8 1.4 copy-done.13
  61.3 1.3 copy-done.26
  62.6 6.6 %shard_map.121 = (bf16[256,1280]{1,0:T(8,128)(2,1)S(1)}, f32[256,1280]{1,0:T(8,128)S(1)}) custom-call(s32[4]{0:T(128)S(1)} %pad_add_fusion.info_ref, bf16[256,5120]{1,0:T(8,128)(2,1)} %copy-done.8, f32[1,1280]{1,0:T(1,128)S(1)} %reshape.95.b_ref, f32[256,1280]{1,0:T(8,128)S(1)} %copy-done.26, bf16[640,1280]{1,0:T(8,128)(2,1)} %shard_map.116.refs_1_.p1, ...), custom_call_target="tpu_custom_call" | custom-call | flops 2281701376 | bytes 12582912 | tf_op jit(solution)/shard_map/pallas_call | solution.py:54
  69.2 5.1 %shard_map.122 = (bf16[2,256,2048]{2,1,0:T(8,128)(2,1)S(1)}, f32[8,128]{1,0:T(8,128)S(1)}) custom-call(s32[4]{0:T(128)S(1)} %pad_add_fusion.info_ref, bf16[256,1280]{1,0:T(8,128)(2,1)S(1)} %get-tuple-element.31.h_ref, bf16[1280,2048]{1,0:T(8,128)(2,1)S(1)} %bitcast.33, bf16[1280,2048]{1,0:T(8,128)(2,1)} %collective-permute-done.2.refs_3_.other_ref.refs_4_.refs_7_), custom_call_target="tpu_custom_call" | custom-call | flops 3623878656 | bytes 13631488 | tf_op jit(solution)/shard_map/pallas_call | solution.py:54
  75.0 1.3 copy-done.40
  76.3 3.6 %collective-permute-done.6.refs_0_ = bf16[896,1024]{1,0:T(8,128)(2,1)} collective-permute-done((bf16[896,1024]{1,0:T(8,128)(2,1)}, bf16[896,1024]{1,0:T(8,128)(2,1)}, u32[]{:S(2)}, u32[]{:S(2)}) %collective-permute-start.6) | collective-permute-done | bytes 1835040 | tf_op jit(solution)/shard_map/ppermute | solution.py:32
  81.6 6.1 %all-to-all-start.1 = ((bf16[32,16,2048]{2,1,0:T(8,128)(2,1)}), bf16[32,16,2048]{2,1,0:T(8,128)(2,1)}, u32[]{:S(2)}, u32[]{:S(2)}) async-start(bf16[32,16,2048]{2,1,0:T(8,128)(2,1)} %bitcast.35), calls=%async_computation.1 | async-start | bytes 4194304 | tf_op jit(solution)/shard_map/all_to_all | solution.py:478
  87.8 1.6 copy-done.39
  89.3 6.7 %shard_map.127 = (bf16[256,1024]{1,0:T(8,128)(2,1)S(1)}, bf16[256,1024]{1,0:T(8,128)(2,1)S(1)}, bf16[256,1024]{1,0:T(8,128)(2,1)S(1)}, bf16[256,1024]{1,0:T(8,12...) custom-call(s32[4]{0:T(128)S(1)} %pad_add_fusion.info_ref, ...), custom_call_target="tpu_custom_call" | custom-call | flops 3623878656 | bytes 17825792 | tf_op jit(solution)/shard_map/pallas_call | solution.py:54
  97.6 2.5 %collective-permute-start.20 = (bf16[256,1024]{1,0:T(8,128)(2,1)S(1)}, bf16[256,1024]{1,0:T(8,128)(2,1)S(1)}, u32[]{:S(2)}, u32[]{:S(2)}) collective-permute-start(bf16[256,1024]{1,0:T(8,128)(2,1)S(1)} %get-tuple-element.43), channel_id=1, source_target_pairs={{0,3},{1,0},{2,1},{3,2},{4,7},{5,4},{6,5},{7,6},{8,11},{9,8},{10,9... | collective-permute-start | bytes 1572872 | tf_op jit(solution)/shard_map/ppermute | solution.py:40
  100.1 3.2 %collective-permute-start.17 = (bf16[256,1024]{1,0:T(8,128)(2,1)}, bf16[256,1024]{1,0:T(8,128)(2,1)}, u32[]{:S(2)}, u32[]{:S(2)}) collective-permute-start(bf16[256,1024]{1,0:T(8,128)(2,1)} %get-tuple-element.38), channel_id=1, source_target_pairs={{0,3},{1,0},{2,1},{3,2},{4,7},{5,4},{6,5},{7,6},{8,11},{9,8},{10,9... | collective-permute-start | bytes 1572872 | tf_op jit(solution)/shard_map/ppermute | solution.py:40
  103.3 9.5 %collective-permute-done.18 = bf16[256,1024]{1,0:T(8,128)(2,1)S(1)} collective-permute-done((bf16[256,1024]{1,0:T(8,128)(2,1)S(1)}, bf16[256,1024]{1,0:T(8,128)(2,1)S(1)}, u32[]{:S(2)}, u32[]{:S(2)}) %collective-permute-start.18) | collective-permute-done | bytes 524320 | tf_op jit(solution)/shard_map/ppermute | solution.py:36
  114.8 3.2 %collective-permute-start.21 = (bf16[256,1024]{1,0:T(8,128)(2,1)}, bf16[256,1024]{1,0:T(8,128)(2,1)}, u32[]{:S(2)}, u32[]{:S(2)}) collective-permute-start(bf16[256,1024]{1,0:T(8,128)(2,1)} %add_convert_fusion), channel_id=1, source_target_pairs={{0,3},{1,0},{2,1},{3,2},{4,7},{5,4},{6,5},{7,6},{8,11},{9,8},{10,9... | collective-permute-start | bytes 1572872 | tf_op jit(solution)/shard_map/ppermute | solution.py:40
  118.1 6.0 %collective-permute-done.16._.refs_4_ = bf16[256,1024]{1,0:T(8,128)(2,1)S(1)} collective-permute-done((bf16[256,1024]{1,0:T(8,128)(2,1)}, bf16[256,1024]{1,0:T(8,128)(2,1)S(1)}, u32[]{:S(2)}, u32[]{:S(2)}) %collective-permute-start.16) | collective-permute-done | bytes 524320 | tf_op jit(solution)/shard_map/ppermute | solution.py:36
  124.0 3.1 %shard_map.128 = (bf16[256,1024]{1,0:T(8,128)(2,1)S(1)}, bf16[256,1024]{1,0:T(8,128)(2,1)}) custom-call(s32[1,256]{1,0:T(1,128)S(1)} %bitcast_add_fusion.code_ref, bf16[512,2048]{1,0:T(8,128)(2,1)} %bitcast.14.rows_ref, bf16[256,1024]{1,0:T(8,128)(2,1)S(1)} %collective-permute-done.16._.refs_4_), custom_call_target="tpu_custom_call" | custom-call | flops 536870912 | bytes 3145728 | tf_op jit(solution)/shard_map/pallas_call | solution.py:54
  127.2 7.4 %collective-permute-done.19.refs_2_ = bf16[256,1024]{1,0:T(8,128)(2,1)} collective-permute-done((bf16[256,1024]{1,0:T(8,128)(2,1)}, bf16[256,1024]{1,0:T(8,128)(2,1)}, u32[]{:S(2)}, u32[]{:S(2)}) %collective-permute-start.19) | collective-permute-done | bytes 524320 | tf_op jit(solution)/shard_map/ppermute | solution.py:36
  134.6 2.2 %shard_map.129 = bf16[512,2048]{1,0:T(8,128)(2,1)S(1)} custom-call(s32[1,256]{1,0:T(1,128)S(1)} %bitcast_add_fusion.code_ref, f32[1,2048]{1,0:T(1,128)S(1)} %bitcast.36, bf16[256,1024]{1,0:T(8,128)(2,1)S(1)} %get-tuple-element.36._.refs_0_, bf16[256,1024]{1,0:T(8,128)(2,1)S(1)} %copy-done.28, bf16[256,1024]{1,0:T(8,128)(2,1)} %collective-permute-done.17.refs_1_, ...), custom_call_target="tpu_custom_call" | custom-call | flops 536870912 | bytes 6291456 | tf_op jit(solution)/shard_map/pallas_call | solution.py:54
  138.1 7.4 %all-to-all-start.2 = ((bf16[32,16,2048]{2,1,0:T(8,128)(2,1)}), bf16[32,16,2048]{2,1,0:T(8,128)(2,1)}, u32[]{:S(2)}, u32[]{:S(2)}) async-start(bf16[32,16,2048]{2,1,0:T(8,128)(2,1)} %bitcast.34), calls=%async_computation.2 | async-start | bytes 4194304 | tf_op jit(solution)/shard_map/all_to_all | solution.py:488
  145.6 1.3 collective-permute-start.24
  146.9 2.0 %collective-permute-start.26 = (bf16[256,1024]{1,0:T(8,128)(2,1)}, bf16[256,1024]{1,0:T(8,128)(2,1)S(1)}, u32[]{:S(2)}, u32[]{:S(2)}) collective-permute-start(bf16[256,1024]{1,0:T(8,128)(2,1)} %get-tuple-element.45.refs_1_), channel_id=1, source_target_pairs={{0,3},{1,0},{2,1},{3,2},{4,7},{5,4},{6,5},{7,6},{8,11},{9,8},{10,9... | collective-permute-start | bytes 1572872 | tf_op jit(solution)/shard_map/ppermute | solution.py:40
  148.9 3.2 %collective-permute-start.23 = (bf16[256,1024]{1,0:T(8,128)(2,1)S(1)}, bf16[256,1024]{1,0:T(8,128)(2,1)}, u32[]{:S(2)}, u32[]{:S(2)}) collective-permute-start(bf16[256,1024]{1,0:T(8,128)(2,1)S(1)} %get-tuple-element.36._.refs_0_), channel_id=1, source_target_pairs={{0,3},{1,0},{2,1},{3,2},{4,7},{5,4},{6,5},{7,6},{8,11},{9,8},{10,9... | collective-permute-start | bytes 1572872 | tf_op jit(solution)/shard_map/ppermute | solution.py:40
  152.1 1.4 copy-done.4
  153.5 4.8 %shard_map.131.refs_1_.refs_2_ = f32[256,1280]{1,0:T(8,128)S(1)} custom-call(s32[4]{0:T(128)S(1)} %pad_add_fusion.info_ref, bf16[256,1024]{1,0:T(8,128)(2,1)S(1)} %get-tuple-element.36._.refs_0_, bf16[256,1024]{1,0:T(8,128)(2,1)} %get-tuple-element.45.refs_1_, bf16[1280,2048]{1,0:T(8,128)(2,1)} %refs_6_.1, ...), custom_call_target="tpu_custom_call" | custom-call | flops 1879048192 | bytes 6291456 | tf_op jit(solution)/shard_map/pallas_call | solution.py:54
  158.3 3.3 %collective-permute-done.24.refs_0_ = bf16[256,1024]{1,0:T(8,128)(2,1)S(1)} collective-permute-done((bf16[256,1024]{1,0:T(8,128)(2,1)S(1)}, bf16[256,1024]{1,0:T(8,128)(2,1)S(1)}, u32[]{:S(2)}, u32[]{:S(2)}) %collective-permute-start.24) | collective-permute-done | bytes 524320 | tf_op jit(solution)/shard_map/ppermute | solution.py:36
  161.9 4.2 %shard_map.134.refs_4_ = f32[256,1280]{1,0:T(8,128)S(1)} custom-call(s32[4]{0:T(128)S(1)} %pad_add_fusion.info_ref, bf16[256,1024]{1,0:T(8,128)(2,1)S(1)} %collective-permute-done.24.refs_0_, bf16[256,1024]{1,0:T(8,128)(2,1)S(1)} %collective-permute-done.26.refs_0_.refs_1_, f32[256,1280]{1,0:T(8,128)S(1)} %shard_map.131.refs_1_.refs_2_, ...), custom_call_target="tpu_custom_call" | custom-call | flops 1879048192 | bytes 6291456 | tf_op jit(solution)/shard_map/pallas_call | solution.py:54
  168.8 1.5 collective-permute-start.25
  170.3 1.8 collective-permute-start.27
  172.5 6.9 %shard_map.130 = (bf16[1024,2048]{1,0:T(8,128)(2,1)}, f32[8,128]{1,0:T(8,128)}) custom-call(s32[1,512]{1,0:T(1,128)} %copy-done.36, bf16[1024,2048]{1,0:T(8,128)(2,1)} %text_ref.1, bf16[512,2048]{1,0:T(8,128)(2,1)} %bitcast.16.got_ref), custom_call_target="tpu_custom_call" | custom-call | flops 2147483648 | bytes 10485760 | tf_op jit(solution)/shard_map/pallas_call | solution.py:330
  179.4 4.0 %collective-permute-done.25.refs_2_ = bf16[256,1024]{1,0:T(8,128)(2,1)} collective-permute-done((bf16[256,1024]{1,0:T(8,128)(2,1)}, bf16[256,1024]{1,0:T(8,128)(2,1)}, u32[]{:S(2)}, u32[]{:S(2)}) %collective-permute-start.25) | collective-permute-done | bytes 524320 | tf_op jit(solution)/shard_map/ppermute | solution.py:36
  184.1 8.1 %shard_map.135 = bf16[256,1280]{1,0:T(8,128)(2,1)} custom-call(s32[4]{0:T(128)S(1)} %pad_add_fusion.info_ref, bf16[256,1024]{1,0:T(8,128)(2,1)} %collective-permute-done.22.refs_0_, bf16[256,1024]{1,0:T(8,128)(2,1)} %collective-permute-done.23.refs_1_, bf16[256,1024]{1,0:T(8,128)(2,1)} %collective-permute-done.25.refs_2_, ...), custom_call_target="tpu_custom_call" | custom-call | flops 3758096384 | bytes 12582912 | tf_op jit(solution)/shard_map/pallas_call | solution.py:54
  (157 shorter events, 25.9 us)
Async XLA Ops:
  0.6 24.9 %collective-permute-start.2 = (bf16[1280,2048]{1,0:T(8,128)(2,1)}, bf16[1280,2048]{1,0:T(8,128)(2,1)}, u32[]{:S(2)}, u32[]{:S(2)}) collective-permute-start(bf16[1280,2048]{1,0:T(8,128)(2,1)} %refs_6_.1), channel_id=1, source_target_pairs={{0,4},{4,0},{8,12},{12,8},{16,20},{20,16},{24,28},{28,24},{32,36},... | collective-permute-start | bytes 15728648 | tf_op jit(solution)/shard_map/ppermute | solution.py:32
  0.7 24.8 %collective-permute-start.1 = (bf16[1280,1280]{1,0:T(8,128)(2,1)}, bf16[1280,1280]{1,0:T(8,128)(2,1)}, u32[]{:S(2)}, u32[]{:S(2)}) collective-permute-start(bf16[1280,1280]{1,0:T(8,128)(2,1)} %own_ref.6), channel_id=1, source_target_pairs={{0,4},{4,0},{8,12},{12,8},{16,20},{20,16},{24,28},{28,24},{32,36},... | collective-permute-start | bytes 9830408 | tf_op jit(solution)/shard_map/ppermute | solution.py:32
  3.2 6.4 %copy-start.43 = (s32[256,1]{0,1:T(1,128)S(1)}, s32[256,1]{0,1:T(1,128)}, u32[]{:S(2)}) copy-start(s32[256,1]{0,1:T(1,128)} %param.17) | copy-start | bytes 3076
  3.2 7.4 %copy-start.46 = (s32[256]{0:T(256)S(1)}, s32[256]{0:T(256)}, u32[]{:S(2)}) copy-start(s32[256]{0:T(256)} %param.18) | copy-start | bytes 3076
  4.0 21.5 %collective-permute-start = (bf16[640,1280]{1,0:T(8,128)(2,1)S(1)}, bf16[640,1280]{1,0:T(8,128)(2,1)}, u32[]{:S(2)}, u32[]{:S(2)}) collective-permute-start(bf16[640,1280]{1,0:T(8,128)(2,1)S(1)} %shard_map.115), channel_id=1, source_target_pairs={{0,8},{4,28},{8,16},{12,4},{16,24},{20,12},{24,0},{28,20},{32,40},... | collective-permute-start | bytes 4915208 | tf_op jit(solution)/shard_map/ppermute | solution.py:32
  5.6 19.8 %collective-permute-start.3 = (bf16[320,1024]{1,0:T(8,128)(2,1)}, bf16[320,1024]{1,0:T(8,128)(2,1)S(1)}, u32[]{:S(2)}, u32[]{:S(2)}) collective-permute-start(bf16[320,1024]{1,0:T(8,128)(2,1)} %bitcast.12.own_ref), channel_id=1, source_target_pairs={{0,1},{1,2},{2,3},{3,0},{4,5},{5,6},{6,7},{7,4},{8,9},{9,10},{10,1... | collective-permute-start | bytes 1966088 | tf_op jit(solution)/shard_map/ppermute | solution.py:36
  7.5 17.9 %collective-permute-start.4 = (bf16[320,1024]{1,0:T(8,128)(2,1)}, bf16[320,1024]{1,0:T(8,128)(2,1)S(1)}, u32[]{:S(2)}, u32[]{:S(2)}) collective-permute-start(bf16[320,1024]{1,0:T(8,128)(2,1)} %bitcast.12.own_ref), channel_id=1, source_target_pairs={{0,3},{1,0},{2,1},{3,2},{4,7},{5,4},{6,5},{7,6},{8,11},{9,8},{10,9... | collective-permute-start | bytes 1966088 | tf_op jit(solution)/shard_map/ppermute | solution.py:40
  11.5 14.0 %all-to-all-start = ((s32[32,1,16]{2,1,0:T(1,128)}), s32[32,1,16]{2,1,0:T(1,128)S(1)}, u32[]{:S(2)}, u32[]{:S(2)}) async-start(s32[32,1,16]{2,1,0:T(1,128)} %bitcast.3), calls=%async_computation | async-start | bytes 32768 | tf_op jit(solution)/shard_map/all_to_all | solution.py:443
  26.5 5.8 %copy-start.22 = (bf16[320,1024]{1,0:T(8,128)(2,1)S(1)}, bf16[320,1024]{1,0:T(8,128)(2,1)}, u32[]{:S(2)}) copy-start(bf16[320,1024]{1,0:T(8,128)(2,1)} %copy-done.21) | copy-start | bytes 1966084
  26.5 8.7 %copy-start.44 = (f32[1280]{0:T(1024)S(1)}, f32[1280]{0:T(1024)}, u32[]{:S(2)}) copy-start(f32[1280]{0:T(1024)} %param.11) | copy-start | bytes 15364
  26.5 9.3 %copy-start.42 = (s32[32,1,16]{2,1,0:T(1,128)S(1)}, s32[32,1,16]{2,1,0:T(1,128)}, u32[]{:S(2)}) copy-start(s32[32,1,16]{2,1,0:T(1,128)} %copy-done.41) | copy-start | bytes 6148
  26.5 27.5 %collective-permute-start.10 = (bf16[640,1280]{1,0:T(8,128)(2,1)}, bf16[640,1280]{1,0:T(8,128)(2,1)S(1)}, u32[]{:S(2)}, u32[]{:S(2)}) collective-permute-start(bf16[640,1280]{1,0:T(8,128)(2,1)} %shard_map.116.refs_1_.p1), channel_id=1, source_target_pairs={{0,32},{4,100},{8,40},{12,108},{16,48},{20,116},{24,56},{28,124},{... | collective-permute-start | bytes 4915208 | tf_op jit(solution)/shard_map/ppermute | solution.py:32
  28.1 27.1 %collective-permute-start.5 = (bf16[896,1024]{1,0:T(8,128)(2,1)}, bf16[896,1024]{1,0:T(8,128)(2,1)}, u32[]{:S(2)}, u32[]{:S(2)}) collective-permute-start(bf16[896,1024]{1,0:T(8,128)(2,1)} %shard_map.117), channel_id=1, source_target_pairs={{0,8},{4,28},{8,16},{12,4},{16,24},{20,12},{24,0},{28,20},{32,40},... | collective-permute-start | bytes 5505032 | tf_op jit(solution)/shard_map/ppermute | solution.py:32
  30.4 11.9 %collective-permute-start.7 = (bf16[160,1024]{1,0:T(8,128)(2,1)}, bf16[160,1024]{1,0:T(8,128)(2,1)S(1)}, u32[]{:S(2)}, u32[]{:S(2)}) collective-permute-start(bf16[160,1024]{1,0:T(8,128)(2,1)} %slice.17), channel_id=1, source_target_pairs={{0,1},{1,2},{2,3},{3,0},{4,5},{5,6},{6,7},{7,4},{8,9},{9,10},{10,1... | collective-permute-start | bytes 983048 | tf_op jit(solution)/shard_map/ppermute | solution.py:36
  33.1 10.5 %collective-permute-start.8 = (bf16[160,1024]{1,0:T(8,128)(2,1)}, bf16[160,1024]{1,0:T(8,128)(2,1)}, u32[]{:S(2)}, u32[]{:S(2)}) collective-permute-start(bf16[160,1024]{1,0:T(8,128)(2,1)} %slice.18), channel_id=1, source_target_pairs={{0,3},{1,0},{2,1},{3,2},{4,7},{5,4},{6,5},{7,6},{8,11},{9,8},{10,9... | collective-permute-start | bytes 983048 | tf_op jit(solution)/shard_map/ppermute | solution.py:40
  52.6 4.9 %collective-permute-start.9 = (bf16[640,1280]{1,0:T(8,128)(2,1)}, bf16[640,1280]{1,0:T(8,128)(2,1)}, u32[]{:S(2)}, u32[]{:S(2)}) collective-permute-start(bf16[640,1280]{1,0:T(8,128)(2,1)} %shard_map.116.refs_1_.p1), channel_id=1, source_target_pairs={{0,4},{4,0},{8,12},{12,8},{16,20},{20,16},{24,28},{28,24},{32,36},... | collective-permute-start | bytes 4915208 | tf_op jit(solution)/shard_map/ppermute | solution.py:32
  55.2 4.6 %collective-permute-start.11 = (bf16[640,1280]{1,0:T(8,128)(2,1)}, bf16[640,1280]{1,0:T(8,128)(2,1)}, u32[]{:S(2)}, u32[]{:S(2)}) collective-permute-start(bf16[640,1280]{1,0:T(8,128)(2,1)} %shard_map.120.p2), channel_id=1, source_target_pairs={{0,4},{4,0},{8,12},{12,8},{16,20},{20,16},{24,28},{28,24},{32,36},... | collective-permute-start | bytes 4915208 | tf_op jit(solution)/shard_map/ppermute | solution.py:32
  55.2 24.8 %collective-permute-start.6 = (bf16[896,1024]{1,0:T(8,128)(2,1)}, bf16[896,1024]{1,0:T(8,128)(2,1)}, u32[]{:S(2)}, u32[]{:S(2)}) collective-permute-start(bf16[896,1024]{1,0:T(8,128)(2,1)} %collective-permute-done.5.refs_1_.p1.refs_4_.refs_5_.refs_8_), channel_id=1, source_target_pairs={{0,32},{4,100},{8,40},{12,108},{16,48},{20,116},{24,56},{28,124},{... | collective-permute-start | bytes 5505032 | tf_op jit(solution)/shard_map/ppermute | solution.py:32
  55.7 13.5 %slice-start = ((s8[5242880]{0:T(1024)(128)(4,1)}), s8[1048576]{0:T(1024)(128)(4,1)S(1)}, s32[]{:S(2)}) async-start(s8[5242880]{0:T(1024)(128)(4,1)} %bitcast.32), calls=%async_computation.3 | async-start | bytes 2097152
  55.8 24.2 %collective-permute-start.12 = (bf16[384,2048]{1,0:T(8,128)(2,1)}, bf16[384,2048]{1,0:T(8,128)(2,1)S(1)}, u32[]{:S(2)}, u32[]{:S(2)}) collective-permute-start(bf16[384,2048]{1,0:T(8,128)(2,1)} %shard_map.124), channel_id=1, source_target_pairs={{0,8},{4,28},{8,16},{12,4},{16,24},{20,12},{24,0},{28,20},{32,40},... | collective-permute-start | bytes 4718600 | tf_op jit(solution)/shard_map/ppermute | solution.py:32
  57.3 30.5 %collective-permute-start.13 = (bf16[896,1024]{1,0:T(8,128)(2,1)}, bf16[896,1024]{1,0:T(8,128)(2,1)}, u32[]{:S(2)}, u32[]{:S(2)}) collective-permute-start(bf16[896,1024]{1,0:T(8,128)(2,1)} %collective-permute-done.5.refs_1_.p1.refs_4_.refs_5_.refs_8_), channel_id=1, source_target_pairs={{0,4},{4,0},{8,12},{12,8},{16,20},{20,16},{24,28},{28,24},{32,36},... | collective-permute-start | bytes 5505032 | tf_op jit(solution)/shard_map/ppermute | solution.py:32
  62.6 6.6 %slice-start.1 = ((s8[5242880]{0:T(1024)(128)(4,1)}), s8[4194304]{0:T(1024)(128)(4,1)S(1)}, s32[]{:S(2)}) async-start(s8[5242880]{0:T(1024)(128)(4,1)} %bitcast.32), calls=%async_computation.4 | async-start | bytes 8388608
  79.9 7.8 %collective-permute-start.14 = (bf16[896,1024]{1,0:T(8,128)(2,1)}, bf16[896,1024]{1,0:T(8,128)(2,1)}, u32[]{:S(2)}, u32[]{:S(2)}) collective-permute-start(bf16[896,1024]{1,0:T(8,128)(2,1)} %shard_map.123.refs_1_.p2.refs_6_.refs_7_.refs_10_), channel_id=1, source_target_pairs={{0,4},{4,0},{8,12},{12,8},{16,20},{20,16},{24,28},{28,24},{32,36},... | collective-permute-start | bytes 5505032 | tf_op jit(solution)/shard_map/ppermute | solution.py:32
  81.1 6.6 %collective-permute-start.15 = (bf16[384,2048]{1,0:T(8,128)(2,1)}, bf16[384,2048]{1,0:T(8,128)(2,1)S(1)}, u32[]{:S(2)}, u32[]{:S(2)}) collective-permute-start(bf16[384,2048]{1,0:T(8,128)(2,1)} %shard_map.125.refs_2_.direct.refs_8_.refs_9_.refs_12_), channel_id=1, source_target_pairs={{0,4},{4,0},{8,12},{12,8},{16,20},{20,16},{24,28},{28,24},{32,36},... | collective-permute-start | bytes 4718600 | tf_op jit(solution)/shard_map/ppermute | solution.py:32
  81.6 6.1 %copy-start.1 = (bf16[384,2048]{1,0:T(8,128)(2,1)S(1)}, bf16[384,2048]{1,0:T(8,128)(2,1)}, u32[]{:S(2)}) copy-start(bf16[384,2048]{1,0:T(8,128)(2,1)} %shard_map.125.refs_2_.direct.refs_8_.refs_9_.refs_12_) | copy-start | bytes 4718596
  81.6 36.4 %all-to-all-start.1 = ((bf16[32,16,2048]{2,1,0:T(8,128)(2,1)}), bf16[32,16,2048]{2,1,0:T(8,128)(2,1)}, u32[]{:S(2)}, u32[]{:S(2)}) async-start(bf16[32,16,2048]{2,1,0:T(8,128)(2,1)} %bitcast.35), calls=%async_computation.1 | async-start | bytes 4194304 | tf_op jit(solution)/shard_map/all_to_all | solution.py:478
  87.7 8.3 %copy-start.3 = (bf16[384,2048]{1,0:T(8,128)(2,1)}, bf16[384,2048]{1,0:T(8,128)(2,1)S(1)}, u32[]{:S(2)}) copy-start(bf16[384,2048]{1,0:T(8,128)(2,1)S(1)} %collective-permute-done.15.crossed.refs_9_.refs_10_.refs_13_) | copy-start | bytes 4718596
  96.8 17.0 %copy-start.29 = (bf16[256,1024]{1,0:T(8,128)(2,1)}, bf16[256,1024]{1,0:T(8,128)(2,1)S(1)}, u32[]{:S(2)}) copy-start(bf16[256,1024]{1,0:T(8,128)(2,1)S(1)} %get-tuple-element.41.refs_3_) | copy-start | bytes 1572868
  96.8 16.0 %collective-permute-start.18 = (bf16[256,1024]{1,0:T(8,128)(2,1)S(1)}, bf16[256,1024]{1,0:T(8,128)(2,1)S(1)}, u32[]{:S(2)}, u32[]{:S(2)}) collective-permute-start(bf16[256,1024]{1,0:T(8,128)(2,1)S(1)} %get-tuple-element.40), channel_id=1, source_target_pairs={{0,1},{1,2},{2,3},{3,0},{4,5},{5,6},{6,7},{7,4},{8,9},{9,10},{10,1... | collective-permute-start | bytes 1572872 | tf_op jit(solution)/shard_map/ppermute | solution.py:36
  97.6 16.3 %collective-permute-start.20 = (bf16[256,1024]{1,0:T(8,128)(2,1)S(1)}, bf16[256,1024]{1,0:T(8,128)(2,1)S(1)}, u32[]{:S(2)}, u32[]{:S(2)}) collective-permute-start(bf16[256,1024]{1,0:T(8,128)(2,1)S(1)} %get-tuple-element.43), channel_id=1, source_target_pairs={{0,3},{1,0},{2,1},{3,2},{4,7},{5,4},{6,5},{7,6},{8,11},{9,8},{10,9... | collective-permute-start | bytes 1572872 | tf_op jit(solution)/shard_map/ppermute | solution.py:40
  100.1 24.0 %collective-permute-start.16 = (bf16[256,1024]{1,0:T(8,128)(2,1)}, bf16[256,1024]{1,0:T(8,128)(2,1)S(1)}, u32[]{:S(2)}, u32[]{:S(2)}) collective-permute-start(bf16[256,1024]{1,0:T(8,128)(2,1)} %get-tuple-element.35), channel_id=1, source_target_pairs={{0,1},{1,2},{2,3},{3,0},{4,5},{5,6},{6,7},{7,4},{8,9},{9,10},{10,1... | collective-permute-start | bytes 1572872 | tf_op jit(solution)/shard_map/ppermute | solution.py:36
  100.1 27.1 %collective-permute-start.17 = (bf16[256,1024]{1,0:T(8,128)(2,1)}, bf16[256,1024]{1,0:T(8,128)(2,1)}, u32[]{:S(2)}, u32[]{:S(2)}) collective-permute-start(bf16[256,1024]{1,0:T(8,128)(2,1)} %get-tuple-element.38), channel_id=1, source_target_pairs={{0,3},{1,0},{2,1},{3,2},{4,7},{5,4},{6,5},{7,6},{8,11},{9,8},{10,9... | collective-permute-start | bytes 1572872 | tf_op jit(solution)/shard_map/ppermute | solution.py:40
  113.8 20.8 %collective-permute-start.19 = (bf16[256,1024]{1,0:T(8,128)(2,1)}, bf16[256,1024]{1,0:T(8,128)(2,1)}, u32[]{:S(2)}, u32[]{:S(2)}) collective-permute-start(bf16[256,1024]{1,0:T(8,128)(2,1)} %add_convert_fusion.1), channel_id=1, source_target_pairs={{0,1},{1,2},{2,3},{3,0},{4,5},{5,6},{6,7},{7,4},{8,9},{9,10},{10,1... | collective-permute-start | bytes 1572872 | tf_op jit(solution)/shard_map/ppermute | solution.py:36
  113.8 20.8 %copy-start.28 = (bf16[256,1024]{1,0:T(8,128)(2,1)S(1)}, bf16[256,1024]{1,0:T(8,128)(2,1)}, u32[]{:S(2)}) copy-start(bf16[256,1024]{1,0:T(8,128)(2,1)} %copy-done.27) | copy-start | bytes 1572868
  113.8 20.8 %copy-start.32 = (f32[2048]{0:T(1024)S(1)}, f32[2048]{0:T(1024)}, u32[]{:S(2)}) copy-start(f32[2048]{0:T(1024)} %param.15) | copy-start | bytes 24580
  114.8 19.7 %collective-permute-start.21 = (bf16[256,1024]{1,0:T(8,128)(2,1)}, bf16[256,1024]{1,0:T(8,128)(2,1)}, u32[]{:S(2)}, u32[]{:S(2)}) collective-permute-start(bf16[256,1024]{1,0:T(8,128)(2,1)} %add_convert_fusion), channel_id=1, source_target_pairs={{0,3},{1,0},{2,1},{3,2},{4,7},{5,4},{6,5},{7,6},{8,11},{9,8},{10,9... | collective-permute-start | bytes 1572872 | tf_op jit(solution)/shard_map/ppermute | solution.py:40
  118.1 16.5 %copy-start.30 = (bf16[256,1024]{1,0:T(8,128)(2,1)S(1)}, bf16[256,1024]{1,0:T(8,128)(2,1)}, u32[]{:S(2)}) copy-start(bf16[256,1024]{1,0:T(8,128)(2,1)} %copy-done.29) | copy-start | bytes 1572868
  138.1 34.4 %all-to-all-start.2 = ((bf16[32,16,2048]{2,1,0:T(8,128)(2,1)}), bf16[32,16,2048]{2,1,0:T(8,128)(2,1)}, u32[]{:S(2)}, u32[]{:S(2)}) async-start(bf16[32,16,2048]{2,1,0:T(8,128)(2,1)} %bitcast.34), calls=%async_computation.2 | async-start | bytes 4194304 | tf_op jit(solution)/shard_map/all_to_all | solution.py:488
  145.6 16.0 %collective-permute-start.24 = (bf16[256,1024]{1,0:T(8,128)(2,1)S(1)}, bf16[256,1024]{1,0:T(8,128)(2,1)S(1)}, u32[]{:S(2)}, u32[]{:S(2)}) collective-permute-start(bf16[256,1024]{1,0:T(8,128)(2,1)S(1)} %get-tuple-element.36._.refs_0_), channel_id=1, source_target_pairs={{0,1},{1,2},{2,3},{3,0},{4,5},{5,6},{6,7},{7,4},{8,9},{9,10},{10,1... | collective-permute-start | bytes 1572872 | tf_op jit(solution)/shard_map/ppermute | solution.py:36
  146.9 15.0 %collective-permute-start.26 = (bf16[256,1024]{1,0:T(8,128)(2,1)}, bf16[256,1024]{1,0:T(8,128)(2,1)S(1)}, u32[]{:S(2)}, u32[]{:S(2)}) collective-permute-start(bf16[256,1024]{1,0:T(8,128)(2,1)} %get-tuple-element.45.refs_1_), channel_id=1, source_target_pairs={{0,3},{1,0},{2,1},{3,2},{4,7},{5,4},{6,5},{7,6},{8,11},{9,8},{10,9... | collective-permute-start | bytes 1572872 | tf_op jit(solution)/shard_map/ppermute | solution.py:40
  148.9 30.6 %collective-permute-start.22 = (bf16[256,1024]{1,0:T(8,128)(2,1)}, bf16[256,1024]{1,0:T(8,128)(2,1)}, u32[]{:S(2)}, u32[]{:S(2)}) collective-permute-start(bf16[256,1024]{1,0:T(8,128)(2,1)} %get-tuple-element.45.refs_1_), channel_id=1, source_target_pairs={{0,1},{1,2},{2,3},{3,0},{4,5},{5,6},{6,7},{7,4},{8,9},{9,10},{10,1... | collective-permute-start | bytes 1572872 | tf_op jit(solution)/shard_map/ppermute | solution.py:36
  148.9 30.5 %collective-permute-start.23 = (bf16[256,1024]{1,0:T(8,128)(2,1)S(1)}, bf16[256,1024]{1,0:T(8,128)(2,1)}, u32[]{:S(2)}, u32[]{:S(2)}) collective-permute-start(bf16[256,1024]{1,0:T(8,128)(2,1)S(1)} %get-tuple-element.36._.refs_0_), channel_id=1, source_target_pairs={{0,3},{1,0},{2,1},{3,2},{4,7},{5,4},{6,5},{7,6},{8,11},{9,8},{10,9... | collective-permute-start | bytes 1572872 | tf_op jit(solution)/shard_map/ppermute | solution.py:40
  158.3 7.8 %copy-start.2 = (f32[256,1280]{1,0:T(8,128)}, f32[256,1280]{1,0:T(8,128)S(1)}, u32[]{:S(2)}) copy-start(f32[256,1280]{1,0:T(8,128)S(1)} %shard_map.131.refs_1_.refs_2_) | copy-start | bytes 3932164
  168.8 14.6 %collective-permute-start.25 = (bf16[256,1024]{1,0:T(8,128)(2,1)}, bf16[256,1024]{1,0:T(8,128)(2,1)}, u32[]{:S(2)}, u32[]{:S(2)}) collective-permute-start(bf16[256,1024]{1,0:T(8,128)(2,1)} %shard_map.132), channel_id=1, source_target_pairs={{0,1},{1,2},{2,3},{3,0},{4,5},{5,6},{6,7},{7,4},{8,9},{9,10},{10,1... | collective-permute-start | bytes 1572872 | tf_op jit(solution)/shard_map/ppermute | solution.py:36
  170.3 13.1 %collective-permute-start.27 = (bf16[256,1024]{1,0:T(8,128)(2,1)}, bf16[256,1024]{1,0:T(8,128)(2,1)}, u32[]{:S(2)}, u32[]{:S(2)}) collective-permute-start(bf16[256,1024]{1,0:T(8,128)(2,1)} %shard_map.133), channel_id=1, source_target_pairs={{0,3},{1,0},{2,1},{3,2},{4,7},{5,4},{6,5},{7,6},{8,11},{9,8},{10,9... | collective-permute-start | bytes 1572872 | tf_op jit(solution)/shard_map/ppermute | solution.py:40
  172.5 10.9 %copy-start.5 = (bf16[384,2048]{1,0:T(8,128)(2,1)S(1)}, bf16[384,2048]{1,0:T(8,128)(2,1)}, u32[]{:S(2)}) copy-start(bf16[384,2048]{1,0:T(8,128)(2,1)} %copy-done.3) | copy-start | bytes 4718596
  172.5 10.9 %copy-start.15 = (f32[256,1280]{1,0:T(8,128)S(1)}, f32[256,1280]{1,0:T(8,128)}, u32[]{:S(2)}) copy-start(f32[256,1280]{1,0:T(8,128)} %copy-done.14) | copy-start | bytes 3932164
  172.5 10.9 %copy-start.24 = (f32[256,1280]{1,0:T(8,128)S(1)}, f32[256,1280]{1,0:T(8,128)}, u32[]{:S(2)}) copy-start(f32[256,1280]{1,0:T(8,128)} %copy-done.23) | copy-start | bytes 3932164
  (32 other events, 59.5 us)

commit v4 on v3

--- a/solution.py
+++ b/solution.py
@@ -12,7 +12,7 @@
 SMEM = pl.BlockSpec(memory_space=pltpu.SMEM)
 ANY = pl.BlockSpec(memory_space=pl.ANY)
 BF16, F32 = jnp.bfloat16, jnp.float32
-DIRECT = 384
+DIRECT = 416
 
 
 TOKEN = jax.ShapeDtypeStruct((8, 128), F32)
@@ -210,7 +210,7 @@
 
 
 def far_kernel(info_ref, h_ref, near_ref, p1, f1, p2, f2, direct, crossed, *refs):
-    outs, (buffer, whole, sems, out_sems) = refs[:8], refs[8:]
+    outs, (buffer, whole, held, sems, out_sems) = refs[:8], refs[8:]
     z, y_lo, core, parity = info_ref[0], info_ref[1], info_ref[2], info_ref[3]
     width = buffer.shape[2]
     jobs = [
@@ -222,10 +222,13 @@
         pltpu.make_async_copy(ref, buffer.at[i, pl.ds(DIRECT, ref.shape[0])], sems.at[i]).start()
         pltpu.make_async_copy(straight, buffer.at[i, pl.ds(0, DIRECT)], sems.at[i]).start()
     here = pltpu.make_async_copy(near_ref, whole.at[pl.ds(2 * y_lo, 2)], sems.at[4])
+    hidden = pltpu.make_async_copy(h_ref, held, sems.at[5])
+    hidden.start()
     here.start()
+    hidden.wait()
     for i, (_, low, half) in enumerate(jobs):
         pltpu.make_async_copy(buffer.at[i], buffer.at[i], sems.at[i]).wait()
-        part = jnp.dot(h_ref[...], buffer[i], preferred_element_type=F32)
+        part = jnp.dot(held[...], buffer[i], preferred_element_type=F32)
         at = pl.multiple_of(half * width, width)
         whole[2 - 2 * y_lo + low, :, pl.ds(at, width)] = part.astype(BF16)
     here.wait()
@@ -246,11 +249,12 @@
     return call(
         far_kernel,
         [out] * 8,
-        [SMEM, VMEM, ANY] + [ANY] * 6, [ANY] * 8,
+        [SMEM, ANY, ANY] + [ANY] * 6, [ANY] * 8,
         [
             pltpu.VMEM((4, h.shape[1], width // 2), BF16),
             pltpu.VMEM((4, rows, width), BF16),
-            pltpu.SemaphoreType.DMA((5,)),
+            pltpu.VMEM(h.shape, BF16),
+            pltpu.SemaphoreType.DMA((6,)),
             pltpu.SemaphoreType.DMA((8,)),
         ],
         27 << 27, 17 << 20,
@@ -311,7 +315,7 @@
         out_shape=(jax.ShapeDtypeStruct((slots, width), BF16), TOKEN),
         in_specs=[pl.BlockSpec((1, slots), lambda i: (0, 0)), pl.BlockSpec((count, step), lambda i: (0, i))],
         out_specs=(pl.BlockSpec((slots, step), lambda i: (0, i)), pl.BlockSpec((8, 128), lambda i: (0, 0))),
-        compiler_params=pltpu.CompilerParams(vmem_limit_bytes=46 << 20),
+        compiler_params=pltpu.CompilerParams(vmem_limit_bytes=61 << 20),
         cost_estimate=pl.CostEstimate(flops=16 << 27, bytes_accessed=6 << 20, transcendentals=0),
     )(at, rows)
 

time: 193 us -> 192 us (level)
  local copies, waits for them, and re-layouts: 29.1 us -> 22.2 us
  starting transfers between devices: 57.7 us -> 59.9 us
  Pallas kernels: 61.7 us -> 63.8 us
    unnamed x98 -> x86, local copies, waits for them, and re-layouts: 26 us -> 20.1 us
    pallas_call x1, Pallas kernels: 3.46 us -> 5.8 us  [pick_rows(): pl.pallas_call(pick_kernel, grid=(4,), out_shape=(jax.ShapeDtypeStruct((s...]
  transfers between devices with their start and end apart: 31 -> 31, of which waited for: 11 -> 13; matrix products, arithmetic and copies ran while one was open for 4% -> 3% of each run, Pallas kernels for 27% -> 28%
where the time goes in v4:
time: 192 us; the launch traced here: 191 us
  Pallas kernels  63.8 us (33%)
  starting transfers between devices  59.9 us (31%)
  waiting for transfers between devices  40.4 us (21%)
  local copies, waits for them, and re-layouts  22.2 us (12%)
  other arithmetic  3.65 us (2%)
    pallas_call x12, Pallas kernels, call(): pl.pallas_call(kernel, out_shape=out_shape, in_specs=in_specs, out_specs=...  51.1 us
    ppermute x8, waiting for transfers between devices, up(): return lax.ppermute(value, 'tensor', [(z, (z + 1) % 4) for z in range(4)])  30.5 us
    unnamed x86, local copies, waits for them, and re-layouts  20.1 us
    ppermute x8, starting transfers between devices, down(): return lax.ppermute(value, 'tensor', [(z, (z + 3) % 4) for z in range(4)])  19.9 us
    ppermute x12, starting transfers between devices, move(): return lax.ppermute(value, PLANE, pairs)  8.98 us
    ppermute x8, starting transfers between devices, up(): return lax.ppermute(value, 'tensor', [(z, (z + 1) % 4) for z in range(4)])  8.62 us
    all_to_all x1, starting transfers between devices, body(): swap(picked.reshape(groups, capacity, width))  7.66 us
    all_to_all x1, starting transfers between devices, body(): swap(send.reshape(groups, capacity, width))  7.54 us
  transfers between devices with their start and end apart: 31, of which 13 were waited for; matrix products, arithmetic and copies ran while one was open for 3% of the time, Pallas kernels for 28%

profile of v4, /device:TPU:8, one launch (start us, length us, event | category | flops | bytes accessed | tf_op | source)
XLA Modules:
  0.0 191.3 jit_solution(16346287040219339545)
XLA Ops:
  1.3 1.9 %copy-done.6 = bf16[1280,1280]{1,0:T(8,128)(2,1)S(1)} copy-done((bf16[1280,1280]{1,0:T(8,128)(2,1)S(1)}, bf16[1280,1280]{1,0:T(8,128)(2,1)}, u32[]{:S(2)}) %copy-start.6) | copy-done | bytes 3276824
  4.0 1.6 collective-permute-start
  5.6 1.9 %collective-permute-start.3 = (bf16[320,1024]{1,0:T(8,128)(2,1)}, bf16[320,1024]{1,0:T(8,128)(2,1)S(1)}, u32[]{:S(2)}, u32[]{:S(2)}) collective-permute-start(bf16[320,1024]{1,0:T(8,128)(2,1)} %bitcast.12.own_ref), channel_id=1, source_target_pairs={{0,1},{1,2},{2,3},{3,0},{4,5},{5,6},{6,7},{7,4},{8,9},{9,10},{10,1... | collective-permute-start | bytes 1966088 | tf_op jit(solution)/shard_map/ppermute | solution.py:36
  7.5 2.1 %collective-permute-start.4 = (bf16[320,1024]{1,0:T(8,128)(2,1)}, bf16[320,1024]{1,0:T(8,128)(2,1)S(1)}, u32[]{:S(2)}, u32[]{:S(2)}) collective-permute-start(bf16[320,1024]{1,0:T(8,128)(2,1)} %bitcast.12.own_ref), channel_id=1, source_target_pairs={{0,3},{1,0},{2,1},{3,2},{4,7},{5,4},{6,5},{7,6},{8,11},{9,8},{10,9... | collective-permute-start | bytes 1966088 | tf_op jit(solution)/shard_map/ppermute | solution.py:40
  11.5 7.2 %all-to-all-start = ((s32[32,1,16]{2,1,0:T(1,128)}), s32[32,1,16]{2,1,0:T(1,128)S(1)}, u32[]{:S(2)}, u32[]{:S(2)}) async-start(s32[32,1,16]{2,1,0:T(1,128)} %bitcast.3), calls=%async_computation | async-start | bytes 32768 | tf_op jit(solution)/shard_map/all_to_all | solution.py:447
  18.7 2.5 %shard_map.114 = (bf16[864,1024]{1,0:T(8,128)(2,1)S(1)}, bf16[416,2048]{1,0:T(8,128)(2,1)S(1)}) custom-call(s32[4]{0:T(128)S(1)} %pad_add_fusion.info_ref, bf16[1280,2048]{1,0:T(8,128)(2,1)} %refs_6_.1), custom_call_target="tpu_custom_call" | custom-call | bytes 5242880 | tf_op jit(solution)/shard_map/pallas_call | solution.py:54
  23.8 1.6 all-to-all-done
  26.5 1.6 collective-permute-start.10
  28.1 1.6 collective-permute-start.5
  29.7 2.0 %collective-permute-start.7 = (bf16[160,1024]{1,0:T(8,128)(2,1)S(1)}, bf16[160,1024]{1,0:T(8,128)(2,1)S(1)}, u32[]{:S(2)}, u32[]{:S(2)}) collective-permute-start(bf16[160,1024]{1,0:T(8,128)(2,1)S(1)} %slice.17), channel_id=1, source_target_pairs={{0,1},{1,2},{2,3},{3,0},{4,5},{5,6},{6,7},{7,4},{8,9},{9,10},{10,1... | collective-permute-start | bytes 983048 | tf_op jit(solution)/shard_map/ppermute | solution.py:36
  31.7 2.2 %collective-permute-start.8 = (bf16[160,1024]{1,0:T(8,128)(2,1)S(1)}, bf16[160,1024]{1,0:T(8,128)(2,1)S(1)}, u32[]{:S(2)}, u32[]{:S(2)}) collective-permute-start(bf16[160,1024]{1,0:T(8,128)(2,1)S(1)} %slice.18), channel_id=1, source_target_pairs={{0,3},{1,0},{2,1},{3,2},{4,7},{5,4},{6,5},{7,6},{8,11},{9,8},{10,9... | collective-permute-start | bytes 983048 | tf_op jit(solution)/shard_map/ppermute | solution.py:40
  35.7 5.8 %shard_map.113 = (bf16[512,2048]{1,0:T(8,128)(2,1)}, f32[8,128]{1,0:T(8,128)}) custom-call(s32[1,512]{1,0:T(1,128)} %reshape.92.at_ref, bf16[1024,2048]{1,0:T(8,128)(2,1)} %rows_ref.1), custom_call_target="tpu_custom_call" | custom-call | flops 2147483648 | bytes 6291456 | tf_op jit(solution)/shard_map/pallas_call | solution.py:312
  41.8 3.3 %shard_map.118 = (bf16[256,5120]{1,0:T(8,128)(2,1)S(1)}, f32[8,128]{1,0:T(8,128)}) custom-call(s32[4]{0:T(128)S(1)} %pad_add_fusion.info_ref, f32[1,1280]{1,0:T(1,128)S(1)} %reshape.94.gain_ref, bf16[320,1024]{1,0:T(8,128)(2,1)} %bitcast.12.own_ref, bf16[320,1024]{1,0:T(8,128)(2,1)S(1)} %copy-done.17, bf16[320,1024]{1,0:T(8,128)(2,1)S(1)} %copy-done.19, ...), custom_call_target="tpu_custom_call" | custom-call | flops 1073741824 | bytes 6291456 | tf_op jit(solution)/shard_map/pallas_call | solution.py:54
  45.1 3.8 %shard_map.119 = (f32[256,1280]{1,0:T(8,128)S(1)}, f32[8,128]{1,0:T(8,128)S(1)}) custom-call(s32[4]{0:T(128)S(1)} %pad_add_fusion.info_ref, bf16[256,5120]{1,0:T(8,128)(2,1)S(1)} %get-tuple-element.27.x_ref, bf16[1280,1280]{1,0:T(8,128)(2,1)S(1)} %copy-done.7, bf16[1280,1280]{1,0:T(8,128)(2,1)} %collective-permute-done.1.refs_2_.other_ref), custom_call_target="tpu_custom_call" | custom-call | flops 2281701376 | bytes 9437184 | tf_op jit(solution)/shard_map/pallas_call | solution.py:54
  50.5 1.3 collective-permute-start.9
  51.8 1.3 collective-permute-start.6
  55.3 2.3 %collective-permute-done.11.f2 = bf16[640,1280]{1,0:T(8,128)(2,1)} collective-permute-done((bf16[640,1280]{1,0:T(8,128)(2,1)}, bf16[640,1280]{1,0:T(8,128)(2,1)}, u32[]{:S(2)}, u32[]{:S(2)}) %collective-permute-start.11) | collective-permute-done | bytes 1638432 | tf_op jit(solution)/shard_map/ppermute | solution.py:32
  57.6 1.3 copy-done.23
  58.9 6.6 %shard_map.121 = (bf16[256,1280]{1,0:T(8,128)(2,1)S(1)}, f32[256,1280]{1,0:T(8,128)S(1)}) custom-call(s32[4]{0:T(128)S(1)} %pad_add_fusion.info_ref, bf16[256,5120]{1,0:T(8,128)(2,1)} %copy-done.8, f32[1,1280]{1,0:T(1,128)S(1)} %reshape.95.b_ref, f32[256,1280]{1,0:T(8,128)S(1)} %copy-done.23, bf16[640,1280]{1,0:T(8,128)(2,1)} %shard_map.116.refs_1_.p1, ...), custom_call_target="tpu_custom_call" | custom-call | flops 2281701376 | bytes 12582912 | tf_op jit(solution)/shard_map/pallas_call | solution.py:54
  65.6 5.1 %shard_map.122 = (bf16[2,256,2048]{2,1,0:T(8,128)(2,1)S(1)}, f32[8,128]{1,0:T(8,128)S(1)}) custom-call(s32[4]{0:T(128)S(1)} %pad_add_fusion.info_ref, bf16[256,1280]{1,0:T(8,128)(2,1)S(1)} %get-tuple-element.31.h_ref, bf16[1280,2048]{1,0:T(8,128)(2,1)S(1)} %bitcast.33, bf16[1280,2048]{1,0:T(8,128)(2,1)} %collective-permute-done.2.refs_3_.other_ref.refs_4_.refs_7_), custom_call_target="tpu_custom_call" | custom-call | flops 3623878656 | bytes 13631488 | tf_op jit(solution)/shard_map/pallas_call | solution.py:54
  71.3 1.3 copy-done.34
  72.6 3.3 %collective-permute-done.6.refs_0_ = bf16[864,1024]{1,0:T(8,128)(2,1)} collective-permute-done((bf16[864,1024]{1,0:T(8,128)(2,1)}, bf16[864,1024]{1,0:T(8,128)(2,1)}, u32[]{:S(2)}, u32[]{:S(2)}) %collective-permute-start.6) | collective-permute-done | bytes 1769504 | tf_op jit(solution)/shard_map/ppermute | solution.py:32
  77.7 7.7 %all-to-all-start.1 = ((bf16[32,16,2048]{2,1,0:T(8,128)(2,1)}), bf16[32,16,2048]{2,1,0:T(8,128)(2,1)}, u32[]{:S(2)}, u32[]{:S(2)}) async-start(bf16[32,16,2048]{2,1,0:T(8,128)(2,1)} %bitcast.36), calls=%async_computation.1 | async-start | bytes 4194304 | tf_op jit(solution)/shard_map/all_to_all | solution.py:482
  85.4 1.6 copy-done.33
  87.0 6.7 %shard_map.127 = (bf16[256,1024]{1,0:T(8,128)(2,1)S(1)}, bf16[256,1024]{1,0:T(8,128)(2,1)S(1)}, bf16[256,1024]{1,0:T(8,128)(2,1)S(1)}, bf16[256,1024]{1,0:T(8,12...) custom-call(s32[4]{0:T(128)S(1)} %pad_add_fusion.info_ref, ...), custom_call_target="tpu_custom_call" | custom-call | flops 3623878656 | bytes 17825792 | tf_op jit(solution)/shard_map/pallas_call | solution.py:54
  94.5 1.9 %collective-permute-start.18 = (bf16[256,1024]{1,0:T(8,128)(2,1)S(1)}, bf16[256,1024]{1,0:T(8,128)(2,1)S(1)}, u32[]{:S(2)}, u32[]{:S(2)}) collective-permute-start(bf16[256,1024]{1,0:T(8,128)(2,1)S(1)} %get-tuple-element.40), channel_id=1, source_target_pairs={{0,1},{1,2},{2,3},{3,0},{4,5},{5,6},{6,7},{7,4},{8,9},{9,10},{10,1... | collective-permute-start | bytes 1572872 | tf_op jit(solution)/shard_map/ppermute | solution.py:36
  96.4 2.1 %collective-permute-start.20 = (bf16[256,1024]{1,0:T(8,128)(2,1)S(1)}, bf16[256,1024]{1,0:T(8,128)(2,1)S(1)}, u32[]{:S(2)}, u32[]{:S(2)}) collective-permute-start(bf16[256,1024]{1,0:T(8,128)(2,1)S(1)} %get-tuple-element.43), channel_id=1, source_target_pairs={{0,3},{1,0},{2,1},{3,2},{4,7},{5,4},{6,5},{7,6},{8,11},{9,8},{10,9... | collective-permute-start | bytes 1572872 | tf_op jit(solution)/shard_map/ppermute | solution.py:40
  98.5 3.2 %collective-permute-start.17 = (bf16[256,1024]{1,0:T(8,128)(2,1)}, bf16[256,1024]{1,0:T(8,128)(2,1)}, u32[]{:S(2)}, u32[]{:S(2)}) collective-permute-start(bf16[256,1024]{1,0:T(8,128)(2,1)} %get-tuple-element.38), channel_id=1, source_target_pairs={{0,3},{1,0},{2,1},{3,2},{4,7},{5,4},{6,5},{7,6},{8,11},{9,8},{10,9... | collective-permute-start | bytes 1572872 | tf_op jit(solution)/shard_map/ppermute | solution.py:40
  101.8 9.5 %collective-permute-done.18 = bf16[256,1024]{1,0:T(8,128)(2,1)S(1)} collective-permute-done((bf16[256,1024]{1,0:T(8,128)(2,1)S(1)}, bf16[256,1024]{1,0:T(8,128)(2,1)S(1)}, u32[]{:S(2)}, u32[]{:S(2)}) %collective-permute-start.18) | collective-permute-done | bytes 524320 | tf_op jit(solution)/shard_map/ppermute | solution.py:36
  113.3 3.2 %collective-permute-start.21 = (bf16[256,1024]{1,0:T(8,128)(2,1)}, bf16[256,1024]{1,0:T(8,128)(2,1)}, u32[]{:S(2)}, u32[]{:S(2)}) collective-permute-start(bf16[256,1024]{1,0:T(8,128)(2,1)} %add_convert_fusion), channel_id=1, source_target_pairs={{0,3},{1,0},{2,1},{3,2},{4,7},{5,4},{6,5},{7,6},{8,11},{9,8},{10,9... | collective-permute-start | bytes 1572872 | tf_op jit(solution)/shard_map/ppermute | solution.py:40
  116.5 6.0 %collective-permute-done.16._.refs_4_ = bf16[256,1024]{1,0:T(8,128)(2,1)S(1)} collective-permute-done((bf16[256,1024]{1,0:T(8,128)(2,1)}, bf16[256,1024]{1,0:T(8,128)(2,1)S(1)}, u32[]{:S(2)}, u32[]{:S(2)}) %collective-permute-start.16) | collective-permute-done | bytes 524320 | tf_op jit(solution)/shard_map/ppermute | solution.py:36
  122.5 3.1 %shard_map.128 = (bf16[256,1024]{1,0:T(8,128)(2,1)S(1)}, bf16[256,1024]{1,0:T(8,128)(2,1)}) custom-call(s32[1,256]{1,0:T(1,128)S(1)} %bitcast_add_fusion.code_ref, bf16[512,2048]{1,0:T(8,128)(2,1)} %bitcast.14.rows_ref, bf16[256,1024]{1,0:T(8,128)(2,1)S(1)} %collective-permute-done.16._.refs_4_), custom_call_target="tpu_custom_call" | custom-call | flops 536870912 | bytes 3145728 | tf_op jit(solution)/shard_map/pallas_call | solution.py:54
  125.6 7.7 %collective-permute-done.19.refs_2_ = bf16[256,1024]{1,0:T(8,128)(2,1)} collective-permute-done((bf16[256,1024]{1,0:T(8,128)(2,1)}, bf16[256,1024]{1,0:T(8,128)(2,1)}, u32[]{:S(2)}, u32[]{:S(2)}) %collective-permute-start.19) | collective-permute-done | bytes 524320 | tf_op jit(solution)/shard_map/ppermute | solution.py:36
  133.4 2.2 %shard_map.129 = bf16[512,2048]{1,0:T(8,128)(2,1)S(1)} custom-call(s32[1,256]{1,0:T(1,128)S(1)} %bitcast_add_fusion.code_ref, f32[1,2048]{1,0:T(1,128)S(1)} %bitcast.35, bf16[256,1024]{1,0:T(8,128)(2,1)S(1)} %get-tuple-element.36._.refs_0_, bf16[256,1024]{1,0:T(8,128)(2,1)S(1)} %copy-done.25, bf16[256,1024]{1,0:T(8,128)(2,1)} %collective-permute-done.17.refs_1_, ...), custom_call_target="tpu_custom_call" | custom-call | flops 536870912 | bytes 6291456 | tf_op jit(solution)/shard_map/pallas_call | solution.py:54
  135.6 1.3 copy-done.9
  136.9 7.5 %all-to-all-start.2 = ((bf16[32,16,2048]{2,1,0:T(8,128)(2,1)}), bf16[32,16,2048]{2,1,0:T(8,128)(2,1)}, u32[]{:S(2)}, u32[]{:S(2)}) async-start(bf16[32,16,2048]{2,1,0:T(8,128)(2,1)} %bitcast.34), calls=%async_computation.2 | async-start | bytes 4194304 | tf_op jit(solution)/shard_map/all_to_all | solution.py:492
  144.4 1.3 collective-permute-start.24
  145.7 2.0 %collective-permute-start.26 = (bf16[256,1024]{1,0:T(8,128)(2,1)}, bf16[256,1024]{1,0:T(8,128)(2,1)S(1)}, u32[]{:S(2)}, u32[]{:S(2)}) collective-permute-start(bf16[256,1024]{1,0:T(8,128)(2,1)} %get-tuple-element.45.refs_1_), channel_id=1, source_target_pairs={{0,3},{1,0},{2,1},{3,2},{4,7},{5,4},{6,5},{7,6},{8,11},{9,8},{10,9... | collective-permute-start | bytes 1572872 | tf_op jit(solution)/shard_map/ppermute | solution.py:40
  147.8 3.2 %collective-permute-start.23 = (bf16[256,1024]{1,0:T(8,128)(2,1)S(1)}, bf16[256,1024]{1,0:T(8,128)(2,1)}, u32[]{:S(2)}, u32[]{:S(2)}) collective-permute-start(bf16[256,1024]{1,0:T(8,128)(2,1)S(1)} %get-tuple-element.36._.refs_0_), channel_id=1, source_target_pairs={{0,3},{1,0},{2,1},{3,2},{4,7},{5,4},{6,5},{7,6},{8,11},{9,8},{10,9... | collective-permute-start | bytes 1572872 | tf_op jit(solution)/shard_map/ppermute | solution.py:40
  151.0 1.5 copy-done.4
  152.4 4.7 %shard_map.131.refs_1_.refs_2_ = f32[256,1280]{1,0:T(8,128)S(1)} custom-call(s32[4]{0:T(128)S(1)} %pad_add_fusion.info_ref, bf16[256,1024]{1,0:T(8,128)(2,1)S(1)} %get-tuple-element.36._.refs_0_, bf16[256,1024]{1,0:T(8,128)(2,1)} %get-tuple-element.45.refs_1_, bf16[1280,2048]{1,0:T(8,128)(2,1)} %refs_6_.1, ...), custom_call_target="tpu_custom_call" | custom-call | flops 1879048192 | bytes 6291456 | tf_op jit(solution)/shard_map/pallas_call | solution.py:54
  157.2 3.3 %collective-permute-done.24.refs_0_ = bf16[256,1024]{1,0:T(8,128)(2,1)S(1)} collective-permute-done((bf16[256,1024]{1,0:T(8,128)(2,1)S(1)}, bf16[256,1024]{1,0:T(8,128)(2,1)S(1)}, u32[]{:S(2)}, u32[]{:S(2)}) %collective-permute-start.24) | collective-permute-done | bytes 524320 | tf_op jit(solution)/shard_map/ppermute | solution.py:36
  160.8 4.2 %shard_map.134.refs_4_ = f32[256,1280]{1,0:T(8,128)S(1)} custom-call(s32[4]{0:T(128)S(1)} %pad_add_fusion.info_ref, bf16[256,1024]{1,0:T(8,128)(2,1)S(1)} %collective-permute-done.24.refs_0_, bf16[256,1024]{1,0:T(8,128)(2,1)S(1)} %collective-permute-done.26.refs_0_.refs_1_, f32[256,1280]{1,0:T(8,128)S(1)} %shard_map.131.refs_1_.refs_2_, ...), custom_call_target="tpu_custom_call" | custom-call | flops 1879048192 | bytes 6291456 | tf_op jit(solution)/shard_map/pallas_call | solution.py:54
  167.7 1.4 collective-permute-start.25
  169.1 1.8 collective-permute-start.27
  171.4 6.9 %shard_map.130 = (bf16[1024,2048]{1,0:T(8,128)(2,1)}, f32[8,128]{1,0:T(8,128)}) custom-call(s32[1,512]{1,0:T(1,128)} %reshape.92.at_ref, bf16[1024,2048]{1,0:T(8,128)(2,1)} %text_ref.1, bf16[512,2048]{1,0:T(8,128)(2,1)} %bitcast.16.got_ref), custom_call_target="tpu_custom_call" | custom-call | flops 2147483648 | bytes 10485760 | tf_op jit(solution)/shard_map/pallas_call | solution.py:334
  178.3 4.0 %collective-permute-done.25.refs_2_ = bf16[256,1024]{1,0:T(8,128)(2,1)} collective-permute-done((bf16[256,1024]{1,0:T(8,128)(2,1)}, bf16[256,1024]{1,0:T(8,128)(2,1)}, u32[]{:S(2)}, u32[]{:S(2)}) %collective-permute-start.25) | collective-permute-done | bytes 524320 | tf_op jit(solution)/shard_map/ppermute | solution.py:36
  183.0 8.1 %shard_map.135 = bf16[256,1280]{1,0:T(8,128)(2,1)} custom-call(s32[4]{0:T(128)S(1)} %pad_add_fusion.info_ref, bf16[256,1024]{1,0:T(8,128)(2,1)} %collective-permute-done.22.refs_0_, bf16[256,1024]{1,0:T(8,128)(2,1)} %collective-permute-done.23.refs_1_, bf16[256,1024]{1,0:T(8,128)(2,1)} %collective-permute-done.25.refs_2_, ...), custom_call_target="tpu_custom_call" | custom-call | flops 3758096384 | bytes 12582912 | tf_op jit(solution)/shard_map/pallas_call | solution.py:54
  (145 shorter events, 22.0 us)
Async XLA Ops:
  0.6 24.9 %collective-permute-start.2 = (bf16[1280,2048]{1,0:T(8,128)(2,1)}, bf16[1280,2048]{1,0:T(8,128)(2,1)}, u32[]{:S(2)}, u32[]{:S(2)}) collective-permute-start(bf16[1280,2048]{1,0:T(8,128)(2,1)} %refs_6_.1), channel_id=1, source_target_pairs={{0,4},{4,0},{8,12},{12,8},{16,20},{20,16},{24,28},{28,24},{32,36},... | collective-permute-start | bytes 15728648 | tf_op jit(solution)/shard_map/ppermute | solution.py:32
  0.7 24.8 %collective-permute-start.1 = (bf16[1280,1280]{1,0:T(8,128)(2,1)}, bf16[1280,1280]{1,0:T(8,128)(2,1)}, u32[]{:S(2)}, u32[]{:S(2)}) collective-permute-start(bf16[1280,1280]{1,0:T(8,128)(2,1)} %own_ref.6), channel_id=1, source_target_pairs={{0,4},{4,0},{8,12},{12,8},{16,20},{20,16},{24,28},{28,24},{32,36},... | collective-permute-start | bytes 9830408 | tf_op jit(solution)/shard_map/ppermute | solution.py:32
  3.2 6.4 %copy-start.37 = (s32[256,1]{0,1:T(1,128)S(1)}, s32[256,1]{0,1:T(1,128)}, u32[]{:S(2)}) copy-start(s32[256,1]{0,1:T(1,128)} %param.17) | copy-start | bytes 3076
  3.2 7.4 %copy-start.40 = (s32[256]{0:T(256)S(1)}, s32[256]{0:T(256)}, u32[]{:S(2)}) copy-start(s32[256]{0:T(256)} %param.18) | copy-start | bytes 3076
  4.0 21.5 %collective-permute-start = (bf16[640,1280]{1,0:T(8,128)(2,1)S(1)}, bf16[640,1280]{1,0:T(8,128)(2,1)}, u32[]{:S(2)}, u32[]{:S(2)}) collective-permute-start(bf16[640,1280]{1,0:T(8,128)(2,1)S(1)} %shard_map.115), channel_id=1, source_target_pairs={{0,8},{4,28},{8,16},{12,4},{16,24},{20,12},{24,0},{28,20},{32,40},... | collective-permute-start | bytes 4915208 | tf_op jit(solution)/shard_map/ppermute | solution.py:32
  5.6 19.8 %collective-permute-start.3 = (bf16[320,1024]{1,0:T(8,128)(2,1)}, bf16[320,1024]{1,0:T(8,128)(2,1)S(1)}, u32[]{:S(2)}, u32[]{:S(2)}) collective-permute-start(bf16[320,1024]{1,0:T(8,128)(2,1)} %bitcast.12.own_ref), channel_id=1, source_target_pairs={{0,1},{1,2},{2,3},{3,0},{4,5},{5,6},{6,7},{7,4},{8,9},{9,10},{10,1... | collective-permute-start | bytes 1966088 | tf_op jit(solution)/shard_map/ppermute | solution.py:36
  7.5 17.9 %collective-permute-start.4 = (bf16[320,1024]{1,0:T(8,128)(2,1)}, bf16[320,1024]{1,0:T(8,128)(2,1)S(1)}, u32[]{:S(2)}, u32[]{:S(2)}) collective-permute-start(bf16[320,1024]{1,0:T(8,128)(2,1)} %bitcast.12.own_ref), channel_id=1, source_target_pairs={{0,3},{1,0},{2,1},{3,2},{4,7},{5,4},{6,5},{7,6},{8,11},{9,8},{10,9... | collective-permute-start | bytes 1966088 | tf_op jit(solution)/shard_map/ppermute | solution.py:40
  11.5 14.0 %all-to-all-start = ((s32[32,1,16]{2,1,0:T(1,128)}), s32[32,1,16]{2,1,0:T(1,128)S(1)}, u32[]{:S(2)}, u32[]{:S(2)}) async-start(s32[32,1,16]{2,1,0:T(1,128)} %bitcast.3), calls=%async_computation | async-start | bytes 32768 | tf_op jit(solution)/shard_map/all_to_all | solution.py:447
  26.5 5.2 %copy-start.19 = (bf16[320,1024]{1,0:T(8,128)(2,1)S(1)}, bf16[320,1024]{1,0:T(8,128)(2,1)}, u32[]{:S(2)}) copy-start(bf16[320,1024]{1,0:T(8,128)(2,1)} %copy-done.18) | copy-start | bytes 1966084
  26.5 7.4 %copy-start.38 = (f32[1280]{0:T(1024)S(1)}, f32[1280]{0:T(1024)}, u32[]{:S(2)}) copy-start(f32[1280]{0:T(1024)} %param.11) | copy-start | bytes 15364
  26.5 7.9 %copy-start.36 = (s32[32,1,16]{2,1,0:T(1,128)S(1)}, s32[32,1,16]{2,1,0:T(1,128)}, u32[]{:S(2)}) copy-start(s32[32,1,16]{2,1,0:T(1,128)} %copy-done.35) | copy-start | bytes 6148
  26.5 25.3 %collective-permute-start.10 = (bf16[640,1280]{1,0:T(8,128)(2,1)}, bf16[640,1280]{1,0:T(8,128)(2,1)}, u32[]{:S(2)}, u32[]{:S(2)}) collective-permute-start(bf16[640,1280]{1,0:T(8,128)(2,1)} %shard_map.116.refs_1_.p1), channel_id=1, source_target_pairs={{0,32},{4,100},{8,40},{12,108},{16,48},{20,116},{24,56},{28,124},{... | collective-permute-start | bytes 4915208 | tf_op jit(solution)/shard_map/ppermute | solution.py:32
  28.1 23.7 %collective-permute-start.5 = (bf16[864,1024]{1,0:T(8,128)(2,1)}, bf16[864,1024]{1,0:T(8,128)(2,1)}, u32[]{:S(2)}, u32[]{:S(2)}) collective-permute-start(bf16[864,1024]{1,0:T(8,128)(2,1)} %shard_map.117), channel_id=1, source_target_pairs={{0,8},{4,28},{8,16},{12,4},{16,24},{20,12},{24,0},{28,20},{32,40},... | collective-permute-start | bytes 5308424 | tf_op jit(solution)/shard_map/ppermute | solution.py:32
  29.7 11.9 %collective-permute-start.7 = (bf16[160,1024]{1,0:T(8,128)(2,1)S(1)}, bf16[160,1024]{1,0:T(8,128)(2,1)S(1)}, u32[]{:S(2)}, u32[]{:S(2)}) collective-permute-start(bf16[160,1024]{1,0:T(8,128)(2,1)S(1)} %slice.17), channel_id=1, source_target_pairs={{0,1},{1,2},{2,3},{3,0},{4,5},{5,6},{6,7},{7,4},{8,9},{9,10},{10,1... | collective-permute-start | bytes 983048 | tf_op jit(solution)/shard_map/ppermute | solution.py:36
  31.7 10.1 %collective-permute-start.8 = (bf16[160,1024]{1,0:T(8,128)(2,1)S(1)}, bf16[160,1024]{1,0:T(8,128)(2,1)S(1)}, u32[]{:S(2)}, u32[]{:S(2)}) collective-permute-start(bf16[160,1024]{1,0:T(8,128)(2,1)S(1)} %slice.18), channel_id=1, source_target_pairs={{0,3},{1,0},{2,1},{3,2},{4,7},{5,4},{6,5},{7,6},{8,11},{9,8},{10,9... | collective-permute-start | bytes 983048 | tf_op jit(solution)/shard_map/ppermute | solution.py:40
  50.5 4.8 %collective-permute-start.9 = (bf16[640,1280]{1,0:T(8,128)(2,1)}, bf16[640,1280]{1,0:T(8,128)(2,1)}, u32[]{:S(2)}, u32[]{:S(2)}) collective-permute-start(bf16[640,1280]{1,0:T(8,128)(2,1)} %shard_map.116.refs_1_.p1), channel_id=1, source_target_pairs={{0,4},{4,0},{8,12},{12,8},{16,20},{20,16},{24,28},{28,24},{32,36},... | collective-permute-start | bytes 4915208 | tf_op jit(solution)/shard_map/ppermute | solution.py:32
  51.8 5.8 %collective-permute-start.11 = (bf16[640,1280]{1,0:T(8,128)(2,1)}, bf16[640,1280]{1,0:T(8,128)(2,1)}, u32[]{:S(2)}, u32[]{:S(2)}) collective-permute-start(bf16[640,1280]{1,0:T(8,128)(2,1)} %shard_map.120.p2), channel_id=1, source_target_pairs={{0,4},{4,0},{8,12},{12,8},{16,20},{20,16},{24,28},{28,24},{32,36},... | collective-permute-start | bytes 4915208 | tf_op jit(solution)/shard_map/ppermute | solution.py:32
  51.8 24.1 %collective-permute-start.6 = (bf16[864,1024]{1,0:T(8,128)(2,1)}, bf16[864,1024]{1,0:T(8,128)(2,1)}, u32[]{:S(2)}, u32[]{:S(2)}) collective-permute-start(bf16[864,1024]{1,0:T(8,128)(2,1)} %collective-permute-done.5.refs_1_.p1.refs_4_.refs_5_.refs_8_), channel_id=1, source_target_pairs={{0,32},{4,100},{8,40},{12,108},{16,48},{20,116},{24,56},{28,124},{... | collective-permute-start | bytes 5308424 | tf_op jit(solution)/shard_map/ppermute | solution.py:32
  53.2 12.4 %slice-start = ((s8[5242880]{0:T(1024)(128)(4,1)}), s8[1048576]{0:T(1024)(128)(4,1)S(1)}, s32[]{:S(2)}) async-start(s8[5242880]{0:T(1024)(128)(4,1)} %bitcast.32), calls=%async_computation.3 | async-start | bytes 2097152
  53.2 23.2 %collective-permute-start.12 = (bf16[416,2048]{1,0:T(8,128)(2,1)}, bf16[416,2048]{1,0:T(8,128)(2,1)S(1)}, u32[]{:S(2)}, u32[]{:S(2)}) collective-permute-start(bf16[416,2048]{1,0:T(8,128)(2,1)} %shard_map.124), channel_id=1, source_target_pairs={{0,8},{4,28},{8,16},{12,4},{16,24},{20,12},{24,0},{28,20},{32,40},... | collective-permute-start | bytes 5111816 | tf_op jit(solution)/shard_map/ppermute | solution.py:32
  54.0 31.4 %collective-permute-start.13 = (bf16[864,1024]{1,0:T(8,128)(2,1)}, bf16[864,1024]{1,0:T(8,128)(2,1)}, u32[]{:S(2)}, u32[]{:S(2)}) collective-permute-start(bf16[864,1024]{1,0:T(8,128)(2,1)} %collective-permute-done.5.refs_1_.p1.refs_4_.refs_5_.refs_8_), channel_id=1, source_target_pairs={{0,4},{4,0},{8,12},{12,8},{16,20},{20,16},{24,28},{28,24},{32,36},... | collective-permute-start | bytes 5308424 | tf_op jit(solution)/shard_map/ppermute | solution.py:32
  58.9 6.6 %slice-start.1 = ((s8[5242880]{0:T(1024)(128)(4,1)}), s8[4194304]{0:T(1024)(128)(4,1)S(1)}, s32[]{:S(2)}) async-start(s8[5242880]{0:T(1024)(128)(4,1)} %bitcast.32), calls=%async_computation.4 | async-start | bytes 8388608
  75.9 9.5 %collective-permute-start.14 = (bf16[864,1024]{1,0:T(8,128)(2,1)}, bf16[864,1024]{1,0:T(8,128)(2,1)}, u32[]{:S(2)}, u32[]{:S(2)}) collective-permute-start(bf16[864,1024]{1,0:T(8,128)(2,1)} %shard_map.123.refs_1_.p2.refs_6_.refs_7_.refs_10_), channel_id=1, source_target_pairs={{0,4},{4,0},{8,12},{12,8},{16,20},{20,16},{24,28},{28,24},{32,36},... | collective-permute-start | bytes 5308424 | tf_op jit(solution)/shard_map/ppermute | solution.py:32
  77.7 7.7 %collective-permute-start.15 = (bf16[416,2048]{1,0:T(8,128)(2,1)}, bf16[416,2048]{1,0:T(8,128)(2,1)S(1)}, u32[]{:S(2)}, u32[]{:S(2)}) collective-permute-start(bf16[416,2048]{1,0:T(8,128)(2,1)} %shard_map.125.refs_2_.direct.refs_8_.refs_9_.refs_12_), channel_id=1, source_target_pairs={{0,4},{4,0},{8,12},{12,8},{16,20},{20,16},{24,28},{28,24},{32,36},... | collective-permute-start | bytes 5111816 | tf_op jit(solution)/shard_map/ppermute | solution.py:32
  77.7 7.7 %copy-start.1 = (bf16[416,2048]{1,0:T(8,128)(2,1)S(1)}, bf16[416,2048]{1,0:T(8,128)(2,1)}, u32[]{:S(2)}) copy-start(bf16[416,2048]{1,0:T(8,128)(2,1)} %shard_map.125.refs_2_.direct.refs_8_.refs_9_.refs_12_) | copy-start | bytes 5111812
  77.7 38.8 %all-to-all-start.1 = ((bf16[32,16,2048]{2,1,0:T(8,128)(2,1)}), bf16[32,16,2048]{2,1,0:T(8,128)(2,1)}, u32[]{:S(2)}, u32[]{:S(2)}) async-start(bf16[32,16,2048]{2,1,0:T(8,128)(2,1)} %bitcast.36), calls=%async_computation.1 | async-start | bytes 4194304 | tf_op jit(solution)/shard_map/all_to_all | solution.py:482
  85.4 8.3 %copy-start.3 = (bf16[416,2048]{1,0:T(8,128)(2,1)}, bf16[416,2048]{1,0:T(8,128)(2,1)S(1)}, u32[]{:S(2)}) copy-start(bf16[416,2048]{1,0:T(8,128)(2,1)S(1)} %collective-permute-done.15.crossed.refs_9_.refs_10_.refs_13_) | copy-start | bytes 5111812
  94.5 17.8 %copy-start.26 = (bf16[256,1024]{1,0:T(8,128)(2,1)}, bf16[256,1024]{1,0:T(8,128)(2,1)S(1)}, u32[]{:S(2)}) copy-start(bf16[256,1024]{1,0:T(8,128)(2,1)S(1)} %get-tuple-element.41.refs_3_) | copy-start | bytes 1572868
  94.5 16.7 %collective-permute-start.18 = (bf16[256,1024]{1,0:T(8,128)(2,1)S(1)}, bf16[256,1024]{1,0:T(8,128)(2,1)S(1)}, u32[]{:S(2)}, u32[]{:S(2)}) collective-permute-start(bf16[256,1024]{1,0:T(8,128)(2,1)S(1)} %get-tuple-element.40), channel_id=1, source_target_pairs={{0,1},{1,2},{2,3},{3,0},{4,5},{5,6},{6,7},{7,4},{8,9},{9,10},{10,1... | collective-permute-start | bytes 1572872 | tf_op jit(solution)/shard_map/ppermute | solution.py:36
  96.4 15.8 %collective-permute-start.20 = (bf16[256,1024]{1,0:T(8,128)(2,1)S(1)}, bf16[256,1024]{1,0:T(8,128)(2,1)S(1)}, u32[]{:S(2)}, u32[]{:S(2)}) collective-permute-start(bf16[256,1024]{1,0:T(8,128)(2,1)S(1)} %get-tuple-element.43), channel_id=1, source_target_pairs={{0,3},{1,0},{2,1},{3,2},{4,7},{5,4},{6,5},{7,6},{8,11},{9,8},{10,9... | collective-permute-start | bytes 1572872 | tf_op jit(solution)/shard_map/ppermute | solution.py:40
  98.5 23.9 %collective-permute-start.16 = (bf16[256,1024]{1,0:T(8,128)(2,1)}, bf16[256,1024]{1,0:T(8,128)(2,1)S(1)}, u32[]{:S(2)}, u32[]{:S(2)}) collective-permute-start(bf16[256,1024]{1,0:T(8,128)(2,1)} %get-tuple-element.35), channel_id=1, source_target_pairs={{0,1},{1,2},{2,3},{3,0},{4,5},{5,6},{6,7},{7,4},{8,9},{9,10},{10,1... | collective-permute-start | bytes 1572872 | tf_op jit(solution)/shard_map/ppermute | solution.py:36
  98.5 27.1 %collective-permute-start.17 = (bf16[256,1024]{1,0:T(8,128)(2,1)}, bf16[256,1024]{1,0:T(8,128)(2,1)}, u32[]{:S(2)}, u32[]{:S(2)}) collective-permute-start(bf16[256,1024]{1,0:T(8,128)(2,1)} %get-tuple-element.38), channel_id=1, source_target_pairs={{0,3},{1,0},{2,1},{3,2},{4,7},{5,4},{6,5},{7,6},{8,11},{9,8},{10,9... | collective-permute-start | bytes 1572872 | tf_op jit(solution)/shard_map/ppermute | solution.py:40
  112.2 21.1 %collective-permute-start.19 = (bf16[256,1024]{1,0:T(8,128)(2,1)}, bf16[256,1024]{1,0:T(8,128)(2,1)}, u32[]{:S(2)}, u32[]{:S(2)}) collective-permute-start(bf16[256,1024]{1,0:T(8,128)(2,1)} %add_convert_fusion.1), channel_id=1, source_target_pairs={{0,1},{1,2},{2,3},{3,0},{4,5},{5,6},{6,7},{7,4},{8,9},{9,10},{10,1... | collective-permute-start | bytes 1572872 | tf_op jit(solution)/shard_map/ppermute | solution.py:36
  112.3 21.1 %copy-start.25 = (bf16[256,1024]{1,0:T(8,128)(2,1)S(1)}, bf16[256,1024]{1,0:T(8,128)(2,1)}, u32[]{:S(2)}) copy-start(bf16[256,1024]{1,0:T(8,128)(2,1)} %copy-done.24) | copy-start | bytes 1572868
  112.3 21.1 %copy-start.29 = (f32[2048]{0:T(1024)S(1)}, f32[2048]{0:T(1024)}, u32[]{:S(2)}) copy-start(f32[2048]{0:T(1024)} %param.15) | copy-start | bytes 24580
  113.3 20.1 %collective-permute-start.21 = (bf16[256,1024]{1,0:T(8,128)(2,1)}, bf16[256,1024]{1,0:T(8,128)(2,1)}, u32[]{:S(2)}, u32[]{:S(2)}) collective-permute-start(bf16[256,1024]{1,0:T(8,128)(2,1)} %add_convert_fusion), channel_id=1, source_target_pairs={{0,3},{1,0},{2,1},{3,2},{4,7},{5,4},{6,5},{7,6},{8,11},{9,8},{10,9... | collective-permute-start | bytes 1572872 | tf_op jit(solution)/shard_map/ppermute | solution.py:40
  116.5 16.9 %copy-start.27 = (bf16[256,1024]{1,0:T(8,128)(2,1)S(1)}, bf16[256,1024]{1,0:T(8,128)(2,1)}, u32[]{:S(2)}) copy-start(bf16[256,1024]{1,0:T(8,128)(2,1)} %copy-done.26) | copy-start | bytes 1572868
  136.9 34.5 %all-to-all-start.2 = ((bf16[32,16,2048]{2,1,0:T(8,128)(2,1)}), bf16[32,16,2048]{2,1,0:T(8,128)(2,1)}, u32[]{:S(2)}, u32[]{:S(2)}) async-start(bf16[32,16,2048]{2,1,0:T(8,128)(2,1)} %bitcast.34), calls=%async_computation.2 | async-start | bytes 4194304 | tf_op jit(solution)/shard_map/all_to_all | solution.py:492
  144.4 16.0 %collective-permute-start.24 = (bf16[256,1024]{1,0:T(8,128)(2,1)S(1)}, bf16[256,1024]{1,0:T(8,128)(2,1)S(1)}, u32[]{:S(2)}, u32[]{:S(2)}) collective-permute-start(bf16[256,1024]{1,0:T(8,128)(2,1)S(1)} %get-tuple-element.36._.refs_0_), channel_id=1, source_target_pairs={{0,1},{1,2},{2,3},{3,0},{4,5},{5,6},{6,7},{7,4},{8,9},{9,10},{10,1... | collective-permute-start | bytes 1572872 | tf_op jit(solution)/shard_map/ppermute | solution.py:36
  145.7 15.0 %collective-permute-start.26 = (bf16[256,1024]{1,0:T(8,128)(2,1)}, bf16[256,1024]{1,0:T(8,128)(2,1)S(1)}, u32[]{:S(2)}, u32[]{:S(2)}) collective-permute-start(bf16[256,1024]{1,0:T(8,128)(2,1)} %get-tuple-element.45.refs_1_), channel_id=1, source_target_pairs={{0,3},{1,0},{2,1},{3,2},{4,7},{5,4},{6,5},{7,6},{8,11},{9,8},{10,9... | collective-permute-start | bytes 1572872 | tf_op jit(solution)/shard_map/ppermute | solution.py:40
  147.7 30.6 %collective-permute-start.22 = (bf16[256,1024]{1,0:T(8,128)(2,1)}, bf16[256,1024]{1,0:T(8,128)(2,1)}, u32[]{:S(2)}, u32[]{:S(2)}) collective-permute-start(bf16[256,1024]{1,0:T(8,128)(2,1)} %get-tuple-element.45.refs_1_), channel_id=1, source_target_pairs={{0,1},{1,2},{2,3},{3,0},{4,5},{5,6},{6,7},{7,4},{8,9},{9,10},{10,1... | collective-permute-start | bytes 1572872 | tf_op jit(solution)/shard_map/ppermute | solution.py:36
  147.8 30.5 %collective-permute-start.23 = (bf16[256,1024]{1,0:T(8,128)(2,1)S(1)}, bf16[256,1024]{1,0:T(8,128)(2,1)}, u32[]{:S(2)}, u32[]{:S(2)}) collective-permute-start(bf16[256,1024]{1,0:T(8,128)(2,1)S(1)} %get-tuple-element.36._.refs_0_), channel_id=1, source_target_pairs={{0,3},{1,0},{2,1},{3,2},{4,7},{5,4},{6,5},{7,6},{8,11},{9,8},{10,9... | collective-permute-start | bytes 1572872 | tf_op jit(solution)/shard_map/ppermute | solution.py:40
  157.2 7.8 %copy-start.2 = (f32[256,1280]{1,0:T(8,128)}, f32[256,1280]{1,0:T(8,128)S(1)}, u32[]{:S(2)}) copy-start(f32[256,1280]{1,0:T(8,128)S(1)} %shard_map.131.refs_1_.refs_2_) | copy-start | bytes 3932164
  167.7 14.6 %collective-permute-start.25 = (bf16[256,1024]{1,0:T(8,128)(2,1)}, bf16[256,1024]{1,0:T(8,128)(2,1)}, u32[]{:S(2)}, u32[]{:S(2)}) collective-permute-start(bf16[256,1024]{1,0:T(8,128)(2,1)} %shard_map.132), channel_id=1, source_target_pairs={{0,1},{1,2},{2,3},{3,0},{4,5},{5,6},{6,7},{7,4},{8,9},{9,10},{10,1... | collective-permute-start | bytes 1572872 | tf_op jit(solution)/shard_map/ppermute | solution.py:36
  169.1 13.1 %collective-permute-start.27 = (bf16[256,1024]{1,0:T(8,128)(2,1)}, bf16[256,1024]{1,0:T(8,128)(2,1)}, u32[]{:S(2)}, u32[]{:S(2)}) collective-permute-start(bf16[256,1024]{1,0:T(8,128)(2,1)} %shard_map.133), channel_id=1, source_target_pairs={{0,3},{1,0},{2,1},{3,2},{4,7},{5,4},{6,5},{7,6},{8,11},{9,8},{10,9... | collective-permute-start | bytes 1572872 | tf_op jit(solution)/shard_map/ppermute | solution.py:40
  171.4 10.9 %copy-start.5 = (bf16[416,2048]{1,0:T(8,128)(2,1)S(1)}, bf16[416,2048]{1,0:T(8,128)(2,1)}, u32[]{:S(2)}) copy-start(bf16[416,2048]{1,0:T(8,128)(2,1)} %copy-done.3) | copy-start | bytes 5111812
  171.4 10.9 %copy-start.12 = (f32[256,1280]{1,0:T(8,128)S(1)}, f32[256,1280]{1,0:T(8,128)}, u32[]{:S(2)}) copy-start(f32[256,1280]{1,0:T(8,128)} %copy-done.11) | copy-start | bytes 3932164
  171.4 10.9 %copy-start.21 = (f32[256,1280]{1,0:T(8,128)S(1)}, f32[256,1280]{1,0:T(8,128)}, u32[]{:S(2)}) copy-start(f32[256,1280]{1,0:T(8,128)} %copy-done.20) | copy-start | bytes 3932164
  (26 other events, 43.2 us)

commit v5 on v4

--- a/solution.py
+++ b/solution.py
@@ -78,11 +78,11 @@
         copy.wait()
 
 
-def parts_of(info, own, cuts, *tokens):
+def parts_of(info, own, cuts, *tokens, limit=46):
     out = [jax.ShapeDtypeStruct((rows, cols), BF16) for _, rows, _, cols in cuts]
     return call(
         functools.partial(parts_kernel, cuts), out, [SMEM] + [ANY] * (1 + len(tokens)), [VMEM] * len(out),
-        [pltpu.SemaphoreType.DMA((len(out),))], 0, 2 * own.size, info, own, *tokens,
+        [pltpu.SemaphoreType.DMA((len(out),))], 0, 2 * own.size, info, own, *tokens, limit=limit,
     )
 
 
@@ -448,7 +448,7 @@
     got_rows = named.reshape(1, groups * capacity)
 
     rows, cols = w_in.shape
-    p1_in = move(parts_of(info, w_in, [(None, rows // 2, 0, cols)])[0], ALONG_Y)
+    p1_in = move(parts_of(info, w_in, [(None, rows // 2, 0, cols)], limit=61)[0], ALONG_Y)
     other_in = move(w_in, CORE)
     other_out = move(w_out, CORE)
     x = patches.T

time: 192 us -> 194 us (1.010)
  Pallas kernels: 63.8 us -> 66 us
    pallas_call x12, Pallas kernels: 51.1 us -> 53.3 us  [call(): pl.pallas_call(kernel, out_shape=out_shape, in_specs=in_specs, out_specs=...]
    unnamed x86 -> x88, local copies, waits for them, and re-layouts: 20.1 us -> 18.2 us
  transfers between devices with their start and end apart: 31 -> 31, of which waited for: 13 -> 13; matrix products, arithmetic and copies ran while one was open for 3% -> 4% of each run, Pallas kernels for 28% -> 29%
where the time goes in v5:
time: 194 us; the launch traced here: 193 us
  Pallas kernels  66 us (34%)
  starting transfers between devices  59.5 us (31%)
  waiting for transfers between devices  40.7 us (21%)
  local copies, waits for them, and re-layouts  21 us (11%)
  other arithmetic  4.16 us (2%)
    pallas_call x12, Pallas kernels, call(): pl.pallas_call(kernel, out_shape=out_shape, in_specs=in_specs, out_specs=...  53.3 us
    ppermute x8, waiting for transfers between devices, up(): return lax.ppermute(value, 'tensor', [(z, (z + 1) % 4) for z in range(4)])  30.5 us
    ppermute x8, starting transfers between devices, down(): return lax.ppermute(value, 'tensor', [(z, (z + 3) % 4) for z in range(4)])  19.8 us
    unnamed x88, local copies, waits for them, and re-layouts  18.2 us
    ppermute x12, starting transfers between devices, move(): return lax.ppermute(value, PLANE, pairs)  8.81 us
    ppermute x8, starting transfers between devices, up(): return lax.ppermute(value, 'tensor', [(z, (z + 1) % 4) for z in range(4)])  8.63 us
    all_to_all x1, starting transfers between devices, body(): swap(send.reshape(groups, capacity, width))  7.54 us
    all_to_all x1, starting transfers between devices, body(): swap(picked.reshape(groups, capacity, width))  7.5 us
  transfers between devices with their start and end apart: 31, of which 13 were waited for; matrix products, arithmetic and copies ran while one was open for 4% of the time, Pallas kernels for 29%

profile of v5, /device:TPU:8, one launch (start us, length us, event | category | flops | bytes accessed | tf_op | source)
XLA Modules:
  0.0 192.7 jit_solution(1198795792333987930)
XLA Ops:
  1.8 3.4 %shard_map.115 = bf16[640,1280]{1,0:T(8,128)(2,1)} custom-call(s32[4]{0:T(128)} %pad_add_fusion.info_ref, bf16[1280,1280]{1,0:T(8,128)(2,1)} %own_ref.6), custom_call_target="tpu_custom_call" | custom-call | bytes 3276800 | tf_op jit(solution)/shard_map/pallas_call | solution.py:54
  5.2 1.6 collective-permute-start
  6.9 1.9 collective-permute-start.3
  8.8 2.1 %collective-permute-start.4 = (bf16[320,1024]{1,0:T(8,128)(2,1)S(1)}, bf16[320,1024]{1,0:T(8,128)(2,1)S(1)}, u32[]{:S(2)}, u32[]{:S(2)}) collective-permute-start(bf16[320,1024]{1,0:T(8,128)(2,1)S(1)} %bitcast.37), channel_id=1, source_target_pairs={{0,3},{1,0},{2,1},{3,2},{4,7},{5,4},{6,5},{7,6},{8,11},{9,8},{10,9... | collective-permute-start | bytes 1966088 | tf_op jit(solution)/shard_map/ppermute | solution.py:40
  12.7 7.2 %all-to-all-start = ((s32[32,1,16]{2,1,0:T(1,128)}), s32[32,1,16]{2,1,0:T(1,128)S(1)}, u32[]{:S(2)}, u32[]{:S(2)}) async-start(s32[32,1,16]{2,1,0:T(1,128)} %bitcast.3), calls=%async_computation | async-start | bytes 32768 | tf_op jit(solution)/shard_map/all_to_all | solution.py:447
  20.0 2.5 %shard_map.114 = (bf16[864,1024]{1,0:T(8,128)(2,1)S(1)}, bf16[416,2048]{1,0:T(8,128)(2,1)S(1)}) custom-call(s32[4]{0:T(128)S(1)} %copy-done.27, bf16[1280,2048]{1,0:T(8,128)(2,1)} %refs_6_.1), custom_call_target="tpu_custom_call" | custom-call | bytes 5242880 | tf_op jit(solution)/shard_map/pallas_call | solution.py:54
  22.6 1.3 copy-done.9
  25.1 1.8 all-to-all-done
  28.0 1.6 collective-permute-start.10
  29.5 1.6 collective-permute-start.5
  31.1 2.0 %collective-permute-start.7 = (bf16[160,1024]{1,0:T(8,128)(2,1)S(1)}, bf16[160,1024]{1,0:T(8,128)(2,1)S(1)}, u32[]{:S(2)}, u32[]{:S(2)}) collective-permute-start(bf16[160,1024]{1,0:T(8,128)(2,1)S(1)} %slice.17), channel_id=1, source_target_pairs={{0,1},{1,2},{2,3},{3,0},{4,5},{5,6},{6,7},{7,4},{8,9},{9,10},{10,1... | collective-permute-start | bytes 983048 | tf_op jit(solution)/shard_map/ppermute | solution.py:36
  33.9 2.1 %collective-permute-start.8 = (bf16[160,1024]{1,0:T(8,128)(2,1)}, bf16[160,1024]{1,0:T(8,128)(2,1)S(1)}, u32[]{:S(2)}, u32[]{:S(2)}) collective-permute-start(bf16[160,1024]{1,0:T(8,128)(2,1)} %slice.18), channel_id=1, source_target_pairs={{0,3},{1,0},{2,1},{3,2},{4,7},{5,4},{6,5},{7,6},{8,11},{9,8},{10,9... | collective-permute-start | bytes 983048 | tf_op jit(solution)/shard_map/ppermute | solution.py:40
  37.9 5.8 %shard_map.113 = (bf16[512,2048]{1,0:T(8,128)(2,1)}, f32[8,128]{1,0:T(8,128)}) custom-call(s32[1,512]{1,0:T(1,128)} %reshape.92.at_ref, bf16[1024,2048]{1,0:T(8,128)(2,1)} %rows_ref.1), custom_call_target="tpu_custom_call" | custom-call | flops 2147483648 | bytes 6291456 | tf_op jit(solution)/shard_map/pallas_call | solution.py:312
  44.1 2.8 %shard_map.118 = (bf16[256,5120]{1,0:T(8,128)(2,1)S(1)}, f32[8,128]{1,0:T(8,128)}) custom-call(s32[4]{0:T(128)S(1)} %copy-done.27, f32[1,1280]{1,0:T(1,128)S(1)} %reshape.94.gain_ref, bf16[320,1024]{1,0:T(8,128)(2,1)S(1)} %bitcast.38, bf16[320,1024]{1,0:T(8,128)(2,1)S(1)} %copy-done.16, bf16[320,1024]{1,0:T(8,128)(2,1)S(1)} %copy-done.18, ...), custom_call_target="tpu_custom_call" | custom-call | flops 1073741824 | bytes 6291456 | tf_op jit(solution)/shard_map/pallas_call | solution.py:54
  46.9 3.8 %shard_map.119 = (f32[256,1280]{1,0:T(8,128)S(1)}, f32[8,128]{1,0:T(8,128)S(1)}) custom-call(s32[4]{0:T(128)S(1)} %copy-done.27, bf16[256,5120]{1,0:T(8,128)(2,1)S(1)} %get-tuple-element.27.x_ref, bf16[1280,1280]{1,0:T(8,128)(2,1)S(1)} %copy-done.6, bf16[1280,1280]{1,0:T(8,128)(2,1)} %collective-permute-done.1.refs_2_.other_ref), custom_call_target="tpu_custom_call" | custom-call | flops 2281701376 | bytes 9437184 | tf_op jit(solution)/shard_map/pallas_call | solution.py:54
  55.6 1.3 collective-permute-done.9.f1
  56.9 2.3 %collective-permute-done.11.f2 = bf16[640,1280]{1,0:T(8,128)(2,1)} collective-permute-done((bf16[640,1280]{1,0:T(8,128)(2,1)}, bf16[640,1280]{1,0:T(8,128)(2,1)}, u32[]{:S(2)}, u32[]{:S(2)}) %collective-permute-start.11) | collective-permute-done | bytes 1638432 | tf_op jit(solution)/shard_map/ppermute | solution.py:32
  59.3 1.3 copy-done.22
  60.6 6.6 %shard_map.121 = (bf16[256,1280]{1,0:T(8,128)(2,1)S(1)}, f32[256,1280]{1,0:T(8,128)S(1)}) custom-call(s32[4]{0:T(128)S(1)} %copy-done.27, bf16[256,5120]{1,0:T(8,128)(2,1)} %copy-done.7, f32[1,1280]{1,0:T(1,128)S(1)} %reshape.95.b_ref, f32[256,1280]{1,0:T(8,128)S(1)} %copy-done.22, bf16[640,1280]{1,0:T(8,128)(2,1)} %shard_map.116.refs_1_.p1, ...), custom_call_target="tpu_custom_call" | custom-call | flops 2281701376 | bytes 12582912 | tf_op jit(solution)/shard_map/pallas_call | solution.py:54
  67.2 5.1 %shard_map.122 = (bf16[2,256,2048]{2,1,0:T(8,128)(2,1)S(1)}, f32[8,128]{1,0:T(8,128)S(1)}) custom-call(s32[4]{0:T(128)S(1)} %copy-done.27, bf16[256,1280]{1,0:T(8,128)(2,1)S(1)} %get-tuple-element.31.h_ref, bf16[1280,2048]{1,0:T(8,128)(2,1)S(1)} %bitcast.33, bf16[1280,2048]{1,0:T(8,128)(2,1)} %collective-permute-done.2.refs_3_.other_ref.refs_4_.refs_7_), custom_call_target="tpu_custom_call" | custom-call | flops 3623878656 | bytes 13631488 | tf_op jit(solution)/shard_map/pallas_call | solution.py:54
  73.0 1.3 copy-done.35
  74.3 3.3 %collective-permute-done.6.refs_0_ = bf16[864,1024]{1,0:T(8,128)(2,1)} collective-permute-done((bf16[864,1024]{1,0:T(8,128)(2,1)}, bf16[864,1024]{1,0:T(8,128)(2,1)}, u32[]{:S(2)}, u32[]{:S(2)}) %collective-permute-start.6) | collective-permute-done | bytes 1769504 | tf_op jit(solution)/shard_map/ppermute | solution.py:32
  79.3 7.5 %all-to-all-start.1 = ((bf16[32,16,2048]{2,1,0:T(8,128)(2,1)}), bf16[32,16,2048]{2,1,0:T(8,128)(2,1)}, u32[]{:S(2)}, u32[]{:S(2)}) async-start(bf16[32,16,2048]{2,1,0:T(8,128)(2,1)} %bitcast.39), calls=%async_computation.1 | async-start | bytes 4194304 | tf_op jit(solution)/shard_map/all_to_all | solution.py:482
  86.9 1.6 copy-done.34
  88.5 6.7 %shard_map.127 = (bf16[256,1024]{1,0:T(8,128)(2,1)S(1)}, bf16[256,1024]{1,0:T(8,128)(2,1)S(1)}, bf16[256,1024]{1,0:T(8,128)(2,1)S(1)}, bf16[256,1024]{1,0:T(8,12...) custom-call(s32[4]{0:T(128)S(1)} %copy-done.27, ...), custom_call_target="tpu_custom_call" | custom-call | flops 3623878656 | bytes 17825792 | tf_op jit(solution)/shard_map/pallas_call | solution.py:54
  96.0 1.9 collective-permute-start.18
  97.9 2.1 %collective-permute-start.20 = (bf16[256,1024]{1,0:T(8,128)(2,1)S(1)}, bf16[256,1024]{1,0:T(8,128)(2,1)S(1)}, u32[]{:S(2)}, u32[]{:S(2)}) collective-permute-start(bf16[256,1024]{1,0:T(8,128)(2,1)S(1)} %get-tuple-element.43), channel_id=1, source_target_pairs={{0,3},{1,0},{2,1},{3,2},{4,7},{5,4},{6,5},{7,6},{8,11},{9,8},{10,9... | collective-permute-start | bytes 1572872 | tf_op jit(solution)/shard_map/ppermute | solution.py:40
  100.0 3.2 %collective-permute-start.17 = (bf16[256,1024]{1,0:T(8,128)(2,1)}, bf16[256,1024]{1,0:T(8,128)(2,1)}, u32[]{:S(2)}, u32[]{:S(2)}) collective-permute-start(bf16[256,1024]{1,0:T(8,128)(2,1)} %get-tuple-element.38), channel_id=1, source_target_pairs={{0,3},{1,0},{2,1},{3,2},{4,7},{5,4},{6,5},{7,6},{8,11},{9,8},{10,9... | collective-permute-start | bytes 1572872 | tf_op jit(solution)/shard_map/ppermute | solution.py:40
  103.2 9.5 %collective-permute-done.18 = bf16[256,1024]{1,0:T(8,128)(2,1)S(1)} collective-permute-done((bf16[256,1024]{1,0:T(8,128)(2,1)S(1)}, bf16[256,1024]{1,0:T(8,128)(2,1)S(1)}, u32[]{:S(2)}, u32[]{:S(2)}) %collective-permute-start.18) | collective-permute-done | bytes 524320 | tf_op jit(solution)/shard_map/ppermute | solution.py:36
  114.7 3.2 %collective-permute-start.21 = (bf16[256,1024]{1,0:T(8,128)(2,1)}, bf16[256,1024]{1,0:T(8,128)(2,1)}, u32[]{:S(2)}, u32[]{:S(2)}) collective-permute-start(bf16[256,1024]{1,0:T(8,128)(2,1)} %add_convert_fusion), channel_id=1, source_target_pairs={{0,3},{1,0},{2,1},{3,2},{4,7},{5,4},{6,5},{7,6},{8,11},{9,8},{10,9... | collective-permute-start | bytes 1572872 | tf_op jit(solution)/shard_map/ppermute | solution.py:40
  117.9 6.0 %collective-permute-done.16._.refs_4_ = bf16[256,1024]{1,0:T(8,128)(2,1)S(1)} collective-permute-done((bf16[256,1024]{1,0:T(8,128)(2,1)}, bf16[256,1024]{1,0:T(8,128)(2,1)S(1)}, u32[]{:S(2)}, u32[]{:S(2)}) %collective-permute-start.16) | collective-permute-done | bytes 524320 | tf_op jit(solution)/shard_map/ppermute | solution.py:36
  123.9 3.1 %shard_map.128 = (bf16[256,1024]{1,0:T(8,128)(2,1)S(1)}, bf16[256,1024]{1,0:T(8,128)(2,1)}) custom-call(s32[1,256]{1,0:T(1,128)S(1)} %bitcast_add_fusion.code_ref, bf16[512,2048]{1,0:T(8,128)(2,1)} %bitcast.14.rows_ref, bf16[256,1024]{1,0:T(8,128)(2,1)S(1)} %collective-permute-done.16._.refs_4_), custom_call_target="tpu_custom_call" | custom-call | flops 536870912 | bytes 3145728 | tf_op jit(solution)/shard_map/pallas_call | solution.py:54
  127.1 7.7 %collective-permute-done.19.refs_2_ = bf16[256,1024]{1,0:T(8,128)(2,1)} collective-permute-done((bf16[256,1024]{1,0:T(8,128)(2,1)}, bf16[256,1024]{1,0:T(8,128)(2,1)}, u32[]{:S(2)}, u32[]{:S(2)}) %collective-permute-start.19) | collective-permute-done | bytes 524320 | tf_op jit(solution)/shard_map/ppermute | solution.py:36
  134.8 2.2 %shard_map.129 = bf16[512,2048]{1,0:T(8,128)(2,1)S(1)} custom-call(s32[1,256]{1,0:T(1,128)S(1)} %bitcast_add_fusion.code_ref, f32[1,2048]{1,0:T(1,128)S(1)} %bitcast.35, bf16[256,1024]{1,0:T(8,128)(2,1)S(1)} %get-tuple-element.36._.refs_0_, bf16[256,1024]{1,0:T(8,128)(2,1)S(1)} %copy-done.24, bf16[256,1024]{1,0:T(8,128)(2,1)} %collective-permute-done.17.refs_1_, ...), custom_call_target="tpu_custom_call" | custom-call | flops 536870912 | bytes 6291456 | tf_op jit(solution)/shard_map/pallas_call | solution.py:54
  137.0 1.3 copy-done.8
  138.3 7.5 %all-to-all-start.2 = ((bf16[32,16,2048]{2,1,0:T(8,128)(2,1)}), bf16[32,16,2048]{2,1,0:T(8,128)(2,1)}, u32[]{:S(2)}, u32[]{:S(2)}) async-start(bf16[32,16,2048]{2,1,0:T(8,128)(2,1)} %bitcast.34), calls=%async_computation.2 | async-start | bytes 4194304 | tf_op jit(solution)/shard_map/all_to_all | solution.py:492
  145.9 1.3 collective-permute-start.24
  147.2 2.0 %collective-permute-start.26 = (bf16[256,1024]{1,0:T(8,128)(2,1)}, bf16[256,1024]{1,0:T(8,128)(2,1)S(1)}, u32[]{:S(2)}, u32[]{:S(2)}) collective-permute-start(bf16[256,1024]{1,0:T(8,128)(2,1)} %get-tuple-element.45.refs_1_), channel_id=1, source_target_pairs={{0,3},{1,0},{2,1},{3,2},{4,7},{5,4},{6,5},{7,6},{8,11},{9,8},{10,9... | collective-permute-start | bytes 1572872 | tf_op jit(solution)/shard_map/ppermute | solution.py:40
  149.2 3.2 %collective-permute-start.23 = (bf16[256,1024]{1,0:T(8,128)(2,1)S(1)}, bf16[256,1024]{1,0:T(8,128)(2,1)}, u32[]{:S(2)}, u32[]{:S(2)}) collective-permute-start(bf16[256,1024]{1,0:T(8,128)(2,1)S(1)} %get-tuple-element.36._.refs_0_), channel_id=1, source_target_pairs={{0,3},{1,0},{2,1},{3,2},{4,7},{5,4},{6,5},{7,6},{8,11},{9,8},{10,9... | collective-permute-start | bytes 1572872 | tf_op jit(solution)/shard_map/ppermute | solution.py:40
  152.4 1.5 copy-done.4
  153.9 4.7 %shard_map.131.refs_1_.refs_2_ = f32[256,1280]{1,0:T(8,128)S(1)} custom-call(s32[4]{0:T(128)S(1)} %copy-done.27, bf16[256,1024]{1,0:T(8,128)(2,1)S(1)} %get-tuple-element.36._.refs_0_, bf16[256,1024]{1,0:T(8,128)(2,1)} %get-tuple-element.45.refs_1_, bf16[1280,2048]{1,0:T(8,128)(2,1)} %refs_6_.1, ...), custom_call_target="tpu_custom_call" | custom-call | flops 1879048192 | bytes 6291456 | tf_op jit(solution)/shard_map/pallas_call | solution.py:54
  158.6 3.3 %collective-permute-done.24.refs_0_ = bf16[256,1024]{1,0:T(8,128)(2,1)S(1)} collective-permute-done((bf16[256,1024]{1,0:T(8,128)(2,1)S(1)}, bf16[256,1024]{1,0:T(8,128)(2,1)S(1)}, u32[]{:S(2)}, u32[]{:S(2)}) %collective-permute-start.24) | collective-permute-done | bytes 524320 | tf_op jit(solution)/shard_map/ppermute | solution.py:36
  162.2 4.2 %shard_map.134.refs_4_ = f32[256,1280]{1,0:T(8,128)S(1)} custom-call(s32[4]{0:T(128)S(1)} %copy-done.27, bf16[256,1024]{1,0:T(8,128)(2,1)S(1)} %collective-permute-done.24.refs_0_, bf16[256,1024]{1,0:T(8,128)(2,1)S(1)} %collective-permute-done.26.refs_0_.refs_1_, f32[256,1280]{1,0:T(8,128)S(1)} %shard_map.131.refs_1_.refs_2_, bf16[1280,2048]{1,0:T(8,128)(2,1)} %refs_6_.1, ...), custom_call_target="tpu_custom_call" | custom-call | flops 1879048192 | bytes 6291456 | tf_op jit(solution)/shard_map/pallas_call | solution.py:54
  169.1 1.4 collective-permute-start.25
  170.6 1.8 collective-permute-start.27
  172.8 6.9 %shard_map.130 = (bf16[1024,2048]{1,0:T(8,128)(2,1)}, f32[8,128]{1,0:T(8,128)}) custom-call(s32[1,512]{1,0:T(1,128)} %reshape.92.at_ref, bf16[1024,2048]{1,0:T(8,128)(2,1)} %text_ref.1, bf16[512,2048]{1,0:T(8,128)(2,1)} %bitcast.16.got_ref), custom_call_target="tpu_custom_call" | custom-call | flops 2147483648 | bytes 10485760 | tf_op jit(solution)/shard_map/pallas_call | solution.py:334
  179.7 4.0 %collective-permute-done.25.refs_2_ = bf16[256,1024]{1,0:T(8,128)(2,1)} collective-permute-done((bf16[256,1024]{1,0:T(8,128)(2,1)}, bf16[256,1024]{1,0:T(8,128)(2,1)}, u32[]{:S(2)}, u32[]{:S(2)}) %collective-permute-start.25) | collective-permute-done | bytes 524320 | tf_op jit(solution)/shard_map/ppermute | solution.py:36
  184.4 8.1 %shard_map.135 = bf16[256,1280]{1,0:T(8,128)(2,1)} custom-call(s32[4]{0:T(128)S(1)} %copy-done.27, bf16[256,1024]{1,0:T(8,128)(2,1)} %collective-permute-done.22.refs_0_, bf16[256,1024]{1,0:T(8,128)(2,1)} %collective-permute-done.23.refs_1_, bf16[256,1024]{1,0:T(8,128)(2,1)} %collective-permute-done.25.refs_2_, ...), custom_call_target="tpu_custom_call" | custom-call | flops 3758096384 | bytes 12582912 | tf_op jit(solution)/shard_map/pallas_call | solution.py:54
  (147 shorter events, 22.5 us)
Async XLA Ops:
  0.6 26.3 %collective-permute-start.2 = (bf16[1280,2048]{1,0:T(8,128)(2,1)}, bf16[1280,2048]{1,0:T(8,128)(2,1)}, u32[]{:S(2)}, u32[]{:S(2)}) collective-permute-start(bf16[1280,2048]{1,0:T(8,128)(2,1)} %refs_6_.1), channel_id=1, source_target_pairs={{0,4},{4,0},{8,12},{12,8},{16,20},{20,16},{24,28},{28,24},{32,36},... | collective-permute-start | bytes 15728648 | tf_op jit(solution)/shard_map/ppermute | solution.py:32
  0.7 26.2 %collective-permute-start.1 = (bf16[1280,1280]{1,0:T(8,128)(2,1)}, bf16[1280,1280]{1,0:T(8,128)(2,1)}, u32[]{:S(2)}, u32[]{:S(2)}) collective-permute-start(bf16[1280,1280]{1,0:T(8,128)(2,1)} %own_ref.6), channel_id=1, source_target_pairs={{0,4},{4,0},{8,12},{12,8},{16,20},{20,16},{24,28},{28,24},{32,36},... | collective-permute-start | bytes 9830408 | tf_op jit(solution)/shard_map/ppermute | solution.py:32
  1.8 9.1 %copy-start.38 = (s32[256,1]{0,1:T(1,128)S(1)}, s32[256,1]{0,1:T(1,128)}, u32[]{:S(2)}) copy-start(s32[256,1]{0,1:T(1,128)} %param.17) | copy-start | bytes 3076
  1.8 10.0 %copy-start.41 = (s32[256]{0:T(256)S(1)}, s32[256]{0:T(256)}, u32[]{:S(2)}) copy-start(s32[256]{0:T(256)} %param.18) | copy-start | bytes 3076
  1.8 18.2 %copy-start.27 = (s32[4]{0:T(128)S(1)}, s32[4]{0:T(128)}, u32[]{:S(2)}) copy-start(s32[4]{0:T(128)} %pad_add_fusion.info_ref) | copy-start | bytes 52
  5.2 21.7 %collective-permute-start = (bf16[640,1280]{1,0:T(8,128)(2,1)}, bf16[640,1280]{1,0:T(8,128)(2,1)}, u32[]{:S(2)}, u32[]{:S(2)}) collective-permute-start(bf16[640,1280]{1,0:T(8,128)(2,1)} %shard_map.115), channel_id=1, source_target_pairs={{0,8},{4,28},{8,16},{12,4},{16,24},{20,12},{24,0},{28,20},{32,40},... | collective-permute-start | bytes 4915208 | tf_op jit(solution)/shard_map/ppermute | solution.py:32
  6.9 20.0 %collective-permute-start.3 = (bf16[320,1024]{1,0:T(8,128)(2,1)S(1)}, bf16[320,1024]{1,0:T(8,128)(2,1)S(1)}, u32[]{:S(2)}, u32[]{:S(2)}) collective-permute-start(bf16[320,1024]{1,0:T(8,128)(2,1)S(1)} %bitcast.36), channel_id=1, source_target_pairs={{0,1},{1,2},{2,3},{3,0},{4,5},{5,6},{6,7},{7,4},{8,9},{9,10},{10,1... | collective-permute-start | bytes 1966088 | tf_op jit(solution)/shard_map/ppermute | solution.py:36
  8.8 18.1 %collective-permute-start.4 = (bf16[320,1024]{1,0:T(8,128)(2,1)S(1)}, bf16[320,1024]{1,0:T(8,128)(2,1)S(1)}, u32[]{:S(2)}, u32[]{:S(2)}) collective-permute-start(bf16[320,1024]{1,0:T(8,128)(2,1)S(1)} %bitcast.37), channel_id=1, source_target_pairs={{0,3},{1,0},{2,1},{3,2},{4,7},{5,4},{6,5},{7,6},{8,11},{9,8},{10,9... | collective-permute-start | bytes 1966088 | tf_op jit(solution)/shard_map/ppermute | solution.py:40
  12.7 14.2 %all-to-all-start = ((s32[32,1,16]{2,1,0:T(1,128)}), s32[32,1,16]{2,1,0:T(1,128)S(1)}, u32[]{:S(2)}, u32[]{:S(2)}) async-start(s32[32,1,16]{2,1,0:T(1,128)} %bitcast.3), calls=%async_computation | async-start | bytes 32768 | tf_op jit(solution)/shard_map/all_to_all | solution.py:447
  28.0 8.0 %copy-start.39 = (f32[1280]{0:T(1024)S(1)}, f32[1280]{0:T(1024)}, u32[]{:S(2)}) copy-start(f32[1280]{0:T(1024)} %param.11) | copy-start | bytes 15364
  28.0 8.6 %copy-start.37 = (s32[32,1,16]{2,1,0:T(1,128)S(1)}, s32[32,1,16]{2,1,0:T(1,128)}, u32[]{:S(2)}) copy-start(s32[32,1,16]{2,1,0:T(1,128)} %copy-done.36) | copy-start | bytes 6148
  28.0 25.5 %collective-permute-start.10 = (bf16[640,1280]{1,0:T(8,128)(2,1)}, bf16[640,1280]{1,0:T(8,128)(2,1)}, u32[]{:S(2)}, u32[]{:S(2)}) collective-permute-start(bf16[640,1280]{1,0:T(8,128)(2,1)} %shard_map.116.refs_1_.p1), channel_id=1, source_target_pairs={{0,32},{4,100},{8,40},{12,108},{16,48},{20,116},{24,56},{28,124},{... | collective-permute-start | bytes 4915208 | tf_op jit(solution)/shard_map/ppermute | solution.py:32
  29.5 23.9 %collective-permute-start.5 = (bf16[864,1024]{1,0:T(8,128)(2,1)}, bf16[864,1024]{1,0:T(8,128)(2,1)}, u32[]{:S(2)}, u32[]{:S(2)}) collective-permute-start(bf16[864,1024]{1,0:T(8,128)(2,1)} %shard_map.117), channel_id=1, source_target_pairs={{0,8},{4,28},{8,16},{12,4},{16,24},{20,12},{24,0},{28,20},{32,40},... | collective-permute-start | bytes 5308424 | tf_op jit(solution)/shard_map/ppermute | solution.py:32
  31.1 12.6 %collective-permute-start.7 = (bf16[160,1024]{1,0:T(8,128)(2,1)S(1)}, bf16[160,1024]{1,0:T(8,128)(2,1)S(1)}, u32[]{:S(2)}, u32[]{:S(2)}) collective-permute-start(bf16[160,1024]{1,0:T(8,128)(2,1)S(1)} %slice.17), channel_id=1, source_target_pairs={{0,1},{1,2},{2,3},{3,0},{4,5},{5,6},{6,7},{7,4},{8,9},{9,10},{10,1... | collective-permute-start | bytes 983048 | tf_op jit(solution)/shard_map/ppermute | solution.py:36
  33.9 10.2 %collective-permute-start.8 = (bf16[160,1024]{1,0:T(8,128)(2,1)}, bf16[160,1024]{1,0:T(8,128)(2,1)S(1)}, u32[]{:S(2)}, u32[]{:S(2)}) collective-permute-start(bf16[160,1024]{1,0:T(8,128)(2,1)} %slice.18), channel_id=1, source_target_pairs={{0,3},{1,0},{2,1},{3,2},{4,7},{5,4},{6,5},{7,6},{8,11},{9,8},{10,9... | collective-permute-start | bytes 983048 | tf_op jit(solution)/shard_map/ppermute | solution.py:40
  52.4 4.6 %collective-permute-start.9 = (bf16[640,1280]{1,0:T(8,128)(2,1)}, bf16[640,1280]{1,0:T(8,128)(2,1)}, u32[]{:S(2)}, u32[]{:S(2)}) collective-permute-start(bf16[640,1280]{1,0:T(8,128)(2,1)} %shard_map.116.refs_1_.p1), channel_id=1, source_target_pairs={{0,4},{4,0},{8,12},{12,8},{16,20},{20,16},{24,28},{28,24},{32,36},... | collective-permute-start | bytes 4915208 | tf_op jit(solution)/shard_map/ppermute | solution.py:32
  53.4 5.8 %collective-permute-start.11 = (bf16[640,1280]{1,0:T(8,128)(2,1)}, bf16[640,1280]{1,0:T(8,128)(2,1)}, u32[]{:S(2)}, u32[]{:S(2)}) collective-permute-start(bf16[640,1280]{1,0:T(8,128)(2,1)} %shard_map.120.p2), channel_id=1, source_target_pairs={{0,4},{4,0},{8,12},{12,8},{16,20},{20,16},{24,28},{28,24},{32,36},... | collective-permute-start | bytes 4915208 | tf_op jit(solution)/shard_map/ppermute | solution.py:32
  53.4 24.1 %collective-permute-start.6 = (bf16[864,1024]{1,0:T(8,128)(2,1)}, bf16[864,1024]{1,0:T(8,128)(2,1)}, u32[]{:S(2)}, u32[]{:S(2)}) collective-permute-start(bf16[864,1024]{1,0:T(8,128)(2,1)} %collective-permute-done.5.refs_1_.p1.refs_4_.refs_5_.refs_8_), channel_id=1, source_target_pairs={{0,32},{4,100},{8,40},{12,108},{16,48},{20,116},{24,56},{28,124},{... | collective-permute-start | bytes 5308424 | tf_op jit(solution)/shard_map/ppermute | solution.py:32
  54.6 12.6 %slice-start = ((s8[5242880]{0:T(1024)(128)(4,1)}), s8[1048576]{0:T(1024)(128)(4,1)S(1)}, s32[]{:S(2)}) async-start(s8[5242880]{0:T(1024)(128)(4,1)} %bitcast.32), calls=%async_computation.3 | async-start | bytes 2097152
  54.6 23.2 %collective-permute-start.12 = (bf16[416,2048]{1,0:T(8,128)(2,1)}, bf16[416,2048]{1,0:T(8,128)(2,1)S(1)}, u32[]{:S(2)}, u32[]{:S(2)}) collective-permute-start(bf16[416,2048]{1,0:T(8,128)(2,1)} %shard_map.124), channel_id=1, source_target_pairs={{0,8},{4,28},{8,16},{12,4},{16,24},{20,12},{24,0},{28,20},{32,40},... | collective-permute-start | bytes 5111816 | tf_op jit(solution)/shard_map/ppermute | solution.py:32
  55.5 31.3 %collective-permute-start.13 = (bf16[864,1024]{1,0:T(8,128)(2,1)}, bf16[864,1024]{1,0:T(8,128)(2,1)}, u32[]{:S(2)}, u32[]{:S(2)}) collective-permute-start(bf16[864,1024]{1,0:T(8,128)(2,1)} %collective-permute-done.5.refs_1_.p1.refs_4_.refs_5_.refs_8_), channel_id=1, source_target_pairs={{0,4},{4,0},{8,12},{12,8},{16,20},{20,16},{24,28},{28,24},{32,36},... | collective-permute-start | bytes 5308424 | tf_op jit(solution)/shard_map/ppermute | solution.py:32
  60.6 6.6 %slice-start.1 = ((s8[5242880]{0:T(1024)(128)(4,1)}), s8[4194304]{0:T(1024)(128)(4,1)S(1)}, s32[]{:S(2)}) async-start(s8[5242880]{0:T(1024)(128)(4,1)} %bitcast.32), calls=%async_computation.4 | async-start | bytes 8388608
  77.6 9.3 %collective-permute-start.14 = (bf16[864,1024]{1,0:T(8,128)(2,1)}, bf16[864,1024]{1,0:T(8,128)(2,1)}, u32[]{:S(2)}, u32[]{:S(2)}) collective-permute-start(bf16[864,1024]{1,0:T(8,128)(2,1)} %shard_map.123.refs_1_.p2.refs_6_.refs_7_.refs_10_), channel_id=1, source_target_pairs={{0,4},{4,0},{8,12},{12,8},{16,20},{20,16},{24,28},{28,24},{32,36},... | collective-permute-start | bytes 5308424 | tf_op jit(solution)/shard_map/ppermute | solution.py:32
  79.1 7.7 %collective-permute-start.15 = (bf16[416,2048]{1,0:T(8,128)(2,1)}, bf16[416,2048]{1,0:T(8,128)(2,1)S(1)}, u32[]{:S(2)}, u32[]{:S(2)}) collective-permute-start(bf16[416,2048]{1,0:T(8,128)(2,1)} %shard_map.125.refs_2_.direct.refs_8_.refs_9_.refs_12_), channel_id=1, source_target_pairs={{0,4},{4,0},{8,12},{12,8},{16,20},{20,16},{24,28},{28,24},{32,36},... | collective-permute-start | bytes 5111816 | tf_op jit(solution)/shard_map/ppermute | solution.py:32
  79.3 7.5 %copy-start.1 = (bf16[416,2048]{1,0:T(8,128)(2,1)S(1)}, bf16[416,2048]{1,0:T(8,128)(2,1)}, u32[]{:S(2)}) copy-start(bf16[416,2048]{1,0:T(8,128)(2,1)} %shard_map.125.refs_2_.direct.refs_8_.refs_9_.refs_12_) | copy-start | bytes 5111812
  79.3 38.6 %all-to-all-start.1 = ((bf16[32,16,2048]{2,1,0:T(8,128)(2,1)}), bf16[32,16,2048]{2,1,0:T(8,128)(2,1)}, u32[]{:S(2)}, u32[]{:S(2)}) async-start(bf16[32,16,2048]{2,1,0:T(8,128)(2,1)} %bitcast.39), calls=%async_computation.1 | async-start | bytes 4194304 | tf_op jit(solution)/shard_map/all_to_all | solution.py:482
  86.9 8.3 %copy-start.3 = (bf16[416,2048]{1,0:T(8,128)(2,1)}, bf16[416,2048]{1,0:T(8,128)(2,1)S(1)}, u32[]{:S(2)}) copy-start(bf16[416,2048]{1,0:T(8,128)(2,1)S(1)} %collective-permute-done.15.crossed.refs_9_.refs_10_.refs_13_) | copy-start | bytes 5111812
  96.0 17.8 %copy-start.25 = (bf16[256,1024]{1,0:T(8,128)(2,1)}, bf16[256,1024]{1,0:T(8,128)(2,1)S(1)}, u32[]{:S(2)}) copy-start(bf16[256,1024]{1,0:T(8,128)(2,1)S(1)} %get-tuple-element.41.refs_3_) | copy-start | bytes 1572868
  96.0 16.7 %collective-permute-start.18 = (bf16[256,1024]{1,0:T(8,128)(2,1)S(1)}, bf16[256,1024]{1,0:T(8,128)(2,1)S(1)}, u32[]{:S(2)}, u32[]{:S(2)}) collective-permute-start(bf16[256,1024]{1,0:T(8,128)(2,1)S(1)} %get-tuple-element.40), channel_id=1, source_target_pairs={{0,1},{1,2},{2,3},{3,0},{4,5},{5,6},{6,7},{7,4},{8,9},{9,10},{10,1... | collective-permute-start | bytes 1572872 | tf_op jit(solution)/shard_map/ppermute | solution.py:36
  97.9 15.8 %collective-permute-start.20 = (bf16[256,1024]{1,0:T(8,128)(2,1)S(1)}, bf16[256,1024]{1,0:T(8,128)(2,1)S(1)}, u32[]{:S(2)}, u32[]{:S(2)}) collective-permute-start(bf16[256,1024]{1,0:T(8,128)(2,1)S(1)} %get-tuple-element.43), channel_id=1, source_target_pairs={{0,3},{1,0},{2,1},{3,2},{4,7},{5,4},{6,5},{7,6},{8,11},{9,8},{10,9... | collective-permute-start | bytes 1572872 | tf_op jit(solution)/shard_map/ppermute | solution.py:40
  100.0 23.9 %collective-permute-start.16 = (bf16[256,1024]{1,0:T(8,128)(2,1)}, bf16[256,1024]{1,0:T(8,128)(2,1)S(1)}, u32[]{:S(2)}, u32[]{:S(2)}) collective-permute-start(bf16[256,1024]{1,0:T(8,128)(2,1)} %get-tuple-element.35), channel_id=1, source_target_pairs={{0,1},{1,2},{2,3},{3,0},{4,5},{5,6},{6,7},{7,4},{8,9},{9,10},{10,1... | collective-permute-start | bytes 1572872 | tf_op jit(solution)/shard_map/ppermute | solution.py:36
  100.0 27.1 %collective-permute-start.17 = (bf16[256,1024]{1,0:T(8,128)(2,1)}, bf16[256,1024]{1,0:T(8,128)(2,1)}, u32[]{:S(2)}, u32[]{:S(2)}) collective-permute-start(bf16[256,1024]{1,0:T(8,128)(2,1)} %get-tuple-element.38), channel_id=1, source_target_pairs={{0,3},{1,0},{2,1},{3,2},{4,7},{5,4},{6,5},{7,6},{8,11},{9,8},{10,9... | collective-permute-start | bytes 1572872 | tf_op jit(solution)/shard_map/ppermute | solution.py:40
  113.7 21.1 %collective-permute-start.19 = (bf16[256,1024]{1,0:T(8,128)(2,1)}, bf16[256,1024]{1,0:T(8,128)(2,1)}, u32[]{:S(2)}, u32[]{:S(2)}) collective-permute-start(bf16[256,1024]{1,0:T(8,128)(2,1)} %add_convert_fusion.1), channel_id=1, source_target_pairs={{0,1},{1,2},{2,3},{3,0},{4,5},{5,6},{6,7},{7,4},{8,9},{9,10},{10,1... | collective-permute-start | bytes 1572872 | tf_op jit(solution)/shard_map/ppermute | solution.py:36
  113.7 21.1 %copy-start.24 = (bf16[256,1024]{1,0:T(8,128)(2,1)S(1)}, bf16[256,1024]{1,0:T(8,128)(2,1)}, u32[]{:S(2)}) copy-start(bf16[256,1024]{1,0:T(8,128)(2,1)} %copy-done.23) | copy-start | bytes 1572868
  113.7 21.1 %copy-start.29 = (f32[2048]{0:T(1024)S(1)}, f32[2048]{0:T(1024)}, u32[]{:S(2)}) copy-start(f32[2048]{0:T(1024)} %param.15) | copy-start | bytes 24580
  114.7 20.1 %collective-permute-start.21 = (bf16[256,1024]{1,0:T(8,128)(2,1)}, bf16[256,1024]{1,0:T(8,128)(2,1)}, u32[]{:S(2)}, u32[]{:S(2)}) collective-permute-start(bf16[256,1024]{1,0:T(8,128)(2,1)} %add_convert_fusion), channel_id=1, source_target_pairs={{0,3},{1,0},{2,1},{3,2},{4,7},{5,4},{6,5},{7,6},{8,11},{9,8},{10,9... | collective-permute-start | bytes 1572872 | tf_op jit(solution)/shard_map/ppermute | solution.py:40
  117.9 16.9 %copy-start.26 = (bf16[256,1024]{1,0:T(8,128)(2,1)S(1)}, bf16[256,1024]{1,0:T(8,128)(2,1)}, u32[]{:S(2)}) copy-start(bf16[256,1024]{1,0:T(8,128)(2,1)} %copy-done.25) | copy-start | bytes 1572868
  138.3 34.5 %all-to-all-start.2 = ((bf16[32,16,2048]{2,1,0:T(8,128)(2,1)}), bf16[32,16,2048]{2,1,0:T(8,128)(2,1)}, u32[]{:S(2)}, u32[]{:S(2)}) async-start(bf16[32,16,2048]{2,1,0:T(8,128)(2,1)} %bitcast.34), calls=%async_computation.2 | async-start | bytes 4194304 | tf_op jit(solution)/shard_map/all_to_all | solution.py:492
  145.9 16.0 %collective-permute-start.24 = (bf16[256,1024]{1,0:T(8,128)(2,1)S(1)}, bf16[256,1024]{1,0:T(8,128)(2,1)S(1)}, u32[]{:S(2)}, u32[]{:S(2)}) collective-permute-start(bf16[256,1024]{1,0:T(8,128)(2,1)S(1)} %get-tuple-element.36._.refs_0_), channel_id=1, source_target_pairs={{0,1},{1,2},{2,3},{3,0},{4,5},{5,6},{6,7},{7,4},{8,9},{9,10},{10,1... | collective-permute-start | bytes 1572872 | tf_op jit(solution)/shard_map/ppermute | solution.py:36
  147.2 15.0 %collective-permute-start.26 = (bf16[256,1024]{1,0:T(8,128)(2,1)}, bf16[256,1024]{1,0:T(8,128)(2,1)S(1)}, u32[]{:S(2)}, u32[]{:S(2)}) collective-permute-start(bf16[256,1024]{1,0:T(8,128)(2,1)} %get-tuple-element.45.refs_1_), channel_id=1, source_target_pairs={{0,3},{1,0},{2,1},{3,2},{4,7},{5,4},{6,5},{7,6},{8,11},{9,8},{10,9... | collective-permute-start | bytes 1572872 | tf_op jit(solution)/shard_map/ppermute | solution.py:40
  149.2 30.6 %collective-permute-start.22 = (bf16[256,1024]{1,0:T(8,128)(2,1)}, bf16[256,1024]{1,0:T(8,128)(2,1)}, u32[]{:S(2)}, u32[]{:S(2)}) collective-permute-start(bf16[256,1024]{1,0:T(8,128)(2,1)} %get-tuple-element.45.refs_1_), channel_id=1, source_target_pairs={{0,1},{1,2},{2,3},{3,0},{4,5},{5,6},{6,7},{7,4},{8,9},{9,10},{10,1... | collective-permute-start | bytes 1572872 | tf_op jit(solution)/shard_map/ppermute | solution.py:36
  149.2 30.5 %collective-permute-start.23 = (bf16[256,1024]{1,0:T(8,128)(2,1)S(1)}, bf16[256,1024]{1,0:T(8,128)(2,1)}, u32[]{:S(2)}, u32[]{:S(2)}) collective-permute-start(bf16[256,1024]{1,0:T(8,128)(2,1)S(1)} %get-tuple-element.36._.refs_0_), channel_id=1, source_target_pairs={{0,3},{1,0},{2,1},{3,2},{4,7},{5,4},{6,5},{7,6},{8,11},{9,8},{10,9... | collective-permute-start | bytes 1572872 | tf_op jit(solution)/shard_map/ppermute | solution.py:40
  158.6 7.8 %copy-start.2 = (f32[256,1280]{1,0:T(8,128)}, f32[256,1280]{1,0:T(8,128)S(1)}, u32[]{:S(2)}) copy-start(f32[256,1280]{1,0:T(8,128)S(1)} %shard_map.131.refs_1_.refs_2_) | copy-start | bytes 3932164
  169.1 14.6 %collective-permute-start.25 = (bf16[256,1024]{1,0:T(8,128)(2,1)}, bf16[256,1024]{1,0:T(8,128)(2,1)}, u32[]{:S(2)}, u32[]{:S(2)}) collective-permute-start(bf16[256,1024]{1,0:T(8,128)(2,1)} %shard_map.132), channel_id=1, source_target_pairs={{0,1},{1,2},{2,3},{3,0},{4,5},{5,6},{6,7},{7,4},{8,9},{9,10},{10,1... | collective-permute-start | bytes 1572872 | tf_op jit(solution)/shard_map/ppermute | solution.py:36
  170.6 13.1 %collective-permute-start.27 = (bf16[256,1024]{1,0:T(8,128)(2,1)}, bf16[256,1024]{1,0:T(8,128)(2,1)}, u32[]{:S(2)}, u32[]{:S(2)}) collective-permute-start(bf16[256,1024]{1,0:T(8,128)(2,1)} %shard_map.133), channel_id=1, source_target_pairs={{0,3},{1,0},{2,1},{3,2},{4,7},{5,4},{6,5},{7,6},{8,11},{9,8},{10,9... | collective-permute-start | bytes 1572872 | tf_op jit(solution)/shard_map/ppermute | solution.py:40
  172.8 10.9 %copy-start.5 = (bf16[416,2048]{1,0:T(8,128)(2,1)S(1)}, bf16[416,2048]{1,0:T(8,128)(2,1)}, u32[]{:S(2)}) copy-start(bf16[416,2048]{1,0:T(8,128)(2,1)} %copy-done.3) | copy-start | bytes 5111812
  172.8 10.9 %copy-start.11 = (f32[256,1280]{1,0:T(8,128)S(1)}, f32[256,1280]{1,0:T(8,128)}, u32[]{:S(2)}) copy-start(f32[256,1280]{1,0:T(8,128)} %copy-done.10) | copy-start | bytes 3932164
  172.8 10.9 %copy-start.20 = (f32[256,1280]{1,0:T(8,128)S(1)}, f32[256,1280]{1,0:T(8,128)}, u32[]{:S(2)}) copy-start(f32[256,1280]{1,0:T(8,128)} %copy-done.19) | copy-start | bytes 3932164
  (27 other events, 51.2 us)
